TPU v7x, 256 devices: a whole 4x4x8 slice. The times are simulated.
256 devices in a mesh: grp: 8 (over x_lo, y), blk: 32 (over x_hi, z, core).
Axes of the slice: x: 4 (x_hi: 2, x_lo: 2; x = x_hi * 2 + x_lo), y: 4, z: 8, core: 2. Of those that a mesh axis runs over, the one named last changes fastest.
Arguments:
- feat_one: bfloat16 [65536, 256], P(('grp', 'blk')), parts along dimension 0, may hold values from -8 to 8
- feat_two: bfloat16 [65536, 256], P(('grp', 'blk')), parts along dimension 0, may hold values from -8 to 8
- match_one: int32 [256, 256], P(('grp', 'blk')), parts along dimension 0, may hold values from 0 to 255, each once within a row
- match_two: int32 [256, 256], P(('grp', 'blk')), parts along dimension 0, may hold values from 0 to 255, each once within a row
- valid_counts: int32 [256], P(('grp', 'blk')), parts along dimension 0, may hold values from 128 to 256, as said below
Outputs:
- grad_one: float32 [65536, 256], P(('grp', 'blk')), parts along dimension 0
- grad_two: float32 [65536, 256], P(('grp', 'blk')), parts along dimension 0
- row_lse: float32 [65536], P(('grp', 'blk')), parts along dimension 0
- col_lse: float32 [65536], P(('grp', 'blk')), parts along dimension 0
There are 8 independent parts, one for each index of `grp`. A program takes and returns all parts, laid end to end along the dimension named above; each array names one. Nothing has to cross between parts.
Inputs may be any that keep to these rules, and one draw needn't show every extreme that they name: `valid_counts`: at least half of a device's pairs are valid, and some device has all 256 valid.
All inputs are finite; a program needn't handle non-finite values.
Results may differ from a plain program's by a relative error of at most 0.0016.
Values may be sent and summed in bfloat16 or wider, within the bound.
No kernel may reach another device: no remote copies, remote signals or barrier semaphores. Data moves between devices by JAX's collectives and lax.ppermute only.
A program may use at most 64 MiB of HBM per device.

v0:
```python
import math

import jax
import jax.numpy as jnp
from jax import lax
from jax.sharding import PartitionSpec as P

NEG = -1e30


def blocked(array, size):
    return array.reshape((array.shape[0] // size, size) + array.shape[1:])


def local(feat_one, feat_two, match_one, match_two, valid_counts):
    pairs, width = feat_one.shape
    scale = 2.0 / math.sqrt(width)
    own_one = match_one[0]
    own_two = match_two[0]
    query = feat_one[own_one]
    keys = feat_two[own_two]
    valid = (jnp.arange(pairs, dtype=jnp.int32) < valid_counts[0]).astype(jnp.float32)
    valid_bf = valid.astype(jnp.bfloat16)
    position = lax.axis_index("blk") * pairs
    keys_all, kmask_bf = (
        lax.all_gather(keys, "blk", axis=0, tiled=True),
        lax.all_gather(valid_bf, "blk", axis=0, tiled=True),
    )
    kmask_all = kmask_bf.astype(jnp.float32)
    total_rows = keys_all.shape[0]
    size = min(1024, total_rows)

    def forward_step(carry, piece):
        run_max, run_sum = carry
        kb, mb = piece
        s = jnp.dot(query, kb.T, preferred_element_type=jnp.float32) * scale
        sv = jnp.where(mb[None, :] > 0, s, NEG)
        new_max = jnp.maximum(run_max, jnp.max(sv, axis=1))
        terms = jnp.where(mb[None, :] > 0, jnp.exp(sv - new_max[:, None]), 0.0)
        new_sum = run_sum * jnp.exp(run_max - new_max) + jnp.sum(terms, axis=1)
        cs = jnp.where(valid[:, None] > 0, s, NEG)
        col_max = jnp.max(cs, axis=0)
        col_sum = jnp.sum(
            jnp.where(valid[:, None] > 0, jnp.exp(cs - col_max[None, :]), 0.0), axis=0
        )
        return ((new_max, new_sum), (col_max, col_sum))

    start_carry = (jnp.full((pairs,), NEG, jnp.float32), jnp.zeros((pairs,), jnp.float32))
    (row_max, row_sum), (col_max, col_sum) = lax.scan(
        forward_step, start_carry, (blocked(keys_all, size), blocked(kmask_all, size))
    )
    row_lse = row_max + jnp.log(row_sum)
    col_max = col_max.reshape(total_rows)
    col_sum = col_sum.reshape(total_rows)
    peak = lax.pmax(col_max.astype(jnp.bfloat16), "blk").astype(col_max.dtype)
    own_sum = lax.psum_scatter(
        col_sum * jnp.exp(col_max - peak), "blk", scatter_dimension=0, tiled=True
    )
    col_lse = lax.dynamic_slice_in_dim(peak, position, pairs) + jnp.log(own_sum)
    col_lse_all = lax.all_gather(col_lse, "blk", axis=0, tiled=True)
    total = lax.psum(valid_counts[0].astype(jnp.float32), "blk")
    coef = scale / (2.0 * total)

    def query_step(acc, piece):
        kb, mb, lb = piece
        s = jnp.dot(query, kb.T, preferred_element_type=jnp.float32) * scale
        keep = (valid[:, None] > 0) & (mb[None, :] > 0)
        weight = jnp.where(
            keep, jnp.exp(s - row_lse[:, None]) + jnp.exp(s - lb[None, :]), 0.0
        ).astype(jnp.bfloat16)
        return (acc + jnp.dot(weight, kb, preferred_element_type=jnp.float32), None)

    acc_q, _ = lax.scan(
        query_step,
        jnp.zeros((pairs, width), jnp.float32),
        (blocked(keys_all, size), blocked(kmask_all, size), blocked(col_lse_all, size)),
    )
    grad_q = coef * (acc_q - 2.0 * valid[:, None] * keys.astype(jnp.float32))
    kb = keys_all
    mb = kmask_all
    lb = col_lse_all
    s = jnp.dot(query, kb.T, preferred_element_type=jnp.float32) * scale
    keep = (valid[:, None] > 0) & (mb[None, :] > 0)
    weight = jnp.where(keep, jnp.exp(s - row_lse[:, None]) + jnp.exp(s - lb[None, :]), 0.0).astype(
        jnp.bfloat16
    )
    acc_k = lax.psum_scatter(
        lax.dot_general(
            weight, query, (((0,), (0,)), ((), ())), preferred_element_type=jnp.float32
        ),
        "blk",
        scatter_dimension=0,
        tiled=True,
    )
    grad_k = coef * (acc_k - 2.0 * valid[:, None] * query.astype(jnp.float32))
    grad_one = jnp.zeros((pairs, width), jnp.float32).at[own_one].set(grad_q)
    grad_two = jnp.zeros((pairs, width), jnp.float32).at[own_two].set(grad_k)
    return (grad_one, grad_two, row_lse, col_lse)


def solution(mesh):
    placed = (
        P(("grp", "blk"), None),
        P(("grp", "blk"), None),
        P(("grp", "blk"), None),
        P(("grp", "blk"), None),
        P(("grp", "blk")),
    )
    return jax.shard_map(
        local,
        mesh=mesh,
        in_specs=placed,
        out_specs=(
            P(("grp", "blk"), None),
            P(("grp", "blk"), None),
            P(("grp", "blk")),
            P(("grp", "blk")),
        ),
        check_vma=False,
    )
```

profile of v0, /device:TPU:1, one launch (start us, length us, event | category | flops | bytes accessed | tf_op | source)
XLA Modules:
  0.0 589.3 jit_solution(11950548147505435460)
XLA Ops:
  7.2 0.7 compare_select_fusion
  7.9 0.1 copy-done
  8.1 1.8 gather_fusion
  10.7 1.3 dynamic-slice
  12.6 46.0 %all-gather.1 = bf16[32,1,256]{2,1,0:T(2,128)(2,1)S(1)} all-gather(bf16[1,1,256]{2,1,0:T(2,128)(2,1)S(1)} %reshape.145), channel_id=1, replica_groups=mesh['grp'=8,'blk'=32] {'blk'}, dimensions={0}, use_global_device_ids=true | all-gather | bytes 16896 | tf_op jit(solution)/shard_map/all_gather | solution.py:27
  58.8 0.1 compare_reduce_fusion.2
  58.9 0.7 compare_select_fusion.1
  59.6 1.9 gather_fusion.1
  61.5 41.0 %all-gather.5.cloned.1.call-done = bf16[8192,256]{1,0:T(8,128)(2,1)} async-done(((bf16[256,256]{1,0:T(8,128)(2,1)}), bf16[8192,256]{1,0:T(8,128)(2,1)}) %all-gather.5.cloned.1.call-update) | async-done | bytes 4194320 | tf_op jit(solution)/shard_map/all_gather | solution.py:26
  102.4 25.3 %while.28 = (s32[]{:T(128)}, f32[256]{0:T(256)S(1)}, f32[256]{0:T(256)S(1)}, f32[8,1024]{1,0:T(8,128)S(1)}, f32[8,1024]{1,0:T(8,128)S(1)}, /*index=5*/f32[8,1024...) while((s32[]{:T(128)}, f32[256]{0:T(256)S(1)}, ...), condition=%wide.region_6.7_spmd.clone, body=%wide.region_1.6_spmd.clone.sunk | while | flops 137626624 | bytes 2802580 | solution.py:49
  102.4 0.7 fusion.63
  103.1 1.6 select_reduce_fusion.6
  104.7 0.6 select_reduce_fusion.7
  105.3 0.1 dynamic_update_slice.12
  105.5 0.1 dynamic_update_slice.11
  105.6 0.7 fusion.63
  106.3 1.6 select_reduce_fusion.6
  107.9 0.6 select_reduce_fusion.7
  108.5 0.1 dynamic_update_slice.12
  108.6 0.1 dynamic_update_slice.11
  108.8 0.7 fusion.63
  109.5 1.6 select_reduce_fusion.6
  111.0 0.6 select_reduce_fusion.7
  111.7 0.1 dynamic_update_slice.12
  111.8 0.1 dynamic_update_slice.11
  111.9 0.7 fusion.63
  112.6 1.6 select_reduce_fusion.6
  114.2 0.6 select_reduce_fusion.7
  115.1 0.7 fusion.63
  115.8 1.6 select_reduce_fusion.6
  117.3 0.6 select_reduce_fusion.7
  118.2 0.7 fusion.63
  118.9 1.6 select_reduce_fusion.6
  120.5 0.6 select_reduce_fusion.7
  121.4 0.7 fusion.63
  122.1 1.6 select_reduce_fusion.6
  123.7 0.6 select_reduce_fusion.7
  124.6 0.7 fusion.63
  125.2 1.6 select_reduce_fusion.6
  126.8 0.6 select_reduce_fusion.7
  127.7 124.4 %pmax.7 = bf16[8192]{0:T(1024)(128)(2,1)S(1)} all-reduce(bf16[8192]{0:T(1024)(128)(2,1)S(1)} %bitcast.76), channel_id=1, replica_groups=mesh['grp'=8,'blk'=32] {'blk'}, use_global_device_ids=true, to_apply=%region_7.8 | all-reduce | flops 8192 | bytes 32768 | tf_op jit(solution)/shard_map/pmax | solution.py:55
  252.2 128.5 %all-reduce.1 = (f32[8192]{0:T(1024)S(1)}, f32[]{:T(128)}) all-reduce(f32[8192]{0:T(1024)S(1)} %bitcast_multiply_fusion, f32[]{:T(128)S(6)} %convert_element_type.35), channel_id=3, replica_groups=mesh['grp'=8,'blk'=32] {'blk'}, use_global_device_ids=true, to_apply=%region_8.9.clone | all-reduce | flops 8193 | bytes 65544
  380.7 42.2 %all-gather.2 = f32[32,1,256]{2,1,0:T(1,128)S(1)} all-gather(f32[1,1,256]{2,1,0:T(1,128)S(1)} %bitcast.82), channel_id=1, replica_groups=mesh['grp'=8,'blk'=32] {'blk'}, dimensions={0}, use_global_device_ids=true | all-gather | bytes 33792 | tf_op jit(solution)/shard_map/all_gather | solution.py:60
  422.9 9.9 %fusion.27 = f32[8192,256]{1,0:T(8,128)} fusion(bf16[256,256]{1,0:T(8,128)(2,1)S(1)} %get-tuple-element.388, bf16[8192,256]{1,0:T(8,128)(2,1)} %bitcast.84, f32[8192]{0:T(1024)S(1)} %bitcast.74, f32[256]{0:T(256)S(1)} %log_add_fusion, pred[8192]{0:T(1024)(128)(4,1)S(1)} %reshape.153, pred[256]{0:T(512)(128)(4,1)S(1)} %convert_compare_fusion), kind=kOutput, calls=%fused_computation.43 | convolution fusion | flops 2162163712 | bytes 12756224 | tf_op jit(solution)/shard_map/dot_general | solution.py:88
  433.7 23.1 %while.29 = (s32[]{:T(128)}, f32[256,256]{1,0:T(8,128)S(1)}, f32[8,1024]{1,0:T(8,128)S(1)}, bf16[8,1024,256]{2,1,0:T(8,128)(2,1)}, bf16[256,256]{1,0:T(8,128)(2,...) while((s32[]{:T(128)}, f32[256,256]{1,0:T(8,128)S(1)}, ...), condition=%wide.region_10.11_spmd.clone, body=%wide.region_9.10_spmd.clone.sunk | while | flops 270403328 | bytes 1725570 | solution.py:73
  433.7 0.7 fusion.69
  434.5 2.1 convolution_add_fusion.2
  436.6 0.7 fusion.69
  437.3 2.1 convolution_add_fusion.2
  439.4 0.7 fusion.69
  440.1 2.2 convolution_add_fusion.2
  442.4 0.7 fusion.69
  443.1 2.1 convolution_add_fusion.2
  445.3 0.7 fusion.69
  446.0 2.1 convolution_add_fusion.2
  448.2 0.7 fusion.69
  448.9 2.1 convolution_add_fusion.2
  451.0 0.7 fusion.69
  451.8 2.1 convolution_add_fusion.2
  453.9 0.7 fusion.69
  454.6 2.1 convolution_add_fusion.2
  456.8 2.2 scatter_custom_fusion
  459.0 120.8 %reduce-scatter.2.cloned.1.call-done = f32[256,256]{1,0:T(8,128)} async-done(((f32[8192,256]{1,0:T(8,128)}), f32[256,256]{1,0:T(8,128)}) %reduce-scatter.2.cloned.1.call-update) | async-done | bytes 262160 | tf_op jit(solution)/shard_map/reduce_scatter | solution.py:87
  579.8 2.6 scatter_custom_fusion.1
  (90 shorter events, 2.4 us)
Async XLA Ops:
  7.2 0.9 copy-start
  7.2 95.3 %all-gather.5.cloned.1.call-start = ((), (), s32[]{:S(2)}) async-start(), calls=%async_computation.2 | async-start | bytes 4325376 | tf_op jit(solution)/shard_map/all_gather | solution.py:26
  9.9 569.9 %reduce-scatter.2.cloned.1.call-start = ((), (), s32[]{:S(2)}) async-start(), calls=%async_computation.1 | async-start | bytes 8650752 | tf_op jit(solution)/shard_map/reduce_scatter | solution.py:87
  380.7 52.1 %copy-start.2 = (f32[256]{0:T(256)}, f32[256]{0:T(256)S(1)}, u32[]{:S(2)}) copy-start(f32[256]{0:T(256)S(1)} %fusion.45) | copy-start | bytes 3076
  433.7 23.1 %copy-start.1 = (bf16[256,256]{1,0:T(8,128)(2,1)S(1)}, bf16[256,256]{1,0:T(8,128)(2,1)}, u32[]{:S(2)}) copy-start(bf16[256,256]{1,0:T(8,128)(2,1)} %gather_fusion) | copy-start | bytes 393220
  456.8 125.6 %copy-start.3 = (f32[256]{0:T(256)}, f32[256]{0:T(256)S(1)}, u32[]{:S(2)}) copy-start(f32[256]{0:T(256)S(1)} %get-tuple-element.392) | copy-start | bytes 3076
Sparse Core Ops, SparseCore 0:
  11.4 91.0 all-gather.4
  432.9 146.8 reduce-scatter.1
where the time goes:
time: 594 us; the launch traced here: 589 us
  blocking collectives  341 us (57%)
  waiting for transfers between devices  162 us (27%)
  matrix products  39.5 us (7%)
  other arithmetic  22.8 us (4%)
  between operations  16.3 us (3%)
  local copies, waits for them, and re-layouts  7 us (1%)
    unnamed x1, blocking collectives  128 us
    pmax x1, blocking collectives, local(): peak = lax.pmax(col_max.astype(jnp.bfloat16), 'blk').astype(col_max.dtype)  124 us
    reduce_scatter x1, waiting for transfers between devices, local(): lax.psum_scatter(lax.dot_general(weight, query, (((0,), (0,)), ((), ())),...  121 us
    all_gather x1, blocking collectives, local(): lax.all_gather(valid_bf, 'blk', axis=0, tiled=True)  46 us
    all_gather x1, blocking collectives, local(): col_lse_all = lax.all_gather(col_lse, 'blk', axis=0, tiled=True)  42.2 us
    all_gather x1, waiting for transfers between devices, local(): lax.all_gather(keys, 'blk', axis=0, tiled=True)  41 us
    dot_general x8, matrix products, query_step(): return (acc + jnp.dot(weight, kb, preferred_element_type=jnp.float32), None)  17.2 us
    dot_general x8, matrix products, forward_step(): s = jnp.dot(query, kb.T, preferred_element_type=jnp.float32) * scale  12.5 us
  transfers between devices with their start and end apart: 2, of which 2 were waited for; matrix products, arithmetic and copies ran while one was open for 5% of the time, Pallas kernels for 0%

commit v1 on v0

v1 whole, which is shorter than its diff:
```python
import math

import jax
import jax.numpy as jnp
from jax import lax
from jax.experimental import pallas as pl
from jax.experimental.pallas import tpu as pltpu
from jax.sharding import PartitionSpec as P

NEG = -1e30
BF = jnp.bfloat16
F32 = jnp.float32
N = 256
PACK = 272
SCALE2 = (2.0 / math.sqrt(256)) * math.log2(math.e)
LN2 = math.log(2.0)
NT = (((1,), (1,)), ((), ()))
NN = (((1,), (0,)), ((), ()))


def dot(a, b, dims):
    return lax.dot_general(a, b, dims, preferred_element_type=F32)


def perm(move):
    pairs = []
    for x in range(2):
        for z in range(8):
            for c in range(2):
                x2, z2, c2 = move(x, z, c)
                pairs.append(((x * 8 + z) * 2 + c, (x2 * 8 + z2 % 8) * 2 + c2))
    return pairs


CORE = perm(lambda x, z, c: (x, z, 1 - c))
XX = perm(lambda x, z, c: (1 - x, z, c))
ZZ = perm(lambda x, z, c: (x, z ^ 1, c))
XZ = perm(lambda x, z, c: (1 - x, z ^ 1, c))
UP2 = perm(lambda x, z, c: (x, z + 2, c))
UP4 = perm(lambda x, z, c: (x, z + 4, c))
UP6 = perm(lambda x, z, c: (x, z + 6, c))


def send(array, pairs):
    return lax.ppermute(array, "blk", pairs)


def eye():
    return lax.broadcasted_iota(jnp.int32, (N, N), 0) == lax.broadcasted_iota(
        jnp.int32, (N, N), 1
    )


def to_column(row, diag):
    return jnp.sum(jnp.where(diag, row, 0.0), axis=1, keepdims=True)


def to_row(column, diag):
    return jnp.sum(jnp.where(diag, column, 0.0), axis=0, keepdims=True)


def merge(a, b):
    top = jnp.maximum(a, b)
    return top + jnp.log2(jnp.exp2(a - top) + jnp.exp2(b - top))


def onehot(match_ref):
    return lax.broadcasted_iota(jnp.int32, (N, N), 0) == match_ref[...]


def pack_kernel(count_ref, m1_ref, m2_ref, f1_ref, f2_ref, q_ref, k_ref):
    valid = (lax.broadcasted_iota(jnp.int32, (16, N), 1) < count_ref[0]).astype(F32).astype(BF)
    for m_ref, f_ref, o_ref in ((m1_ref, f1_ref, q_ref), (m2_ref, f2_ref, k_ref)):
        pick = onehot(m_ref).astype(F32).astype(BF)
        o_ref[:N, :] = f_ref[...]
        o_ref[N:, :] = dot(valid, pick, NT).astype(BF)


def pair_kernel(count_ref, m1_ref, m2_ref, f1_ref, f2_ref, pk_ref, pq_ref):
    valid = lax.broadcasted_iota(jnp.int32, (N, N), 1) < count_ref[0]
    one = onehot(m1_ref)
    two = onehot(m2_ref)
    one_valid = (one & valid).astype(F32).astype(BF)
    two_valid = (two & valid).astype(F32).astype(BF)
    to_one = dot(one_valid, two.astype(F32).astype(BF), NT).astype(BF)
    to_two = dot(two_valid, one.astype(F32).astype(BF), NT).astype(BF)
    pk_ref[...] = dot(to_one, f2_ref[...], NN)
    pq_ref[...] = dot(to_two, f1_ref[...], NN)


def load_blocks(q_refs, k_refs, q_all, k_all, q_mask, k_bias):
    for i, ref in enumerate(q_refs):
        q_all[i * N : (i + 1) * N, :] = ref[:N, :]
        q_mask[i : i + 1, :] = ref[N:, :].astype(F32)[:1, :]
    for j, ref in enumerate(k_refs):
        k_all[j * N : (j + 1) * N, :] = ref[:N, :]
        k_bias[:, j * N : (j + 1) * N] = (1.0 - ref[N:, :].astype(F32)[:1, :]) * NEG


def stats_kernel(*refs):
    q_refs, k_refs = refs[:8], refs[8:12]
    rl_ref, cl_ref, q_all, k_all, q_mask, k_bias = refs[12:]
    load_blocks(q_refs, k_refs, q_all, k_all, q_mask, k_bias)
    diag = eye()

    def step(i, carry):
        col_max, col_sum = carry
        q = q_all[pl.ds(pl.multiple_of(i * N, N), N), :]
        t = dot(q, k_all[...], NT) * SCALE2
        row_bias = (1.0 - to_column(q_mask[pl.ds(i, 1), :], diag)) * NEG
        a = t + k_bias[...]
        row_max = jnp.max(a, axis=1, keepdims=True)
        row_sum = jnp.sum(jnp.exp2(a - row_max), axis=1, keepdims=True)
        rl_ref[pl.ds(i, 1), :] = to_row(row_max + jnp.log2(row_sum), diag)
        b = t + row_bias
        top = jnp.max(b, axis=0, keepdims=True)
        new_max = jnp.maximum(col_max, top)
        new_sum = col_sum * jnp.exp2(col_max - new_max) + jnp.sum(
            jnp.exp2(b - new_max), axis=0, keepdims=True
        )
        return new_max, new_sum

    width = 4 * N
    col_max, col_sum = lax.fori_loop(
        0, 8, step, (jnp.full((1, width), NEG, F32), jnp.zeros((1, width), F32))
    )
    col_lse = col_max + jnp.log2(col_sum)
    cl_ref[...] = jnp.zeros((8, N), F32) + jnp.sum(q_mask[...])
    for j in range(4):
        cl_ref[j : j + 1, :] = col_lse[:, j * N : (j + 1) * N]


def core_kernel(a_ref, b_ref, o_ref):
    b = b_ref[...]
    o_ref[...] = merge(a_ref[...], jnp.concatenate([b[4:], b[:4]], axis=0))


def grad_kernel(*refs):
    q_refs, k_refs, r_refs, c_refs = refs[:8], refs[8:12], refs[12:16], refs[16:20]
    dq_own, dq_other, dk_own, dk1, dk2, dk3, lse_ref = refs[20:27]
    q_all, k_all, q_mask, k_bias, row_lse, acc = refs[27:]
    load_blocks(q_refs, k_refs, q_all, k_all, q_mask, k_bias)
    diag = eye()
    rows = r_refs[0][...]
    for step, ref in enumerate(r_refs[1:], start=1):
        other = ref[...]
        order = [i ^ step for i in range(8)]
        other = jnp.concatenate([other[i : i + 1] for i in order], axis=0)
        rows = merge(rows, other)
    row_lse[...] = rows
    cols = c_refs[0][...]
    total = cols[7:8, :]
    parts = [cols[j : j + 1] for j in range(4)]
    for step, ref in enumerate(c_refs[1:], start=1):
        other = ref[...]
        total = total + other[7:8, :]
        parts = [merge(parts[j], other[(j - step) % 4 : (j - step) % 4 + 1]) for j in range(4)]
    lse_ref[...] = jnp.concatenate(
        [rows[:1], parts[0], total, jnp.zeros((5, N), F32)], axis=0
    )
    col_lse = jnp.concatenate(parts, axis=1)
    acc[...] = jnp.zeros_like(acc)

    def step(i, carry):
        q = q_all[pl.ds(pl.multiple_of(i * N, N), N), :]
        t = dot(q, k_all[...], NT) * SCALE2
        row_bias = (1.0 - to_column(q_mask[pl.ds(i, 1), :], diag)) * NEG
        row = to_column(row_lse[pl.ds(i, 1), :], diag)
        t = t + row_bias + k_bias[...]
        w = (jnp.exp2(t - row) + jnp.exp2(t - col_lse)).astype(BF)
        dq = dot(w, k_all[...], NN)

        @pl.when(i < 4)
        def _():
            dq_own[pl.ds(pl.multiple_of(i * N, N), N), :] = dq

        @pl.when(i >= 4)
        def _():
            dq_other[pl.ds(pl.multiple_of((i - 4) * N, N), N), :] = dq.astype(BF)

        acc[...] += dot(q.astype(F32).T.astype(BF), w, NN)
        return carry

    lax.fori_loop(0, 8, step, 0)
    dk_own[...] = acc[:, :N]
    for j, ref in enumerate((dk1, dk2, dk3), start=1):
        ref[...] = acc[:, j * N : (j + 1) * N].astype(BF)


def core_sum_kernel(own_ref, other_ref, a_ref, b1_ref, b2_ref, b3_ref):
    for i, ref in enumerate((a_ref, b1_ref, b2_ref, b3_ref)):
        block = slice(i * N, (i + 1) * N)
        ref[...] = (own_ref[block, :] + other_ref[block, :].astype(F32)).astype(ref.dtype)


def final_kernel(m1_ref, m2_ref, lse_ref, pk_ref, pq_ref, a0, a1, a2, a3, b0, b1, b2, b3, *outs):
    g1, g2, rl, cl = outs
    total = lse_ref[2:3, :1]
    coef = (2.0 / math.sqrt(N)) / (2.0 * total)
    acc = a0[...] + a1[...].astype(F32) + a2[...].astype(F32) + a3[...].astype(F32)
    g1[...] = coef * (acc - 2.0 * pk_ref[...])
    acc = b0[...] + b1[...].astype(F32) + b2[...].astype(F32) + b3[...].astype(F32)
    g2[...] = coef * (acc.T - 2.0 * pq_ref[...])
    diag = eye()
    for at, m_ref, out in ((0, m1_ref, rl), (1, m2_ref, cl)):
        column = to_column(lse_ref[at : at + 1, :], diag)
        out[...] = jnp.sum(jnp.where(onehot(m_ref), column, 0.0), axis=0, keepdims=True) * LN2


def vmem(n):
    return [pl.BlockSpec(memory_space=pltpu.VMEM)] * n


def call(kernel, ins, outs, scratch=(), smem=0, flops=0, trans=0, limit=32):
    return pl.pallas_call(
        kernel,
        out_shape=[jax.ShapeDtypeStruct(s, d) for s, d in outs],
        in_specs=[pl.BlockSpec(memory_space=pltpu.SMEM)] * smem + vmem(len(ins) - smem),
        out_specs=vmem(len(outs)),
        scratch_shapes=list(scratch),
        compiler_params=pltpu.CompilerParams(vmem_limit_bytes=limit * 2**20),
        cost_estimate=pl.CostEstimate(flops=flops, bytes_accessed=2**20, transcendentals=trans),
    )(*ins)


def local(feat_one, feat_two, match_one, match_two, valid_counts):
    ins = (valid_counts, match_one, match_two, feat_one, feat_two)
    qm, km = call(pack_kernel, ins, [((PACK, N), BF)] * 2, smem=1)
    k_all = [km, send(km, UP6), send(km, UP4), send(km, UP2)]
    q_all = [qm, send(qm, XX), send(qm, ZZ), send(qm, XZ)]
    q_all += [send(a, CORE) for a in q_all]
    pk, pq = call(pair_kernel, ins, [((N, N), F32)] * 2, smem=1)
    blocks = [
        pltpu.VMEM((8 * N, N), BF),
        pltpu.VMEM((4 * N, N), BF),
        pltpu.VMEM((8, N), F32),
        pltpu.VMEM((1, 4 * N), F32),
    ]
    size = 2 * 2048 * 1024 * 256
    rl, cl = call(
        stats_kernel, q_all + k_all, [((8, N), F32)] * 2, blocks, flops=size, trans=2**22
    )
    rl_other = send(rl, CORE)
    cl_all = [cl, send(cl, UP2), send(cl, UP4), send(cl, UP6)]
    cl_all = [cl_all[0], cl_all[3], cl_all[2], cl_all[1]]
    (rl,) = call(core_kernel, (rl, rl_other), [((8, N), F32)])
    rl_all = [rl, send(rl, XX), send(rl, ZZ), send(rl, XZ)]
    out = [((4 * N, N), F32), ((4 * N, N), BF), ((N, N), F32)] + [((N, N), BF)] * 3
    dq_own, dq_other, dk0, dk1, dk2, dk3, lse = call(
        grad_kernel,
        q_all + k_all + rl_all + cl_all,
        out + [((8, N), F32)],
        blocks + [pltpu.VMEM((8, N), F32), pltpu.VMEM((N, 4 * N), F32)],
        flops=3 * size,
        trans=2**22,
    )
    dk = [dk0, send(dk1, UP2), send(dk2, UP4), send(dk3, UP6)]
    dq_other = send(dq_other, CORE)
    dq = call(
        core_sum_kernel, (dq_own, dq_other), [((N, N), F32)] + [((N, N), BF)] * 3
    )
    dq = [dq[0], send(dq[1], XX), send(dq[2], ZZ), send(dq[3], XZ)]
    grad_one, grad_two, row_lse, col_lse = call(
        final_kernel,
        [match_one, match_two, lse, pk, pq] + dq + dk,
        [((N, N), F32)] * 2 + [((1, N), F32)] * 2,
    )
    return grad_one, grad_two, row_lse.reshape(N), col_lse.reshape(N)


def solution(mesh):
    both = ("grp", "blk")
    return jax.shard_map(
        local,
        mesh=mesh,
        in_specs=(P(both, None),) * 4 + (P(both),),
        out_specs=(P(both, None), P(both, None), P(both), P(both)),
        check_vma=False,
    )
```

time: 594 us -> 90.7 us (0.15)
  blocking collectives: 341 us -> 0 us
  waiting for transfers between devices: 162 us -> 24.2 us
  starting transfers between devices: 0.08 us -> 42.3 us
  matrix products: 39.5 us -> 0 us
  other arithmetic: 22.8 us -> 0 us
  Pallas kernels: 0 us -> 19 us
  between operations: 16.3 us -> 1.4 us
    unnamed x1 -> x0, blocking collectives: 128 us -> none
    pmax x1 -> x0, blocking collectives: 124 us -> none  [local(): peak = lax.pmax(col_max.astype(jnp.bfloat16), 'blk').astype(col_max.dtype)]
    reduce_scatter x1 -> x0, waiting for transfers between devices: 121 us -> none  [local(): lax.psum_scatter(lax.dot_general(weight, query, (((0,), (0,)), ((), ())),...]
    all_gather x2 -> x0, blocking collectives: 88.2 us -> none  [the longest x1 46 us: local(): lax.all_gather(valid_bf, 'blk', axis=0, tiled=True)]
    ppermute x0 -> x24, starting transfers between devices: none -> 42.3 us  [send(): return lax.ppermute(array, 'blk', pairs)]
    all_gather x1 -> x0, waiting for transfers between devices: 41 us -> none  [local(): lax.all_gather(keys, 'blk', axis=0, tiled=True)]
    dot_general x17 -> x0, matrix products: 39.5 us -> none  [the longest x8 17.2 us: query_step(): return (acc + jnp.dot(weight, kb, preferred_element_type=jnp.float32), None)]
    ppermute x0 -> x24, waiting for transfers between devices: none -> 24.2 us  [send(): return lax.ppermute(array, 'blk', pairs)]
  transfers between devices with their start and end apart: 2 -> 24, of which waited for: 2 -> 11; matrix products, arithmetic and copies ran while one was open for 5% -> 0% of each run, Pallas kernels for 0% -> 1%
where the time goes in v1:
time: 90.7 us; the launch traced here: 89.4 us
  starting transfers between devices  42.3 us (47%)
  waiting for transfers between devices  24.2 us (27%)
  Pallas kernels  19 us (21%)
  local copies, waits for them, and re-layouts  2.5 us (3%)
  between operations  1.4 us (2%)
    ppermute x24, starting transfers between devices, send(): return lax.ppermute(array, 'blk', pairs)  42.3 us
    ppermute x24, waiting for transfers between devices, send(): return lax.ppermute(array, 'blk', pairs)  24.2 us
    pallas_call x7, Pallas kernels, call(): pl.pallas_call(kernel, out_shape=[jax.ShapeDtypeStruct(s, d) for s, d in...  19 us
    unnamed x14, local copies, waits for them, and re-layouts  2.5 us
  transfers between devices with their start and end apart: 24, of which 11 were waited for; matrix products, arithmetic and copies ran while one was open for 0% of the time, Pallas kernels for 1%

profile of v1, /device:TPU:1, one launch (start us, length us, event | category | flops | bytes accessed | tf_op | source)
XLA Modules:
  0.0 89.4 jit_solution(15192434250928730793)
XLA Ops:
  0.6 0.0 copy-start.4
  1.3 0.0 copy-done.4
  1.3 0.0 copy-start
  1.3 0.9 %copy-done = bf16[256,256]{1,0:T(8,128)(2,1)S(1)} copy-done((bf16[256,256]{1,0:T(8,128)(2,1)S(1)}, bf16[256,256]{1,0:T(8,128)(2,1)}, u32[]{:S(2)}) %copy-start) | copy-done | bytes 131096
  2.2 0.0 copy-start.2
  2.2 0.9 %copy-done.2 = bf16[256,256]{1,0:T(8,128)(2,1)S(1)} copy-done((bf16[256,256]{1,0:T(8,128)(2,1)S(1)}, bf16[256,256]{1,0:T(8,128)(2,1)}, u32[]{:S(2)}) %copy-start.2) | copy-done | bytes 131096
  3.1 0.7 copy-done.5
  3.8 0.2 shard_map.84
  4.0 3.8 %collective-permute-start.9 = (bf16[272,256]{1,0:T(8,128)(2,1)S(1)}, bf16[272,256]{1,0:T(8,128)(2,1)S(1)}, u32[]{:S(2)}, u32[]{:S(2)}) collective-permute-start(bf16[272,256]{1,0:T(8,128)(2,1)S(1)} %get-tuple-element.26.refs_8_), channel_id=1, source_target_pairs={{0,4},{1,5},{2,6},{3,7},{4,8},{5,9},{6,10},{7,11},{8,12},{9,13},{1... | collective-permute-start | bytes 417800 | tf_op jit(solution)/shard_map/ppermute | solution.py:45
  7.8 5.1 %collective-permute-start.8 = (bf16[272,256]{1,0:T(8,128)(2,1)S(1)}, bf16[272,256]{1,0:T(8,128)(2,1)S(1)}, u32[]{:S(2)}, u32[]{:S(2)}) collective-permute-start(bf16[272,256]{1,0:T(8,128)(2,1)S(1)} %get-tuple-element.26.refs_8_), channel_id=1, source_target_pairs={{0,8},{1,9},{2,10},{3,11},{4,12},{5,13},{6,14},{7,15},{8,0},{9,1},... | collective-permute-start | bytes 417800 | tf_op jit(solution)/shard_map/ppermute | solution.py:45
  12.9 3.2 %collective-permute-start.2 = (bf16[272,256]{1,0:T(8,128)(2,1)S(1)}, bf16[272,256]{1,0:T(8,128)(2,1)S(1)}, u32[]{:S(2)}, u32[]{:S(2)}) collective-permute-start(bf16[272,256]{1,0:T(8,128)(2,1)S(1)} %get-tuple-element.25.refs_0_), channel_id=1, source_target_pairs={{0,18},{1,19},{2,16},{3,17},{4,22},{5,23},{6,20},{7,21},{8,26},{9,... | collective-permute-start | bytes 417800 | tf_op jit(solution)/shard_map/ppermute | solution.py:45
  16.1 0.7 collective-permute-start.1
  16.9 0.2 collective-permute-start
  17.1 0.0 collective-permute-done.9.refs_11_
  17.1 2.4 %collective-permute-start.7 = (bf16[272,256]{1,0:T(8,128)(2,1)S(1)}, bf16[272,256]{1,0:T(8,128)(2,1)S(1)}, u32[]{:S(2)}, u32[]{:S(2)}) collective-permute-start(bf16[272,256]{1,0:T(8,128)(2,1)S(1)} %get-tuple-element.26.refs_8_), channel_id=1, source_target_pairs={{0,12},{1,13},{2,14},{3,15},{4,0},{5,1},{6,2},{7,3},{8,4},{9,5},{1... | collective-permute-start | bytes 417800 | tf_op jit(solution)/shard_map/ppermute | solution.py:45
  19.5 2.6 %collective-permute-done.8.refs_10_ = bf16[272,256]{1,0:T(8,128)(2,1)S(1)} collective-permute-done((bf16[272,256]{1,0:T(8,128)(2,1)S(1)}, bf16[272,256]{1,0:T(8,128)(2,1)S(1)}, u32[]{:S(2)}, u32[]{:S(2)}) %collective-permute-start.8) | collective-permute-done | bytes 139296 | tf_op jit(solution)/shard_map/ppermute | solution.py:45
  22.1 3.1 %collective-permute-start.3 = (bf16[272,256]{1,0:T(8,128)(2,1)S(1)}, bf16[272,256]{1,0:T(8,128)(2,1)S(1)}, u32[]{:S(2)}, u32[]{:S(2)}) collective-permute-start(bf16[272,256]{1,0:T(8,128)(2,1)S(1)} %get-tuple-element.25.refs_0_), channel_id=1, source_target_pairs={{0,1},{1,0},{2,3},{3,2},{4,5},{5,4},{6,7},{7,6},{8,9},{9,8},{10,11... | collective-permute-start | bytes 417800 | tf_op jit(solution)/shard_map/ppermute | solution.py:45
  25.2 3.4 %collective-permute-done.2.refs_3_ = bf16[272,256]{1,0:T(8,128)(2,1)S(1)} collective-permute-done((bf16[272,256]{1,0:T(8,128)(2,1)S(1)}, bf16[272,256]{1,0:T(8,128)(2,1)S(1)}, u32[]{:S(2)}, u32[]{:S(2)}) %collective-permute-start.2) | collective-permute-done | bytes 139296 | tf_op jit(solution)/shard_map/ppermute | solution.py:45
  28.6 1.4 %collective-permute-start.6 = (bf16[272,256]{1,0:T(8,128)(2,1)S(1)}, bf16[272,256]{1,0:T(8,128)(2,1)S(1)}, u32[]{:S(2)}, u32[]{:S(2)}) collective-permute-start(bf16[272,256]{1,0:T(8,128)(2,1)S(1)} %collective-permute-done.2.refs_3_), channel_id=1, source_target_pairs={{0,1},{1,0},{2,3},{3,2},{4,5},{5,4},{6,7},{7,6},{8,9},{9,8},{10,11... | collective-permute-start | bytes 417800 | tf_op jit(solution)/shard_map/ppermute | solution.py:45
  30.0 0.0 collective-permute-done.1.refs_2_
  30.0 0.5 collective-permute-start.5
  30.5 0.0 collective-permute-done.refs_1_
  30.5 0.0 collective-permute-start.4
  30.5 0.0 collective-permute-done.7.refs_9_
  30.5 0.0 collective-permute-done.3.refs_4_
  30.5 0.5 collective-permute-done.6.refs_7_
  31.0 0.5 collective-permute-done.5.refs_6_
  31.5 0.4 collective-permute-done.4.refs_5_
  31.9 6.9 %shard_map.85 = (f32[8,256]{1,0:T(8,128)S(1)}, f32[8,256]{1,0:T(8,128)S(1)}) custom-call(bf16[272,256]{1,0:T(8,128)(2,1)S(1)} %get-tuple-element.25.refs_0_, bf16[272,256]{1,0:T(8,128)(2,1)S(1)} %collective-permute-done.refs_1_, bf16[272,256]{1,0:T(8,128)(2,1)S(1)} %collective-permute-done.1.refs_2_, bf16[272,256]{1,0:T(8,128)(2,1)S(1)} %collective-permute-done.2.refs_3_, ...), custom_call_target="tpu_custom_call" | custom-call | flops 1073741824 | bytes 1048576 | tf_op jit(solution)/shard_map/pallas_call | solution.py:215
  38.8 0.3 collective-permute-start.10
  39.1 0.9 %collective-permute-start.16 = (f32[8,256]{1,0:T(8,128)S(1)}, f32[8,256]{1,0:T(8,128)S(1)}, u32[]{:S(2)}, u32[]{:S(2)}) collective-permute-start(f32[8,256]{1,0:T(8,128)S(1)} %get-tuple-element.28.refs_16_), channel_id=1, source_target_pairs={{0,4},{1,5},{2,6},{3,7},{4,8},{5,9},{6,10},{7,11},{8,12},{9,13},{1... | collective-permute-start | bytes 24584 | tf_op jit(solution)/shard_map/ppermute | solution.py:45
  40.0 4.5 %collective-permute-start.15 = (f32[8,256]{1,0:T(8,128)S(1)}, f32[8,256]{1,0:T(8,128)S(1)}, u32[]{:S(2)}, u32[]{:S(2)}) collective-permute-start(f32[8,256]{1,0:T(8,128)S(1)} %get-tuple-element.28.refs_16_), channel_id=1, source_target_pairs={{0,8},{1,9},{2,10},{3,11},{4,12},{5,13},{6,14},{7,15},{8,0},{9,1},... | collective-permute-start | bytes 24584 | tf_op jit(solution)/shard_map/ppermute | solution.py:45
  44.5 0.0 collective-permute-start.14
  44.5 0.0 collective-permute-done.10.b_ref
  44.5 6.4 %collective-permute-start.13 = (f32[8,256]{1,0:T(8,128)S(1)}, f32[8,256]{1,0:T(8,128)S(1)}, u32[]{:S(2)}, u32[]{:S(2)}) collective-permute-start(f32[8,256]{1,0:T(8,128)S(1)} %shard_map.86.refs_12_), channel_id=1, source_target_pairs={{0,18},{1,19},{2,16},{3,17},{4,22},{5,23},{6,20},{7,21},{8,26},{9,... | collective-permute-start | bytes 24584 | tf_op jit(solution)/shard_map/ppermute | solution.py:45
  50.9 0.0 collective-permute-start.12
  50.9 0.0 collective-permute-done.16.refs_19_
  50.9 0.4 collective-permute-start.11
  51.3 0.0 collective-permute-done.15.refs_18_
  51.3 0.0 collective-permute-done.14.refs_17_
  51.3 0.7 collective-permute-done.13.refs_15_
  52.0 1.4 %collective-permute-done.12.refs_14_ = f32[8,256]{1,0:T(8,128)S(1)} collective-permute-done((f32[8,256]{1,0:T(8,128)S(1)}, f32[8,256]{1,0:T(8,128)S(1)}, u32[]{:S(2)}, u32[]{:S(2)}) %collective-permute-start.12) | collective-permute-done | bytes 8224 | tf_op jit(solution)/shard_map/ppermute | solution.py:45
  53.4 1.5 %collective-permute-done.11.refs_13_ = f32[8,256]{1,0:T(8,128)S(1)} collective-permute-done((f32[8,256]{1,0:T(8,128)S(1)}, f32[8,256]{1,0:T(8,128)S(1)}, u32[]{:S(2)}, u32[]{:S(2)}) %collective-permute-start.11) | collective-permute-done | bytes 8224 | tf_op jit(solution)/shard_map/ppermute | solution.py:45
  54.9 10.3 %shard_map.87 = (f32[1024,256]{1,0:T(8,128)S(1)}, bf16[1024,256]{1,0:T(8,128)(2,1)S(1)}, f32[256,256]{1,0:T(8,128)S(1)}, bf16[256,256]{1,0:T(8,128)(2,1)S(1)}, b...) custom-call(bf16[272,256]{1,0:T(8,128)(2,1)S(1)} %get-tuple-element.25.refs_0_, ...), custom_call_target="tpu_custom_call" | custom-call | flops 3221225472 | bytes 1048576 | tf_op jit(solution)/shard_map/pallas_call | solution.py:215
  65.2 2.4 %collective-permute-start.17 = (bf16[1024,256]{1,0:T(8,128)(2,1)S(1)}, bf16[1024,256]{1,0:T(8,128)(2,1)S(1)}, u32[]{:S(2)}, u32[]{:S(2)}) collective-permute-start(bf16[1024,256]{1,0:T(8,128)(2,1)S(1)} %get-tuple-element.33), channel_id=1, source_target_pairs={{0,1},{1,0},{2,3},{3,2},{4,5},{5,4},{6,7},{7,6},{8,9},{9,8},{10,11... | collective-permute-start | bytes 1572872 | tf_op jit(solution)/shard_map/ppermute | solution.py:45
  67.6 0.7 collective-permute-start.21
  68.4 1.1 %collective-permute-start.22 = (bf16[256,256]{1,0:T(8,128)(2,1)S(1)}, bf16[256,256]{1,0:T(8,128)(2,1)S(1)}, u32[]{:S(2)}, u32[]{:S(2)}) collective-permute-start(bf16[256,256]{1,0:T(8,128)(2,1)S(1)} %get-tuple-element.40), channel_id=1, source_target_pairs={{0,8},{1,9},{2,10},{3,11},{4,12},{5,13},{6,14},{7,15},{8,0},{9,1},... | collective-permute-start | bytes 393224 | tf_op jit(solution)/shard_map/ppermute | solution.py:45
  69.4 3.5 %collective-permute-start.23 = (bf16[256,256]{1,0:T(8,128)(2,1)S(1)}, bf16[256,256]{1,0:T(8,128)(2,1)S(1)}, u32[]{:S(2)}, u32[]{:S(2)}) collective-permute-start(bf16[256,256]{1,0:T(8,128)(2,1)S(1)} %get-tuple-element.41), channel_id=1, source_target_pairs={{0,12},{1,13},{2,14},{3,15},{4,0},{5,1},{6,2},{7,3},{8,4},{9,5},{1... | collective-permute-start | bytes 393224 | tf_op jit(solution)/shard_map/ppermute | solution.py:45
  72.9 0.0 collective-permute-done.17.other_ref
  72.9 0.1 shard_map.89
  73.0 0.3 collective-permute-start.18
  73.4 1.0 %collective-permute-start.19 = (bf16[256,256]{1,0:T(8,128)(2,1)S(1)}, bf16[256,256]{1,0:T(8,128)(2,1)S(1)}, u32[]{:S(2)}, u32[]{:S(2)}) collective-permute-start(bf16[256,256]{1,0:T(8,128)(2,1)S(1)} %get-tuple-element.36), channel_id=1, source_target_pairs={{0,2},{1,3},{2,0},{3,1},{4,6},{5,7},{6,4},{7,5},{8,10},{9,11},{10,... | collective-permute-start | bytes 393224 | tf_op jit(solution)/shard_map/ppermute | solution.py:45
  74.4 5.9 %collective-permute-done.21.b1 = bf16[256,256]{1,0:T(8,128)(2,1)S(1)} collective-permute-done((bf16[256,256]{1,0:T(8,128)(2,1)S(1)}, bf16[256,256]{1,0:T(8,128)(2,1)S(1)}, u32[]{:S(2)}, u32[]{:S(2)}) %collective-permute-start.21) | collective-permute-done | bytes 131104 | tf_op jit(solution)/shard_map/ppermute | solution.py:45
  80.3 0.3 collective-permute-start.20
  80.6 0.0 copy-done.1
  80.6 0.0 copy-done.3
  80.6 0.0 copy-done.6
  80.6 0.4 shard_map.88
  81.0 0.0 collective-permute-done.22.b2
  81.1 0.0 collective-permute-done.23.b3
  81.1 0.0 collective-permute-done.18.a1
  81.1 4.9 %collective-permute-done.19.a2 = bf16[256,256]{1,0:T(8,128)(2,1)S(1)} collective-permute-done((bf16[256,256]{1,0:T(8,128)(2,1)S(1)}, bf16[256,256]{1,0:T(8,128)(2,1)S(1)}, u32[]{:S(2)}, u32[]{:S(2)}) %collective-permute-start.19) | collective-permute-done | bytes 131104 | tf_op jit(solution)/shard_map/ppermute | solution.py:45
  86.0 2.3 %collective-permute-done.20.a3 = bf16[256,256]{1,0:T(8,128)(2,1)S(1)} collective-permute-done((bf16[256,256]{1,0:T(8,128)(2,1)S(1)}, bf16[256,256]{1,0:T(8,128)(2,1)S(1)}, u32[]{:S(2)}, u32[]{:S(2)}) %collective-permute-start.20) | collective-permute-done | bytes 131104 | tf_op jit(solution)/shard_map/ppermute | solution.py:45
  88.3 1.0 %shard_map.90 = (f32[256,256]{1,0:T(8,128)}, f32[256,256]{1,0:T(8,128)}, f32[1,256]{1,0:T(1,128)}, f32[1,256]{1,0:T(1,128)}) custom-call(s32[1,256]{1,0:T(1,128)S(1)} %copy-done.4, s32[1,256]{1,0:T(1,128)S(1)} %copy-done.6, f32[8,256]{1,0:T(8,128)S(1)} %get-tuple-element.29.lse_ref, f32[256,256]{1,0:T(8,128)S(1)} %get-tuple-element.30.pk_ref, ...), custom_call_target="tpu_custom_call" | custom-call | bytes 1048576 | tf_op jit(solution)/shard_map/pallas_call | solution.py:215
  (5 shorter events, 0.0 us)
Async XLA Ops:
  0.6 0.7 copy-start.4
  1.3 0.9 %copy-start = (bf16[256,256]{1,0:T(8,128)(2,1)S(1)}, bf16[256,256]{1,0:T(8,128)(2,1)}, u32[]{:S(2)}) copy-start(bf16[256,256]{1,0:T(8,128)(2,1)} %f1_ref.3) | copy-start | bytes 393220
  2.2 0.9 %copy-start.2 = (bf16[256,256]{1,0:T(8,128)(2,1)S(1)}, bf16[256,256]{1,0:T(8,128)(2,1)}, u32[]{:S(2)}) copy-start(bf16[256,256]{1,0:T(8,128)(2,1)} %f2_ref.3) | copy-start | bytes 393220
  3.1 0.7 copy-start.5
  4.0 13.1 %collective-permute-start.9 = (bf16[272,256]{1,0:T(8,128)(2,1)S(1)}, bf16[272,256]{1,0:T(8,128)(2,1)S(1)}, u32[]{:S(2)}, u32[]{:S(2)}) collective-permute-start(bf16[272,256]{1,0:T(8,128)(2,1)S(1)} %get-tuple-element.26.refs_8_), channel_id=1, source_target_pairs={{0,4},{1,5},{2,6},{3,7},{4,8},{5,9},{6,10},{7,11},{8,12},{9,13},{1... | collective-permute-start | bytes 417800 | tf_op jit(solution)/shard_map/ppermute | solution.py:45
  7.8 14.2 %collective-permute-start.8 = (bf16[272,256]{1,0:T(8,128)(2,1)S(1)}, bf16[272,256]{1,0:T(8,128)(2,1)S(1)}, u32[]{:S(2)}, u32[]{:S(2)}) collective-permute-start(bf16[272,256]{1,0:T(8,128)(2,1)S(1)} %get-tuple-element.26.refs_8_), channel_id=1, source_target_pairs={{0,8},{1,9},{2,10},{3,11},{4,12},{5,13},{6,14},{7,15},{8,0},{9,1},... | collective-permute-start | bytes 417800 | tf_op jit(solution)/shard_map/ppermute | solution.py:45
  12.9 15.7 %collective-permute-start.2 = (bf16[272,256]{1,0:T(8,128)(2,1)S(1)}, bf16[272,256]{1,0:T(8,128)(2,1)S(1)}, u32[]{:S(2)}, u32[]{:S(2)}) collective-permute-start(bf16[272,256]{1,0:T(8,128)(2,1)S(1)} %get-tuple-element.25.refs_0_), channel_id=1, source_target_pairs={{0,18},{1,19},{2,16},{3,17},{4,22},{5,23},{6,20},{7,21},{8,26},{9,... | collective-permute-start | bytes 417800 | tf_op jit(solution)/shard_map/ppermute | solution.py:45
  16.1 13.8 %collective-permute-start.1 = (bf16[272,256]{1,0:T(8,128)(2,1)S(1)}, bf16[272,256]{1,0:T(8,128)(2,1)S(1)}, u32[]{:S(2)}, u32[]{:S(2)}) collective-permute-start(bf16[272,256]{1,0:T(8,128)(2,1)S(1)} %get-tuple-element.25.refs_0_), channel_id=1, source_target_pairs={{0,2},{1,3},{2,0},{3,1},{4,6},{5,7},{6,4},{7,5},{8,10},{9,11},{10,... | collective-permute-start | bytes 417800 | tf_op jit(solution)/shard_map/ppermute | solution.py:45
  16.9 13.6 %collective-permute-start = (bf16[272,256]{1,0:T(8,128)(2,1)S(1)}, bf16[272,256]{1,0:T(8,128)(2,1)S(1)}, u32[]{:S(2)}, u32[]{:S(2)}) collective-permute-start(bf16[272,256]{1,0:T(8,128)(2,1)S(1)} %get-tuple-element.25.refs_0_), channel_id=1, source_target_pairs={{0,16},{1,17},{2,18},{3,19},{4,20},{5,21},{6,22},{7,23},{8,24},{9,... | collective-permute-start | bytes 417800 | tf_op jit(solution)/shard_map/ppermute | solution.py:45
  17.1 13.4 %collective-permute-start.7 = (bf16[272,256]{1,0:T(8,128)(2,1)S(1)}, bf16[272,256]{1,0:T(8,128)(2,1)S(1)}, u32[]{:S(2)}, u32[]{:S(2)}) collective-permute-start(bf16[272,256]{1,0:T(8,128)(2,1)S(1)} %get-tuple-element.26.refs_8_), channel_id=1, source_target_pairs={{0,12},{1,13},{2,14},{3,15},{4,0},{5,1},{6,2},{7,3},{8,4},{9,5},{1... | collective-permute-start | bytes 417800 | tf_op jit(solution)/shard_map/ppermute | solution.py:45
  22.1 8.5 %collective-permute-start.3 = (bf16[272,256]{1,0:T(8,128)(2,1)S(1)}, bf16[272,256]{1,0:T(8,128)(2,1)S(1)}, u32[]{:S(2)}, u32[]{:S(2)}) collective-permute-start(bf16[272,256]{1,0:T(8,128)(2,1)S(1)} %get-tuple-element.25.refs_0_), channel_id=1, source_target_pairs={{0,1},{1,0},{2,3},{3,2},{4,5},{5,4},{6,7},{7,6},{8,9},{9,8},{10,11... | collective-permute-start | bytes 417800 | tf_op jit(solution)/shard_map/ppermute | solution.py:45
  28.6 2.4 %collective-permute-start.6 = (bf16[272,256]{1,0:T(8,128)(2,1)S(1)}, bf16[272,256]{1,0:T(8,128)(2,1)S(1)}, u32[]{:S(2)}, u32[]{:S(2)}) collective-permute-start(bf16[272,256]{1,0:T(8,128)(2,1)S(1)} %collective-permute-done.2.refs_3_), channel_id=1, source_target_pairs={{0,1},{1,0},{2,3},{3,2},{4,5},{5,4},{6,7},{7,6},{8,9},{9,8},{10,11... | collective-permute-start | bytes 417800 | tf_op jit(solution)/shard_map/ppermute | solution.py:45
  30.0 1.5 %collective-permute-start.5 = (bf16[272,256]{1,0:T(8,128)(2,1)S(1)}, bf16[272,256]{1,0:T(8,128)(2,1)S(1)}, u32[]{:S(2)}, u32[]{:S(2)}) collective-permute-start(bf16[272,256]{1,0:T(8,128)(2,1)S(1)} %collective-permute-done.1.refs_2_), channel_id=1, source_target_pairs={{0,1},{1,0},{2,3},{3,2},{4,5},{5,4},{6,7},{7,6},{8,9},{9,8},{10,11... | collective-permute-start | bytes 417800 | tf_op jit(solution)/shard_map/ppermute | solution.py:45
  30.5 1.4 %collective-permute-start.4 = (bf16[272,256]{1,0:T(8,128)(2,1)S(1)}, bf16[272,256]{1,0:T(8,128)(2,1)S(1)}, u32[]{:S(2)}, u32[]{:S(2)}) collective-permute-start(bf16[272,256]{1,0:T(8,128)(2,1)S(1)} %collective-permute-done.refs_1_), channel_id=1, source_target_pairs={{0,1},{1,0},{2,3},{3,2},{4,5},{5,4},{6,7},{7,6},{8,9},{9,8},{10,11... | collective-permute-start | bytes 417800 | tf_op jit(solution)/shard_map/ppermute | solution.py:45
  38.8 5.7 %collective-permute-start.10 = (f32[8,256]{1,0:T(8,128)S(1)}, f32[8,256]{1,0:T(8,128)S(1)}, u32[]{:S(2)}, u32[]{:S(2)}) collective-permute-start(f32[8,256]{1,0:T(8,128)S(1)} %get-tuple-element.27.a_ref), channel_id=1, source_target_pairs={{0,1},{1,0},{2,3},{3,2},{4,5},{5,4},{6,7},{7,6},{8,9},{9,8},{10,11... | collective-permute-start | bytes 24584 | tf_op jit(solution)/shard_map/ppermute | solution.py:45
  39.1 11.8 %collective-permute-start.16 = (f32[8,256]{1,0:T(8,128)S(1)}, f32[8,256]{1,0:T(8,128)S(1)}, u32[]{:S(2)}, u32[]{:S(2)}) collective-permute-start(f32[8,256]{1,0:T(8,128)S(1)} %get-tuple-element.28.refs_16_), channel_id=1, source_target_pairs={{0,4},{1,5},{2,6},{3,7},{4,8},{5,9},{6,10},{7,11},{8,12},{9,13},{1... | collective-permute-start | bytes 24584 | tf_op jit(solution)/shard_map/ppermute | solution.py:45
  40.0 11.3 %collective-permute-start.15 = (f32[8,256]{1,0:T(8,128)S(1)}, f32[8,256]{1,0:T(8,128)S(1)}, u32[]{:S(2)}, u32[]{:S(2)}) collective-permute-start(f32[8,256]{1,0:T(8,128)S(1)} %get-tuple-element.28.refs_16_), channel_id=1, source_target_pairs={{0,8},{1,9},{2,10},{3,11},{4,12},{5,13},{6,14},{7,15},{8,0},{9,1},... | collective-permute-start | bytes 24584 | tf_op jit(solution)/shard_map/ppermute | solution.py:45
  44.5 6.8 %collective-permute-start.14 = (f32[8,256]{1,0:T(8,128)S(1)}, f32[8,256]{1,0:T(8,128)S(1)}, u32[]{:S(2)}, u32[]{:S(2)}) collective-permute-start(f32[8,256]{1,0:T(8,128)S(1)} %get-tuple-element.28.refs_16_), channel_id=1, source_target_pairs={{0,12},{1,13},{2,14},{3,15},{4,0},{5,1},{6,2},{7,3},{8,4},{9,5},{1... | collective-permute-start | bytes 24584 | tf_op jit(solution)/shard_map/ppermute | solution.py:45
  44.5 7.5 %collective-permute-start.13 = (f32[8,256]{1,0:T(8,128)S(1)}, f32[8,256]{1,0:T(8,128)S(1)}, u32[]{:S(2)}, u32[]{:S(2)}) collective-permute-start(f32[8,256]{1,0:T(8,128)S(1)} %shard_map.86.refs_12_), channel_id=1, source_target_pairs={{0,18},{1,19},{2,16},{3,17},{4,22},{5,23},{6,20},{7,21},{8,26},{9,... | collective-permute-start | bytes 24584 | tf_op jit(solution)/shard_map/ppermute | solution.py:45
  50.9 2.5 %collective-permute-start.12 = (f32[8,256]{1,0:T(8,128)S(1)}, f32[8,256]{1,0:T(8,128)S(1)}, u32[]{:S(2)}, u32[]{:S(2)}) collective-permute-start(f32[8,256]{1,0:T(8,128)S(1)} %shard_map.86.refs_12_), channel_id=1, source_target_pairs={{0,2},{1,3},{2,0},{3,1},{4,6},{5,7},{6,4},{7,5},{8,10},{9,11},{10,... | collective-permute-start | bytes 24584 | tf_op jit(solution)/shard_map/ppermute | solution.py:45
  50.9 4.0 %collective-permute-start.11 = (f32[8,256]{1,0:T(8,128)S(1)}, f32[8,256]{1,0:T(8,128)S(1)}, u32[]{:S(2)}, u32[]{:S(2)}) collective-permute-start(f32[8,256]{1,0:T(8,128)S(1)} %shard_map.86.refs_12_), channel_id=1, source_target_pairs={{0,16},{1,17},{2,18},{3,19},{4,20},{5,21},{6,22},{7,23},{8,24},{9,... | collective-permute-start | bytes 24584 | tf_op jit(solution)/shard_map/ppermute | solution.py:45
  65.2 7.7 %collective-permute-start.17 = (bf16[1024,256]{1,0:T(8,128)(2,1)S(1)}, bf16[1024,256]{1,0:T(8,128)(2,1)S(1)}, u32[]{:S(2)}, u32[]{:S(2)}) collective-permute-start(bf16[1024,256]{1,0:T(8,128)(2,1)S(1)} %get-tuple-element.33), channel_id=1, source_target_pairs={{0,1},{1,0},{2,3},{3,2},{4,5},{5,4},{6,7},{7,6},{8,9},{9,8},{10,11... | collective-permute-start | bytes 1572872 | tf_op jit(solution)/shard_map/ppermute | solution.py:45
  67.6 12.7 %collective-permute-start.21 = (bf16[256,256]{1,0:T(8,128)(2,1)S(1)}, bf16[256,256]{1,0:T(8,128)(2,1)S(1)}, u32[]{:S(2)}, u32[]{:S(2)}) collective-permute-start(bf16[256,256]{1,0:T(8,128)(2,1)S(1)} %get-tuple-element.39), channel_id=1, source_target_pairs={{0,4},{1,5},{2,6},{3,7},{4,8},{5,9},{6,10},{7,11},{8,12},{9,13},{1... | collective-permute-start | bytes 393224 | tf_op jit(solution)/shard_map/ppermute | solution.py:45
  68.4 12.7 %collective-permute-start.22 = (bf16[256,256]{1,0:T(8,128)(2,1)S(1)}, bf16[256,256]{1,0:T(8,128)(2,1)S(1)}, u32[]{:S(2)}, u32[]{:S(2)}) collective-permute-start(bf16[256,256]{1,0:T(8,128)(2,1)S(1)} %get-tuple-element.40), channel_id=1, source_target_pairs={{0,8},{1,9},{2,10},{3,11},{4,12},{5,13},{6,14},{7,15},{8,0},{9,1},... | collective-permute-start | bytes 393224 | tf_op jit(solution)/shard_map/ppermute | solution.py:45
  69.4 11.6 %collective-permute-start.23 = (bf16[256,256]{1,0:T(8,128)(2,1)S(1)}, bf16[256,256]{1,0:T(8,128)(2,1)S(1)}, u32[]{:S(2)}, u32[]{:S(2)}) collective-permute-start(bf16[256,256]{1,0:T(8,128)(2,1)S(1)} %get-tuple-element.41), channel_id=1, source_target_pairs={{0,12},{1,13},{2,14},{3,15},{4,0},{5,1},{6,2},{7,3},{8,4},{9,5},{1... | collective-permute-start | bytes 393224 | tf_op jit(solution)/shard_map/ppermute | solution.py:45
  72.9 7.7 %copy-start.1 = (bf16[256,256]{1,0:T(8,128)(2,1)S(1)}, bf16[256,256]{1,0:T(8,128)(2,1)}, u32[]{:S(2)}) copy-start(bf16[256,256]{1,0:T(8,128)(2,1)} %f1_ref.3) | copy-start | bytes 393220
  72.9 7.7 %copy-start.3 = (bf16[256,256]{1,0:T(8,128)(2,1)S(1)}, bf16[256,256]{1,0:T(8,128)(2,1)}, u32[]{:S(2)}) copy-start(bf16[256,256]{1,0:T(8,128)(2,1)} %f2_ref.3) | copy-start | bytes 393220
  73.0 8.0 %collective-permute-start.18 = (bf16[256,256]{1,0:T(8,128)(2,1)S(1)}, bf16[256,256]{1,0:T(8,128)(2,1)S(1)}, u32[]{:S(2)}, u32[]{:S(2)}) collective-permute-start(bf16[256,256]{1,0:T(8,128)(2,1)S(1)} %get-tuple-element.35), channel_id=1, source_target_pairs={{0,16},{1,17},{2,18},{3,19},{4,20},{5,21},{6,22},{7,23},{8,24},{9,... | collective-permute-start | bytes 393224 | tf_op jit(solution)/shard_map/ppermute | solution.py:45
  73.4 7.3 %copy-start.6 = (s32[1,256]{1,0:T(1,128)S(1)}, s32[1,256]{1,0:T(1,128)}, u32[]{:S(2)}) copy-start(s32[1,256]{1,0:T(1,128)} %m2_ref.5) | copy-start | bytes 3076
  73.4 12.6 %collective-permute-start.19 = (bf16[256,256]{1,0:T(8,128)(2,1)S(1)}, bf16[256,256]{1,0:T(8,128)(2,1)S(1)}, u32[]{:S(2)}, u32[]{:S(2)}) collective-permute-start(bf16[256,256]{1,0:T(8,128)(2,1)S(1)} %get-tuple-element.36), channel_id=1, source_target_pairs={{0,2},{1,3},{2,0},{3,1},{4,6},{5,7},{6,4},{7,5},{8,10},{9,11},{10,... | collective-permute-start | bytes 393224 | tf_op jit(solution)/shard_map/ppermute | solution.py:45
  80.3 8.0 %collective-permute-start.20 = (bf16[256,256]{1,0:T(8,128)(2,1)S(1)}, bf16[256,256]{1,0:T(8,128)(2,1)S(1)}, u32[]{:S(2)}, u32[]{:S(2)}) collective-permute-start(bf16[256,256]{1,0:T(8,128)(2,1)S(1)} %get-tuple-element.37), channel_id=1, source_target_pairs={{0,18},{1,19},{2,16},{3,17},{4,22},{5,23},{6,20},{7,21},{8,26},{9,... | collective-permute-start | bytes 393224 | tf_op jit(solution)/shard_map/ppermute | solution.py:45

commit v2 on v1

v2 whole, which is shorter than its diff:
```python
import math

import jax
import jax.numpy as jnp
from jax import lax
from jax.experimental import pallas as pl
from jax.experimental.pallas import tpu as pltpu
from jax.sharding import PartitionSpec as P

NEG = -1e30
BF = jnp.bfloat16
F32 = jnp.float32
N = 256
PACK = 272
SCALE2 = (2.0 / math.sqrt(256)) * math.log2(math.e)
LN2 = math.log(2.0)
NT = (((1,), (1,)), ((), ()))
NN = (((1,), (0,)), ((), ()))
ARRIVAL = [(0, 0), (0, 1)]
for hop in (1, 2, 3):
    ARRIVAL += [(-hop, 0), (hop, 0), (-hop, 1), (hop, 1)]
ARRIVAL += [(-4, 0), (4, 1)]


def dot(a, b, dims):
    return lax.dot_general(a, b, dims, preferred_element_type=F32)


def perm(move):
    pairs = []
    for x in range(2):
        for z in range(8):
            for c in range(2):
                x2, z2, c2 = move(x, z, c)
                pairs.append(((x * 8 + z) * 2 + c, (x2 * 8 + z2 % 8) * 2 + c2))
    return pairs


CORE = perm(lambda x, z, c: (x, z, 1 - c))
XX = perm(lambda x, z, c: (1 - x, z, c))
UP = perm(lambda x, z, c: (x, z + 1, c))
DOWN = perm(lambda x, z, c: (x, z - 1, c))


def send(array, pairs):
    return lax.ppermute(array, "blk", pairs)


def place():
    me = lax.axis_index("blk")
    return me // 16, (me // 2) % 8, me % 2


def eye():
    return lax.broadcasted_iota(jnp.int32, (N, N), 0) == lax.broadcasted_iota(
        jnp.int32, (N, N), 1
    )


def to_column(row, diag):
    return jnp.sum(jnp.where(diag, row, 0.0), axis=1, keepdims=True)


def merge(a, b):
    top = jnp.maximum(a, b)
    return top + jnp.log2(jnp.exp2(a - top) + jnp.exp2(b - top))


def onehot(match_ref):
    return lax.broadcasted_iota(jnp.int32, (N, N), 0) == match_ref[...]


def pack_kernel(count_ref, m1_ref, m2_ref, f1_ref, f2_ref, x_ref, y_ref):
    first = place()[2] == 0
    valid = (lax.broadcasted_iota(jnp.int32, (16, N), 1) < count_ref[0]).astype(F32).astype(BF)

    def write(m_ref, f_ref, o_ref):
        pick = onehot(m_ref).astype(F32).astype(BF)
        o_ref[:N, :] = f_ref[...]
        o_ref[N:, :] = dot(valid, pick, NT).astype(BF)

    @pl.when(first)
    def _():
        write(m1_ref, f1_ref, x_ref)
        write(m2_ref, f2_ref, y_ref)

    @pl.when(jnp.logical_not(first))
    def _():
        write(m2_ref, f2_ref, x_ref)
        write(m1_ref, f1_ref, y_ref)


def pair_kernel(count_ref, m1_ref, m2_ref, f1_ref, f2_ref, pk_ref, pq_ref):
    valid = lax.broadcasted_iota(jnp.int32, (N, N), 1) < count_ref[0]
    one = onehot(m1_ref)
    two = onehot(m2_ref)
    one_valid = (one & valid).astype(F32).astype(BF)
    two_valid = (two & valid).astype(F32).astype(BF)
    to_one = dot(one_valid, two.astype(F32).astype(BF), NT).astype(BF)
    to_two = dot(two_valid, one.astype(F32).astype(BF), NT).astype(BF)
    pk_ref[...] = dot(to_one, f2_ref[...], NN)
    pq_ref[...] = dot(to_two, f1_ref[...], NN)


def stats_kernel(first, last, *refs):
    x_refs, refs = refs[:4], refs[4:]
    if not first:
        carry_ref, refs = refs[0], refs[1:]
    y_refs, o_ref, x_all = refs[:-2], refs[-2], refs[-1]
    for i, ref in enumerate(x_refs):
        x_all[i * N : (i + 1) * N, :] = ref[:N, :]
    diag = eye()
    width = 4 * N
    if first:
        top = jnp.full((1, width), NEG, F32)
        total = jnp.zeros((1, width), F32)
        count = jnp.zeros((1, 1), F32)
    else:
        top = carry_ref[0:1, :]
        total = carry_ref[1:2, :]
        count = carry_ref[2:3, :1]
    for ref in y_refs:
        mask = ref[N:, :].astype(F32)[:1, :]
        count = count + jnp.sum(mask, axis=1, keepdims=True)
        bias = (1.0 - to_column(mask, diag)) * NEG
        t = dot(ref[:N, :], x_all[...], NT) * SCALE2 + bias
        new = jnp.maximum(top, jnp.max(t, axis=0, keepdims=True))
        total = total * jnp.exp2(top - new) + jnp.sum(jnp.exp2(t - new), axis=0, keepdims=True)
        top = new
    if last:
        o_ref[:, :width] = top + jnp.log2(total)
        o_ref[:, width:] = jnp.broadcast_to(count, (1, 128))
    else:
        o_ref[0:1, :] = top
        o_ref[1:2, :] = total
        o_ref[2:3, :] = jnp.broadcast_to(count, (1, width))


def grad_kernel(pair, *refs):
    recv, x_refs, y_refs, refs = refs[0], refs[1:3], refs[3:19], refs[19:]
    d_ref, refs = refs[0], refs[1:]
    if pair == 0:
        lse_ref, refs = refs[0], refs[1:]
    y_all, bias, col = refs
    x, z, c = place()

    def source(x1, z1, c1):
        return recv[(x1 * 8 + z1) * 2 + c1]

    for j, (ref, (offset, chain)) in enumerate(zip(y_refs, ARRIVAL)):
        block = slice(j * N, (j + 1) * N)
        y_all[block, :] = ref[:N, :]
        bias[:, block] = (1.0 - ref[N:, :].astype(F32)[:1, :]) * NEG
        z1 = lax.rem(z + offset + 8, 8)
        near = 1 - chain
        col[:, block] = merge(
            source(x, z1, 1 - c)[:, near * N : (near + 1) * N],
            source(1 - x, z1, 1 - c)[:, (near + 2) * N : (near + 3) * N],
        )
    mine = source(x, z, c)
    theirs = source(1 - x, z, c)
    diag = eye()
    for i in range(2):
        at = 2 * pair + i
        other = (at + 2) % 4
        row = merge(mine[:, at * N : (at + 1) * N], theirs[:, other * N : (other + 1) * N])
        if pair == 0 and i == 0:
            total = mine[:, 4 * N :][:, :1] + theirs[:, 4 * N :][:, :1]
            lse_ref[...] = jnp.concatenate(
                [row, col[:, :N], jnp.broadcast_to(total, (1, N)), jnp.zeros((5, N), F32)], axis=0
            )
        row = to_column(row, diag)
        xb = x_refs[i][:N, :]

        def step(j, acc):
            block = pl.ds(pl.multiple_of(j * 1024, 1024), 1024)
            y = y_all[block, :]
            t = dot(xb, y, NT) * SCALE2 + bias[:, block]
            w = (jnp.exp2(t - row) + jnp.exp2(t - col[:, block])).astype(BF)
            return acc + dot(w, y, NN)

        acc = lax.fori_loop(0, 4, step, jnp.zeros((N, N), F32))
        d_ref[i * N : (i + 1) * N, :] = acc.astype(d_ref.dtype)


def sum_kernel(own_ref, other_ref, b_ref):
    b_ref[...] = own_ref[N:, :] + other_ref[N:, :].astype(F32)


def final_kernel(count_ref, m1_ref, m2_ref, lse_ref, pk_ref, pq_ref, own_ref, other_ref, b_ref, *outs):
    g1, g2, rl, cl = outs
    coef = (2.0 / math.sqrt(N)) / (2.0 * lse_ref[2:3, :1])
    near = own_ref[:N, :] + other_ref[:N, :].astype(F32)
    far = b_ref[...]
    valid = lax.broadcasted_iota(jnp.int32, (N, N), 1) < count_ref[0]
    diag = eye()

    def write(m_ref, acc, pair_ref, at, g_ref, l_ref):
        pick = onehot(m_ref)
        live = jnp.sum(jnp.where(pick & valid, 1.0, 0.0), axis=1, keepdims=True) > 0.0
        g_ref[...] = coef * (jnp.where(live, acc, 0.0) - 2.0 * pair_ref[...])
        column = to_column(lse_ref[at : at + 1, :], diag)
        l_ref[...] = jnp.sum(jnp.where(pick, column, 0.0), axis=0, keepdims=True) * LN2

    first = place()[2] == 0

    @pl.when(first)
    def _():
        write(m1_ref, near, pk_ref, 0, g1, rl)
        write(m2_ref, far, pq_ref, 1, g2, cl)

    @pl.when(jnp.logical_not(first))
    def _():
        write(m1_ref, far, pk_ref, 1, g1, rl)
        write(m2_ref, near, pq_ref, 0, g2, cl)


def vmem(n):
    return [pl.BlockSpec(memory_space=pltpu.VMEM)] * n


def call(kernel, ins, outs, scratch=(), smem=0, flops=0, trans=0, limit=32):
    return pl.pallas_call(
        kernel,
        out_shape=[jax.ShapeDtypeStruct(s, d) for s, d in outs],
        in_specs=[pl.BlockSpec(memory_space=pltpu.SMEM)] * smem + vmem(len(ins) - smem),
        out_specs=vmem(len(outs)),
        scratch_shapes=list(scratch),
        compiler_params=pltpu.CompilerParams(vmem_limit_bytes=limit * 2**20),
        cost_estimate=pl.CostEstimate(flops=flops, bytes_accessed=2**20, transcendentals=trans),
    )(*ins)


def stats(first, last, xs, ys, carry):
    def kernel(*refs):
        stats_kernel(first, last, *refs)

    shape = (1, 1152) if last else (8, 4 * N)
    ins = list(xs) + ([] if first else [carry]) + list(ys)
    work = len(ys) * 4 * N**3
    (out,) = call(
        kernel, ins, [(shape, F32)], [pltpu.VMEM((4 * N, N), BF)], flops=2 * work, trans=work // N
    )
    return out


def grads(pair, recv, xs, ys):
    def kernel(*refs):
        grad_kernel(pair, *refs)

    outs = [((2 * N, N), F32), ((8, N), F32)] if pair == 0 else [((2 * N, N), BF)]
    scratch = [
        pltpu.VMEM((16 * N, N), BF),
        pltpu.VMEM((1, 16 * N), F32),
        pltpu.VMEM((1, 16 * N), F32),
    ]
    work = 32 * N**3
    return call(
        kernel, [recv] + list(xs) + list(ys), outs, scratch, flops=4 * work, trans=2 * work // N
    )


def local(feat_one, feat_two, match_one, match_two, valid_counts):
    ins = (valid_counts, match_one, match_two, feat_one, feat_two)
    xa, ya = call(pack_kernel, ins, [((PACK, N), BF)] * 2, smem=1)
    yb = send(xa, CORE)
    xb = send(ya, CORE)
    xs = [xa, xb, send(xa, XX), send(xb, XX)]
    ups, downs = [[ya, yb]], [[ya, yb]]
    for hop in range(3):
        ups.append([send(a, UP) for a in ups[-1]])
        downs.append([send(a, DOWN) for a in downs[-1]])
    groups = [[ya, yb]]
    for hop in (1, 2, 3):
        groups.append([ups[hop][0], downs[hop][0], ups[hop][1], downs[hop][1]])
    groups.append([send(ups[3][0], UP), send(downs[3][1], DOWN)])
    carry = None
    for i, ys in enumerate(groups):
        carry = stats(i == 0, i == 4, xs, ys, carry)
    recv = lax.all_to_all(jnp.broadcast_to(carry[None], (32, 1, 1152)), "blk", 0, 0)
    ys = [y for group in groups for y in group]
    (away,) = grads(1, recv, xs[2:], ys)
    away = send(away, XX)
    own, lse = grads(0, recv, xs[:2], ys)
    (b,) = call(sum_kernel, (own, away), [((N, N), F32)])
    b = send(b, CORE)
    pk, pq = call(pair_kernel, ins, [((N, N), F32)] * 2, smem=1)
    grad_one, grad_two, row_lse, col_lse = call(
        final_kernel,
        [valid_counts, match_one, match_two, lse, pk, pq, own, away, b],
        [((N, N), F32)] * 2 + [((1, N), F32)] * 2,
        smem=1,
    )
    return grad_one, grad_two, row_lse.reshape(N), col_lse.reshape(N)


def solution(mesh):
    both = ("grp", "blk")
    return jax.shard_map(
        local,
        mesh=mesh,
        in_specs=(P(both, None),) * 4 + (P(both),),
        out_specs=(P(both, None), P(both, None), P(both), P(both)),
        check_vma=False,
    )
```

time: 90.7 us -> 75.9 us (0.84); the launches traced: 89.4 us -> 75.7 us
  waiting for transfers between devices: 24.2 us -> 4.85 us
  blocking collectives: 0 us -> 18.3 us
  starting transfers between devices: 42.3 us -> 30.2 us
    ppermute x24 -> x20, waiting for transfers between devices: 24.2 us -> 4.85 us  [send(): return lax.ppermute(array, 'blk', pairs)]
    all_to_all x0 -> x1, blocking collectives: none -> 18.3 us  [local(): lax.all_to_all(jnp.broadcast_to(carry[None], (32, 1, 1152)), 'blk', 0, 0)]
    ppermute x24 -> x20, starting transfers between devices: 42.3 us -> 30.2 us  [send(): return lax.ppermute(array, 'blk', pairs)]
    pallas_call x7 -> x11, Pallas kernels: 19 us -> 18.3 us  [call(): pl.pallas_call(kernel, out_shape=[jax.ShapeDtypeStruct(s, d) for s, d in...]
  transfers between devices with their start and end apart: 24 -> 20, of which waited for: 11 -> 3; matrix products, arithmetic and copies ran while one was open for 0% -> 0% of each run, Pallas kernels for 1% -> 14%
where the time goes in v2:
time: 75.9 us; the launch traced here: 75.7 us
  starting transfers between devices  30.2 us (40%)
  Pallas kernels  18.3 us (24%)
  blocking collectives  18.3 us (24%)
  waiting for transfers between devices  4.85 us (6%)
  local copies, waits for them, and re-layouts  2.58 us (3%)
  between operations  1.42 us (2%)
    ppermute x20, starting transfers between devices, send(): return lax.ppermute(array, 'blk', pairs)  30.2 us
    all_to_all x1, blocking collectives, local(): lax.all_to_all(jnp.broadcast_to(carry[None], (32, 1, 1152)), 'blk', 0, 0)  18.3 us
    pallas_call x11, Pallas kernels, call(): pl.pallas_call(kernel, out_shape=[jax.ShapeDtypeStruct(s, d) for s, d in...  18.3 us
    ppermute x20, waiting for transfers between devices, send(): return lax.ppermute(array, 'blk', pairs)  4.85 us
    unnamed x14, local copies, waits for them, and re-layouts  2.5 us
  transfers between devices with their start and end apart: 20, of which 3 were waited for; matrix products, arithmetic and copies ran while one was open for 0% of the time, Pallas kernels for 14%

profile of v2, /device:TPU:1, one launch (start us, length us, event | category | flops | bytes accessed | tf_op | source)
XLA Modules:
  0.0 75.7 jit_solution(8552921276699779384)
XLA Ops:
  0.6 0.0 copy-start.4
  1.3 0.0 copy-done.4
  1.3 0.0 copy-start
  1.3 0.9 %copy-done = bf16[256,256]{1,0:T(8,128)(2,1)S(1)} copy-done((bf16[256,256]{1,0:T(8,128)(2,1)S(1)}, bf16[256,256]{1,0:T(8,128)(2,1)}, u32[]{:S(2)}) %copy-start) | copy-done | bytes 131096
  2.2 0.0 copy-start.2
  2.2 0.9 %copy-done.2 = bf16[256,256]{1,0:T(8,128)(2,1)S(1)} copy-done((bf16[256,256]{1,0:T(8,128)(2,1)S(1)}, bf16[256,256]{1,0:T(8,128)(2,1)}, u32[]{:S(2)}) %copy-start.2) | copy-done | bytes 131096
  3.1 0.0 copy-start.5
  3.1 0.7 copy-done.5
  3.8 0.2 shard_map.84
  4.0 3.3 %collective-permute-start.3 = (bf16[272,256]{1,0:T(8,128)(2,1)S(1)}, bf16[272,256]{1,0:T(8,128)(2,1)S(1)}, u32[]{:S(2)}, u32[]{:S(2)}) collective-permute-start(bf16[272,256]{1,0:T(8,128)(2,1)S(1)} %get-tuple-element.14.refs_0_.refs_1_), channel_id=1, source_target_pairs={{0,1},{1,0},{2,3},{3,2},{4,5},{5,4},{6,7},{7,6},{8,9},{9,8},{10,11... | collective-permute-start | bytes 417800 | tf_op jit(solution)/shard_map/ppermute | solution.py:46
  7.3 3.8 %collective-permute-start.5 = (bf16[272,256]{1,0:T(8,128)(2,1)S(1)}, bf16[272,256]{1,0:T(8,128)(2,1)S(1)}, u32[]{:S(2)}, u32[]{:S(2)}) collective-permute-start(bf16[272,256]{1,0:T(8,128)(2,1)S(1)} %get-tuple-element.15.refs_4_.refs_3_), channel_id=1, source_target_pairs={{0,14},{1,15},{2,0},{3,1},{4,2},{5,3},{6,4},{7,5},{8,6},{9,7},{10,... | collective-permute-start | bytes 417800 | tf_op jit(solution)/shard_map/ppermute | solution.py:46
  11.1 0.0 collective-permute-start.4
  11.1 0.0 collective-permute-done.3.refs_5_.refs_4_
  11.1 2.7 %collective-permute-start.7 = (bf16[272,256]{1,0:T(8,128)(2,1)S(1)}, bf16[272,256]{1,0:T(8,128)(2,1)S(1)}, u32[]{:S(2)}, u32[]{:S(2)}) collective-permute-start(bf16[272,256]{1,0:T(8,128)(2,1)S(1)} %collective-permute-done.3.refs_5_.refs_4_), channel_id=1, source_target_pairs={{0,14},{1,15},{2,0},{3,1},{4,2},{5,3},{6,4},{7,5},{8,6},{9,7},{10,... | collective-permute-start | bytes 417800 | tf_op jit(solution)/shard_map/ppermute | solution.py:46
  13.8 0.9 %collective-permute-start = (bf16[272,256]{1,0:T(8,128)(2,1)S(1)}, bf16[272,256]{1,0:T(8,128)(2,1)S(1)}, u32[]{:S(2)}, u32[]{:S(2)}) collective-permute-start(bf16[272,256]{1,0:T(8,128)(2,1)S(1)} %get-tuple-element.15.refs_4_.refs_3_), channel_id=1, source_target_pairs={{0,1},{1,0},{2,3},{3,2},{4,5},{5,4},{6,7},{7,6},{8,9},{9,8},{10,11... | collective-permute-start | bytes 417800 | tf_op jit(solution)/shard_map/ppermute | solution.py:46
  14.7 0.0 collective-permute-start.6
  14.7 0.0 collective-permute-done.5.refs_6_
  14.7 2.7 %collective-permute-start.1 = (bf16[272,256]{1,0:T(8,128)(2,1)S(1)}, bf16[272,256]{1,0:T(8,128)(2,1)S(1)}, u32[]{:S(2)}, u32[]{:S(2)}) collective-permute-start(bf16[272,256]{1,0:T(8,128)(2,1)S(1)} %get-tuple-element.14.refs_0_.refs_1_), channel_id=1, source_target_pairs={{0,16},{1,17},{2,18},{3,19},{4,20},{5,21},{6,22},{7,23},{8,24},{9,... | collective-permute-start | bytes 417800 | tf_op jit(solution)/shard_map/ppermute | solution.py:46
  17.4 0.0 collective-permute-done.4.refs_5_
  17.4 0.0 collective-permute-start.8
  17.5 0.0 collective-permute-done.7.refs_8_
  17.5 2.9 %collective-permute-start.11 = (bf16[272,256]{1,0:T(8,128)(2,1)S(1)}, bf16[272,256]{1,0:T(8,128)(2,1)S(1)}, u32[]{:S(2)}, u32[]{:S(2)}) collective-permute-start(bf16[272,256]{1,0:T(8,128)(2,1)S(1)} %collective-permute-done.7.refs_8_), channel_id=1, source_target_pairs={{0,14},{1,15},{2,0},{3,1},{4,2},{5,3},{6,4},{7,5},{8,6},{9,7},{10,... | collective-permute-start | bytes 417800 | tf_op jit(solution)/shard_map/ppermute | solution.py:46
  20.4 0.0 collective-permute-done.refs_1_.refs_2_
  20.4 1.4 %collective-permute-start.9 = (bf16[272,256]{1,0:T(8,128)(2,1)S(1)}, bf16[272,256]{1,0:T(8,128)(2,1)S(1)}, u32[]{:S(2)}, u32[]{:S(2)}) collective-permute-start(bf16[272,256]{1,0:T(8,128)(2,1)S(1)} %collective-permute-done.5.refs_6_), channel_id=1, source_target_pairs={{0,14},{1,15},{2,0},{3,1},{4,2},{5,3},{6,4},{7,5},{8,6},{9,7},{10,... | collective-permute-start | bytes 417800 | tf_op jit(solution)/shard_map/ppermute | solution.py:46
  21.8 0.0 collective-permute-done.6.refs_7_
  21.8 0.1 collective-permute-start.10
  21.9 0.0 collective-permute-done.1.refs_2_.refs_1_
  21.9 2.6 %collective-permute-start.2 = (bf16[272,256]{1,0:T(8,128)(2,1)S(1)}, bf16[272,256]{1,0:T(8,128)(2,1)S(1)}, u32[]{:S(2)}, u32[]{:S(2)}) collective-permute-start(bf16[272,256]{1,0:T(8,128)(2,1)S(1)} %collective-permute-done.refs_1_.refs_2_), channel_id=1, source_target_pairs={{0,16},{1,17},{2,18},{3,19},{4,20},{5,21},{6,22},{7,23},{8,24},{9,... | collective-permute-start | bytes 417800 | tf_op jit(solution)/shard_map/ppermute | solution.py:46
  24.4 0.0 collective-permute-done.8.refs_5_.refs_9_
  24.4 0.1 collective-permute-start.12
  24.5 0.0 collective-permute-done.11.refs_8_.refs_12_
  24.5 2.6 %collective-permute-start.15 = (bf16[272,256]{1,0:T(8,128)(2,1)S(1)}, bf16[272,256]{1,0:T(8,128)(2,1)S(1)}, u32[]{:S(2)}, u32[]{:S(2)}) collective-permute-start(bf16[272,256]{1,0:T(8,128)(2,1)S(1)} %collective-permute-done.11.refs_8_.refs_12_), channel_id=1, source_target_pairs={{0,14},{1,15},{2,0},{3,1},{4,2},{5,3},{6,4},{7,5},{8,6},{9,7},{10,... | collective-permute-start | bytes 417800 | tf_op jit(solution)/shard_map/ppermute | solution.py:46
  27.1 0.0 collective-permute-done.9.refs_6_.refs_10_
  27.1 1.3 %collective-permute-start.13 = (bf16[272,256]{1,0:T(8,128)(2,1)S(1)}, bf16[272,256]{1,0:T(8,128)(2,1)S(1)}, u32[]{:S(2)}, u32[]{:S(2)}) collective-permute-start(bf16[272,256]{1,0:T(8,128)(2,1)S(1)} %collective-permute-done.9.refs_6_.refs_10_), channel_id=1, source_target_pairs={{0,14},{1,15},{2,0},{3,1},{4,2},{5,3},{6,4},{7,5},{8,6},{9,7},{10,... | collective-permute-start | bytes 417800 | tf_op jit(solution)/shard_map/ppermute | solution.py:46
  28.4 0.0 collective-permute-done.10.refs_7_.refs_11_
  28.4 0.2 collective-permute-start.14
  28.6 0.0 collective-permute-done.2.refs_3_.refs_2_
  28.6 0.8 %shard_map.85.refs_4_ = f32[8,1024]{1,0:T(8,128)S(1)} custom-call(bf16[272,256]{1,0:T(8,128)(2,1)S(1)} %get-tuple-element.14.refs_0_.refs_1_, bf16[272,256]{1,0:T(8,128)(2,1)S(1)} %collective-permute-done.refs_1_.refs_2_, bf16[272,256]{1,0:T(8,128)(2,1)S(1)} %collective-permute-done.1.refs_2_.refs_1_, ...), custom_call_target="tpu_custom_call" | custom-call | flops 268435456 | bytes 1048576 | tf_op jit(solution)/shard_map/pallas_call | solution.py:223
  29.4 1.9 %collective-permute-done.12.refs_5_.refs_13_ = bf16[272,256]{1,0:T(8,128)(2,1)S(1)} collective-permute-done((bf16[272,256]{1,0:T(8,128)(2,1)S(1)}, bf16[272,256]{1,0:T(8,128)(2,1)S(1)}, u32[]{:S(2)}, u32[]{:S(2)}) %collective-permute-start.12) | collective-permute-done | bytes 139296 | tf_op jit(solution)/shard_map/ppermute | solution.py:46
  31.3 0.0 collective-permute-start.16
  31.3 0.0 collective-permute-done.15.refs_8_.refs_16_
  31.3 2.7 %collective-permute-start.17 = (bf16[272,256]{1,0:T(8,128)(2,1)S(1)}, bf16[272,256]{1,0:T(8,128)(2,1)S(1)}, u32[]{:S(2)}, u32[]{:S(2)}) collective-permute-start(bf16[272,256]{1,0:T(8,128)(2,1)S(1)} %collective-permute-done.15.refs_8_.refs_16_), channel_id=1, source_target_pairs={{0,14},{1,15},{2,0},{3,1},{4,2},{5,3},{6,4},{7,5},{8,6},{9,7},{10,... | collective-permute-start | bytes 417800 | tf_op jit(solution)/shard_map/ppermute | solution.py:46
  34.0 1.5 %shard_map.86.refs_4_ = f32[8,1024]{1,0:T(8,128)S(1)} custom-call(bf16[272,256]{1,0:T(8,128)(2,1)S(1)} %get-tuple-element.14.refs_0_.refs_1_, bf16[272,256]{1,0:T(8,128)(2,1)S(1)} %collective-permute-done.refs_1_.refs_2_, bf16[272,256]{1,0:T(8,128)(2,1)S(1)} %collective-permute-done.1.refs_2_.refs_1_, ...), custom_call_target="tpu_custom_call" | custom-call | flops 536870912 | bytes 1048576 | tf_op jit(solution)/shard_map/pallas_call | solution.py:223
  35.5 1.5 %shard_map.87.refs_4_ = f32[8,1024]{1,0:T(8,128)S(1)} custom-call(bf16[272,256]{1,0:T(8,128)(2,1)S(1)} %get-tuple-element.14.refs_0_.refs_1_, bf16[272,256]{1,0:T(8,128)(2,1)S(1)} %collective-permute-done.refs_1_.refs_2_, bf16[272,256]{1,0:T(8,128)(2,1)S(1)} %collective-permute-done.1.refs_2_.refs_1_, ...), custom_call_target="tpu_custom_call" | custom-call | flops 536870912 | bytes 1048576 | tf_op jit(solution)/shard_map/pallas_call | solution.py:223
  37.0 0.0 collective-permute-done.13.refs_6_.refs_14_
  37.0 0.0 collective-permute-done.14.refs_7_.refs_15_
  37.0 1.5 %shard_map.88.refs_4_ = f32[8,1024]{1,0:T(8,128)S(1)} custom-call(bf16[272,256]{1,0:T(8,128)(2,1)S(1)} %get-tuple-element.14.refs_0_.refs_1_, bf16[272,256]{1,0:T(8,128)(2,1)S(1)} %collective-permute-done.refs_1_.refs_2_, bf16[272,256]{1,0:T(8,128)(2,1)S(1)} %collective-permute-done.1.refs_2_.refs_1_, ...), custom_call_target="tpu_custom_call" | custom-call | flops 536870912 | bytes 1048576 | tf_op jit(solution)/shard_map/pallas_call | solution.py:223
  38.5 0.0 collective-permute-done.16.refs_5_.refs_17_
  38.5 0.0 collective-permute-done.17.refs_6_.refs_18_
  38.5 0.8 %shard_map.89 = f32[1,1152]{1,0:T(1,128)S(1)} custom-call(bf16[272,256]{1,0:T(8,128)(2,1)S(1)} %get-tuple-element.14.refs_0_.refs_1_, bf16[272,256]{1,0:T(8,128)(2,1)S(1)} %collective-permute-done.refs_1_.refs_2_, bf16[272,256]{1,0:T(8,128)(2,1)S(1)} %collective-permute-done.1.refs_2_.refs_1_, bf16[272,256]{1,0:T(8,128)(2,1)S(1)} %collective-permute-done.2.refs_3_.refs_2_, ...), custom_call_target="tpu_custom_call" | custom-call | flops 268435456 | bytes 1048576 | tf_op jit(solution)/shard_map/pallas_call | solution.py:223
  39.3 0.1 broadcast_in_dim.9
  39.4 18.3 %all_to_all.5.refs_0_ = f32[32,1,1152]{2,1,0:T(1,128)S(1)} all-to-all(f32[32,1,1152]{2,1,0:T(1,128)S(1)} %broadcast_in_dim.9), channel_id=1, replica_groups=mesh['grp'=8,'blk'=32] {'blk'}, dimensions={0} | all-to-all | bytes 294912 | tf_op jit(solution)/shard_map/all_to_all | solution.py:280
  57.7 5.2 %shard_map.92 = bf16[512,256]{1,0:T(8,128)(2,1)S(1)} custom-call(f32[32,1,1152]{2,1,0:T(1,128)S(1)} %all_to_all.5.refs_0_, bf16[272,256]{1,0:T(8,128)(2,1)S(1)} %collective-permute-done.1.refs_2_.refs_1_, bf16[272,256]{1,0:T(8,128)(2,1)S(1)} %collective-permute-done.2.refs_3_.refs_2_, bf16[272,256]{1,0:T(8,128)(2,1)S(1)} %get-tuple-element.15.refs_4_.refs_3_, ...), custom_call_target="tpu_custom_call" | custom-call | flops 2147483648 | bytes 1048576 | tf_op jit(solution)/shard_map/pallas_call | solution.py:223
  63.0 0.3 collective-permute-start.18
  63.2 5.2 %shard_map.90 = (f32[512,256]{1,0:T(8,128)S(1)}, f32[8,256]{1,0:T(8,128)S(1)}) custom-call(f32[32,1,1152]{2,1,0:T(1,128)S(1)} %all_to_all.5.refs_0_, bf16[272,256]{1,0:T(8,128)(2,1)S(1)} %get-tuple-element.14.refs_0_.refs_1_, bf16[272,256]{1,0:T(8,128)(2,1)S(1)} %collective-permute-done.refs_1_.refs_2_, ...), custom_call_target="tpu_custom_call" | custom-call | flops 2147483648 | bytes 1048576 | tf_op jit(solution)/shard_map/pallas_call | solution.py:223
  68.5 2.1 %collective-permute-done.18.other_ref = bf16[512,256]{1,0:T(8,128)(2,1)S(1)} collective-permute-done((bf16[512,256]{1,0:T(8,128)(2,1)S(1)}, bf16[512,256]{1,0:T(8,128)(2,1)S(1)}, u32[]{:S(2)}, u32[]{:S(2)}) %collective-permute-start.18) | collective-permute-done | bytes 262176 | tf_op jit(solution)/shard_map/ppermute | solution.py:46
  70.6 0.0 copy-start.1
  70.7 2.7 %collective-permute-start.19 = (f32[256,256]{1,0:T(8,128)S(1)}, f32[256,256]{1,0:T(8,128)S(1)}, u32[]{:S(2)}, u32[]{:S(2)}) collective-permute-start(f32[256,256]{1,0:T(8,128)S(1)} %shard_map.93), channel_id=1, source_target_pairs={{0,1},{1,0},{2,3},{3,2},{4,5},{5,4},{6,7},{7,6},{8,9},{9,8},{10,11... | collective-permute-start | bytes 786440 | tf_op jit(solution)/shard_map/ppermute | solution.py:46
  73.4 0.0 copy-done.1
  73.4 0.0 copy-done.3
  73.4 0.0 copy-done.6
  73.4 0.4 shard_map.91
  73.8 0.7 collective-permute-done.19.b_ref
  74.6 1.2 %shard_map.94 = (f32[256,256]{1,0:T(8,128)}, f32[256,256]{1,0:T(8,128)}, f32[1,256]{1,0:T(1,128)}, f32[1,256]{1,0:T(1,128)}) custom-call(s32[1]{0:T(128)S(6)} %copy.9.count_ref, s32[1,256]{1,0:T(1,128)S(1)} %copy-done.4, s32[1,256]{1,0:T(1,128)S(1)} %copy-done.6, f32[8,256]{1,0:T(8,128)S(1)} %get-tuple-element.16.lse_ref, ...), custom_call_target="tpu_custom_call" | custom-call | bytes 1048576 | tf_op jit(solution)/shard_map/pallas_call | solution.py:223
  (4 shorter events, 0.1 us)
Async XLA Ops:
  0.6 0.7 copy-start.4
  1.3 0.9 %copy-start = (bf16[256,256]{1,0:T(8,128)(2,1)S(1)}, bf16[256,256]{1,0:T(8,128)(2,1)}, u32[]{:S(2)}) copy-start(bf16[256,256]{1,0:T(8,128)(2,1)} %f1_ref.3) | copy-start | bytes 393220
  2.2 0.9 %copy-start.2 = (bf16[256,256]{1,0:T(8,128)(2,1)S(1)}, bf16[256,256]{1,0:T(8,128)(2,1)}, u32[]{:S(2)}) copy-start(bf16[256,256]{1,0:T(8,128)(2,1)} %f2_ref.3) | copy-start | bytes 393220
  3.1 0.7 copy-start.5
  4.0 7.1 %collective-permute-start.3 = (bf16[272,256]{1,0:T(8,128)(2,1)S(1)}, bf16[272,256]{1,0:T(8,128)(2,1)S(1)}, u32[]{:S(2)}, u32[]{:S(2)}) collective-permute-start(bf16[272,256]{1,0:T(8,128)(2,1)S(1)} %get-tuple-element.14.refs_0_.refs_1_), channel_id=1, source_target_pairs={{0,1},{1,0},{2,3},{3,2},{4,5},{5,4},{6,7},{7,6},{8,9},{9,8},{10,11... | collective-permute-start | bytes 417800 | tf_op jit(solution)/shard_map/ppermute | solution.py:46
  7.3 7.4 %collective-permute-start.5 = (bf16[272,256]{1,0:T(8,128)(2,1)S(1)}, bf16[272,256]{1,0:T(8,128)(2,1)S(1)}, u32[]{:S(2)}, u32[]{:S(2)}) collective-permute-start(bf16[272,256]{1,0:T(8,128)(2,1)S(1)} %get-tuple-element.15.refs_4_.refs_3_), channel_id=1, source_target_pairs={{0,14},{1,15},{2,0},{3,1},{4,2},{5,3},{6,4},{7,5},{8,6},{9,7},{10,... | collective-permute-start | bytes 417800 | tf_op jit(solution)/shard_map/ppermute | solution.py:46
  11.1 6.3 %collective-permute-start.4 = (bf16[272,256]{1,0:T(8,128)(2,1)S(1)}, bf16[272,256]{1,0:T(8,128)(2,1)S(1)}, u32[]{:S(2)}, u32[]{:S(2)}) collective-permute-start(bf16[272,256]{1,0:T(8,128)(2,1)S(1)} %get-tuple-element.15.refs_4_.refs_3_), channel_id=1, source_target_pairs={{0,2},{1,3},{2,4},{3,5},{4,6},{5,7},{6,8},{7,9},{8,10},{9,11},{10,... | collective-permute-start | bytes 417800 | tf_op jit(solution)/shard_map/ppermute | solution.py:46
  11.1 6.3 %collective-permute-start.7 = (bf16[272,256]{1,0:T(8,128)(2,1)S(1)}, bf16[272,256]{1,0:T(8,128)(2,1)S(1)}, u32[]{:S(2)}, u32[]{:S(2)}) collective-permute-start(bf16[272,256]{1,0:T(8,128)(2,1)S(1)} %collective-permute-done.3.refs_5_.refs_4_), channel_id=1, source_target_pairs={{0,14},{1,15},{2,0},{3,1},{4,2},{5,3},{6,4},{7,5},{8,6},{9,7},{10,... | collective-permute-start | bytes 417800 | tf_op jit(solution)/shard_map/ppermute | solution.py:46
  13.8 6.6 %collective-permute-start = (bf16[272,256]{1,0:T(8,128)(2,1)S(1)}, bf16[272,256]{1,0:T(8,128)(2,1)S(1)}, u32[]{:S(2)}, u32[]{:S(2)}) collective-permute-start(bf16[272,256]{1,0:T(8,128)(2,1)S(1)} %get-tuple-element.15.refs_4_.refs_3_), channel_id=1, source_target_pairs={{0,1},{1,0},{2,3},{3,2},{4,5},{5,4},{6,7},{7,6},{8,9},{9,8},{10,11... | collective-permute-start | bytes 417800 | tf_op jit(solution)/shard_map/ppermute | solution.py:46
  14.7 7.1 %collective-permute-start.6 = (bf16[272,256]{1,0:T(8,128)(2,1)S(1)}, bf16[272,256]{1,0:T(8,128)(2,1)S(1)}, u32[]{:S(2)}, u32[]{:S(2)}) collective-permute-start(bf16[272,256]{1,0:T(8,128)(2,1)S(1)} %collective-permute-done.3.refs_5_.refs_4_), channel_id=1, source_target_pairs={{0,2},{1,3},{2,4},{3,5},{4,6},{5,7},{6,8},{7,9},{8,10},{9,11},{10,... | collective-permute-start | bytes 417800 | tf_op jit(solution)/shard_map/ppermute | solution.py:46
  14.7 7.2 %collective-permute-start.1 = (bf16[272,256]{1,0:T(8,128)(2,1)S(1)}, bf16[272,256]{1,0:T(8,128)(2,1)S(1)}, u32[]{:S(2)}, u32[]{:S(2)}) collective-permute-start(bf16[272,256]{1,0:T(8,128)(2,1)S(1)} %get-tuple-element.14.refs_0_.refs_1_), channel_id=1, source_target_pairs={{0,16},{1,17},{2,18},{3,19},{4,20},{5,21},{6,22},{7,23},{8,24},{9,... | collective-permute-start | bytes 417800 | tf_op jit(solution)/shard_map/ppermute | solution.py:46
  17.4 7.0 %collective-permute-start.8 = (bf16[272,256]{1,0:T(8,128)(2,1)S(1)}, bf16[272,256]{1,0:T(8,128)(2,1)S(1)}, u32[]{:S(2)}, u32[]{:S(2)}) collective-permute-start(bf16[272,256]{1,0:T(8,128)(2,1)S(1)} %collective-permute-done.4.refs_5_), channel_id=1, source_target_pairs={{0,2},{1,3},{2,4},{3,5},{4,6},{5,7},{6,8},{7,9},{8,10},{9,11},{10,... | collective-permute-start | bytes 417800 | tf_op jit(solution)/shard_map/ppermute | solution.py:46
  17.5 7.1 %collective-permute-start.11 = (bf16[272,256]{1,0:T(8,128)(2,1)S(1)}, bf16[272,256]{1,0:T(8,128)(2,1)S(1)}, u32[]{:S(2)}, u32[]{:S(2)}) collective-permute-start(bf16[272,256]{1,0:T(8,128)(2,1)S(1)} %collective-permute-done.7.refs_8_), channel_id=1, source_target_pairs={{0,14},{1,15},{2,0},{3,1},{4,2},{5,3},{6,4},{7,5},{8,6},{9,7},{10,... | collective-permute-start | bytes 417800 | tf_op jit(solution)/shard_map/ppermute | solution.py:46
  20.4 6.7 %collective-permute-start.9 = (bf16[272,256]{1,0:T(8,128)(2,1)S(1)}, bf16[272,256]{1,0:T(8,128)(2,1)S(1)}, u32[]{:S(2)}, u32[]{:S(2)}) collective-permute-start(bf16[272,256]{1,0:T(8,128)(2,1)S(1)} %collective-permute-done.5.refs_6_), channel_id=1, source_target_pairs={{0,14},{1,15},{2,0},{3,1},{4,2},{5,3},{6,4},{7,5},{8,6},{9,7},{10,... | collective-permute-start | bytes 417800 | tf_op jit(solution)/shard_map/ppermute | solution.py:46
  21.8 6.6 %collective-permute-start.10 = (bf16[272,256]{1,0:T(8,128)(2,1)S(1)}, bf16[272,256]{1,0:T(8,128)(2,1)S(1)}, u32[]{:S(2)}, u32[]{:S(2)}) collective-permute-start(bf16[272,256]{1,0:T(8,128)(2,1)S(1)} %collective-permute-done.6.refs_7_), channel_id=1, source_target_pairs={{0,2},{1,3},{2,4},{3,5},{4,6},{5,7},{6,8},{7,9},{8,10},{9,11},{10,... | collective-permute-start | bytes 417800 | tf_op jit(solution)/shard_map/ppermute | solution.py:46
  21.9 6.7 %collective-permute-start.2 = (bf16[272,256]{1,0:T(8,128)(2,1)S(1)}, bf16[272,256]{1,0:T(8,128)(2,1)S(1)}, u32[]{:S(2)}, u32[]{:S(2)}) collective-permute-start(bf16[272,256]{1,0:T(8,128)(2,1)S(1)} %collective-permute-done.refs_1_.refs_2_), channel_id=1, source_target_pairs={{0,16},{1,17},{2,18},{3,19},{4,20},{5,21},{6,22},{7,23},{8,24},{9,... | collective-permute-start | bytes 417800 | tf_op jit(solution)/shard_map/ppermute | solution.py:46
  24.4 6.9 %collective-permute-start.12 = (bf16[272,256]{1,0:T(8,128)(2,1)S(1)}, bf16[272,256]{1,0:T(8,128)(2,1)S(1)}, u32[]{:S(2)}, u32[]{:S(2)}) collective-permute-start(bf16[272,256]{1,0:T(8,128)(2,1)S(1)} %collective-permute-done.8.refs_5_.refs_9_), channel_id=1, source_target_pairs={{0,2},{1,3},{2,4},{3,5},{4,6},{5,7},{6,8},{7,9},{8,10},{9,11},{10,... | collective-permute-start | bytes 417800 | tf_op jit(solution)/shard_map/ppermute | solution.py:46
  24.5 6.8 %collective-permute-start.15 = (bf16[272,256]{1,0:T(8,128)(2,1)S(1)}, bf16[272,256]{1,0:T(8,128)(2,1)S(1)}, u32[]{:S(2)}, u32[]{:S(2)}) collective-permute-start(bf16[272,256]{1,0:T(8,128)(2,1)S(1)} %collective-permute-done.11.refs_8_.refs_12_), channel_id=1, source_target_pairs={{0,14},{1,15},{2,0},{3,1},{4,2},{5,3},{6,4},{7,5},{8,6},{9,7},{10,... | collective-permute-start | bytes 417800 | tf_op jit(solution)/shard_map/ppermute | solution.py:46
  27.1 9.9 %collective-permute-start.13 = (bf16[272,256]{1,0:T(8,128)(2,1)S(1)}, bf16[272,256]{1,0:T(8,128)(2,1)S(1)}, u32[]{:S(2)}, u32[]{:S(2)}) collective-permute-start(bf16[272,256]{1,0:T(8,128)(2,1)S(1)} %collective-permute-done.9.refs_6_.refs_10_), channel_id=1, source_target_pairs={{0,14},{1,15},{2,0},{3,1},{4,2},{5,3},{6,4},{7,5},{8,6},{9,7},{10,... | collective-permute-start | bytes 417800 | tf_op jit(solution)/shard_map/ppermute | solution.py:46
  28.4 8.6 %collective-permute-start.14 = (bf16[272,256]{1,0:T(8,128)(2,1)S(1)}, bf16[272,256]{1,0:T(8,128)(2,1)S(1)}, u32[]{:S(2)}, u32[]{:S(2)}) collective-permute-start(bf16[272,256]{1,0:T(8,128)(2,1)S(1)} %collective-permute-done.10.refs_7_.refs_11_), channel_id=1, source_target_pairs={{0,2},{1,3},{2,4},{3,5},{4,6},{5,7},{6,8},{7,9},{8,10},{9,11},{10,... | collective-permute-start | bytes 417800 | tf_op jit(solution)/shard_map/ppermute | solution.py:46
  31.3 7.2 %collective-permute-start.16 = (bf16[272,256]{1,0:T(8,128)(2,1)S(1)}, bf16[272,256]{1,0:T(8,128)(2,1)S(1)}, u32[]{:S(2)}, u32[]{:S(2)}) collective-permute-start(bf16[272,256]{1,0:T(8,128)(2,1)S(1)} %collective-permute-done.12.refs_5_.refs_13_), channel_id=1, source_target_pairs={{0,2},{1,3},{2,4},{3,5},{4,6},{5,7},{6,8},{7,9},{8,10},{9,11},{10,... | collective-permute-start | bytes 417800 | tf_op jit(solution)/shard_map/ppermute | solution.py:46
  31.3 7.2 %collective-permute-start.17 = (bf16[272,256]{1,0:T(8,128)(2,1)S(1)}, bf16[272,256]{1,0:T(8,128)(2,1)S(1)}, u32[]{:S(2)}, u32[]{:S(2)}) collective-permute-start(bf16[272,256]{1,0:T(8,128)(2,1)S(1)} %collective-permute-done.15.refs_8_.refs_16_), channel_id=1, source_target_pairs={{0,14},{1,15},{2,0},{3,1},{4,2},{5,3},{6,4},{7,5},{8,6},{9,7},{10,... | collective-permute-start | bytes 417800 | tf_op jit(solution)/shard_map/ppermute | solution.py:46
  63.0 7.7 %collective-permute-start.18 = (bf16[512,256]{1,0:T(8,128)(2,1)S(1)}, bf16[512,256]{1,0:T(8,128)(2,1)S(1)}, u32[]{:S(2)}, u32[]{:S(2)}) collective-permute-start(bf16[512,256]{1,0:T(8,128)(2,1)S(1)} %shard_map.92), channel_id=1, source_target_pairs={{0,16},{1,17},{2,18},{3,19},{4,20},{5,21},{6,22},{7,23},{8,24},{9,... | collective-permute-start | bytes 786440 | tf_op jit(solution)/shard_map/ppermute | solution.py:46
  70.6 2.8 %copy-start.1 = (bf16[256,256]{1,0:T(8,128)(2,1)S(1)}, bf16[256,256]{1,0:T(8,128)(2,1)}, u32[]{:S(2)}) copy-start(bf16[256,256]{1,0:T(8,128)(2,1)} %f1_ref.3) | copy-start | bytes 393220
  70.6 2.8 %copy-start.3 = (bf16[256,256]{1,0:T(8,128)(2,1)S(1)}, bf16[256,256]{1,0:T(8,128)(2,1)}, u32[]{:S(2)}) copy-start(bf16[256,256]{1,0:T(8,128)(2,1)} %f2_ref.3) | copy-start | bytes 393220
  70.6 2.8 %copy-start.6 = (s32[1,256]{1,0:T(1,128)S(1)}, s32[1,256]{1,0:T(1,128)}, u32[]{:S(2)}) copy-start(s32[1,256]{1,0:T(1,128)} %m2_ref.5) | copy-start | bytes 3076
  70.7 3.9 %collective-permute-start.19 = (f32[256,256]{1,0:T(8,128)S(1)}, f32[256,256]{1,0:T(8,128)S(1)}, u32[]{:S(2)}, u32[]{:S(2)}) collective-permute-start(f32[256,256]{1,0:T(8,128)S(1)} %shard_map.93), channel_id=1, source_target_pairs={{0,1},{1,0},{2,3},{3,2},{4,5},{5,4},{6,7},{7,6},{8,9},{9,8},{10,11... | collective-permute-start | bytes 786440 | tf_op jit(solution)/shard_map/ppermute | solution.py:46

commit v3 on v2

v3 whole, which is shorter than its diff:
```python
import math

import jax
import jax.numpy as jnp
from jax import lax
from jax.experimental import pallas as pl
from jax.experimental.pallas import tpu as pltpu
from jax.sharding import PartitionSpec as P

NEG = -1e30
BF = jnp.bfloat16
F32 = jnp.float32
N = 256
SCALE2 = (2.0 / math.sqrt(256)) * math.log2(math.e)
LN2 = math.log(2.0)
NT = (((1,), (1,)), ((), ()))
NN = (((1,), (0,)), ((), ()))
MARK = 1024.0
ARRIVAL = [(0, 0), (0, 1)]
for hop in (1, 2, 3):
    ARRIVAL += [(-hop, 0), (hop, 0), (-hop, 1), (hop, 1)]
ARRIVAL += [(-4, 0), (4, 1)]
CALLS = (10, 4, 2)


def dot(a, b, dims):
    return lax.dot_general(a, b, dims, preferred_element_type=F32)


def perm(move):
    pairs = []
    for x in range(2):
        for z in range(8):
            for c in range(2):
                x2, z2, c2 = move(x, z, c)
                pairs.append(((x * 8 + z) * 2 + c, (x2 * 8 + z2 % 8) * 2 + c2))
    return pairs


ROLE = perm(lambda x, z, c: (x, z, 1 - c))
HALF = perm(lambda x, z, c: (1 - x, z, c))
UP = perm(lambda x, z, c: (x, z + 1, c))
DOWN = perm(lambda x, z, c: (x, z - 1, c))


def send(array, pairs):
    return lax.ppermute(array, "blk", pairs)


def place():
    me = lax.axis_index("blk")
    return me % 2, me // 16, (me // 2) % 8


def eye():
    return lax.broadcasted_iota(jnp.int32, (N, N), 0) == lax.broadcasted_iota(
        jnp.int32, (N, N), 1
    )


def to_column(row, diag):
    return jnp.sum(jnp.where(diag, row, 0.0), axis=1, keepdims=True)


def merge(a, b):
    top = jnp.maximum(a, b)
    return top + jnp.log2(jnp.exp2(a - top) + jnp.exp2(b - top))


def onehot(match):
    return lax.broadcasted_iota(jnp.int32, (N, N), 0) == match


def to_row(column, diag):
    return jnp.sum(jnp.where(diag, column, 0.0), axis=0, keepdims=True)


def live_column(pick, count):
    valid = lax.broadcasted_iota(jnp.int32, (N, N), 1) < count
    return jnp.sum(jnp.where(pick & valid, 1.0, 0.0), axis=1, keepdims=True) > 0.0


def x_of(ref):
    return ref[:N, :]


def y_of(ref):
    return ref[ref.shape[0] - N :, :]


def fetch(hbm, held, sems):
    copies = [
        pltpu.make_async_copy(src, dst, sems.at[i]) for i, (src, dst) in enumerate(zip(hbm, held))
    ]
    for copy in copies:
        copy.start()
    for copy in copies:
        copy.wait()


def pack_kernel(count_ref, *refs):
    hbm, outs, held, sems = refs[:4], refs[4:10], refs[10:14], refs[14]
    own_ref, x_ref, y_ref, give_x, give_y, match_ref = outs
    fetch(hbm, held, sems)
    m1, m2, f1, f2 = held

    def masked(m_ref, f_ref):
        live = live_column(onehot(m_ref[...]), count_ref[0])
        return jnp.where(live, f_ref[...].astype(F32), MARK).astype(BF)

    def write(mx, fx, my, fy):
        y = masked(my, fy)
        y_ref[...] = y
        own_ref[N:, :] = y
        own_ref[:N, :] = fx[...]
        x_ref[...] = fx[...]
        give_x[...] = masked(mx, fx)
        give_y[...] = fy[...]
        match_ref[...] = jnp.concatenate([mx[...], my[...], jnp.zeros((6, N), jnp.int32)], axis=0)

    role, _, _ = place()

    @pl.when(role == 0)
    def _():
        write(m1, f1, m2, f2)

    @pl.when(role != 0)
    def _():
        write(m2, f2, m1, f1)


def stats_kernel(first, last, *refs):
    x_refs, refs = refs[:4], refs[4:]
    if not first:
        carry_ref, refs = refs[0], refs[1:]
    outs = 3 if last else 2
    y_refs, (o_ref, bias_ref, *message_ref) = refs[:-outs], refs[-outs:]
    diag = eye()
    count = jnp.zeros((1, 1), F32) if first else carry_ref[2:3, :1]
    chunks = []
    for j in range(0, len(y_refs), 2):
        y = jnp.concatenate([y_of(y_refs[j]), y_of(y_refs[j + 1])], axis=0)
        bias = jnp.where(y[:, :1].astype(F32) > 100.0, NEG, 0.0)
        count = count + jnp.sum(jnp.where(bias < 0.0, 0.0, 1.0), axis=0, keepdims=True)
        for k in range(2):
            block = slice((j + k) * N, (j + k + 1) * N)
            bias_ref[:, block] = to_row(bias[k * N : (k + 1) * N], diag)
        chunks.append((y, bias))
    _, half, _ = place()
    for i in range(4):
        block = slice(i * N, (i + 1) * N)
        if first:
            top = jnp.full((1, N), NEG, F32)
            total = jnp.zeros((1, N), F32)
        else:
            top = carry_ref[0:1, block]
            total = carry_ref[1:2, block]
        for y, bias in chunks:
            t = dot(y, x_of(x_refs[i]), NT) * SCALE2 + bias
            new = jnp.maximum(top, jnp.max(t, axis=0, keepdims=True))
            total = total * jnp.exp2(top - new) + jnp.sum(
                jnp.exp2(t - new), axis=0, keepdims=True
            )
            top = new
        if last:
            lse = top + jnp.log2(total)
            o_ref[:, block] = lse
            rows = pl.ds((half if i < 2 else 1 - half) * 16, 16)
            message_ref[0][rows, :, (i % 2) * N : (i % 2 + 1) * N] = jnp.broadcast_to(
                lse[None], (16, 1, N)
            )
        else:
            o_ref[0:1, block] = top
            o_ref[1:2, block] = total
    if last:
        o_ref[:, 4 * N :] = jnp.broadcast_to(count, (1, 128))
    else:
        o_ref[2:3, :] = jnp.broadcast_to(count, (1, 4 * N))


def lse_row(at, own_ref, other_ref):
    other = (at + 2) % 4
    return merge(
        own_ref[:, at * N : (at + 1) * N], other_ref[:, other * N : (other + 1) * N]
    )


def lse_column(recv, z, chain):
    role, half, _ = place()
    near = slice((1 - chain) * N, (2 - chain) * N)
    source = 2 * z + 1 - role
    return merge(recv[half * 16 + source][:, near], recv[(1 - half) * 16 + source][:, near])


def bias_of(bias_refs, j):
    for ref, count in zip(bias_refs, CALLS):
        if j < count:
            return ref[:, j * N : (j + 1) * N]
        j -= count


def ordered(match, lse, diag):
    column = to_column(lse, diag)
    return jnp.sum(jnp.where(onehot(match), column, 0.0), axis=0, keepdims=True) * LN2


def grad_kernel(pair, recv, own_lse, other_lse, match_ref, x0_ref, x1_ref, *refs):
    y_refs, bias_refs, d_refs = refs[:16], refs[16:19], refs[19:]
    role, _, z = place()
    diag = eye()
    cols = [
        lse_column(recv, lax.rem(z + offset + 8, 8), chain) for offset, chain in ARRIVAL
    ]
    for i in range(2):
        row = to_column(lse_row(2 * pair + i, own_lse, other_lse), diag)
        xb = x_of((x0_ref, x1_ref)[i])
        acc = jnp.zeros((N, N), F32)
        for j, col in enumerate(cols):
            y = y_of(y_refs[j])
            t = dot(xb, y, NT) * SCALE2 + bias_of(bias_refs, j)
            w = (jnp.exp2(t - row) + jnp.exp2(t - col)).astype(BF)
            acc = acc + dot(w, y, NN)
        if pair == 0:
            d_refs[i][...] = acc
        else:
            d_refs[0][i * N : (i + 1) * N, :] = acc.astype(BF)
    if pair == 0:
        lse_x = ordered(match_ref[0:1, :], lse_row(0, own_lse, other_lse), diag)
        lse_y = ordered(match_ref[1:2, :], cols[0], diag)
        d_refs[2][...] = jnp.where(role == 0, lse_x, lse_y)
        d_refs[3][...] = jnp.where(role == 0, lse_y, lse_x)


def sum_kernel(d0_ref, d1_ref, away_ref, x_ref, y_ref):
    x_ref[...] = d0_ref[...] + away_ref[:N, :].astype(F32)
    y_ref[...] = d1_ref[...] + away_ref[N:, :].astype(F32)


def scale_of(own_lse, other_lse):
    total = own_lse[:, 4 * N :][:, :1] + other_lse[:, 4 * N :][:, :1]
    return (2.0 / math.sqrt(N)) / (2.0 * total)


def pair_kernel(count_ref, match_ref, fx_ref, fy_ref, px_ref, py_ref):
    valid = lax.broadcasted_iota(jnp.int32, (N, N), 1) < count_ref[0]
    pick_x = onehot(match_ref[0:1, :]).astype(F32)
    pick_y = onehot(match_ref[1:2, :]).astype(F32)
    to_x = dot(jnp.where(valid, pick_x, 0.0).astype(BF), pick_y.astype(BF), NT).astype(BF)
    to_y = dot(jnp.where(valid, pick_y, 0.0).astype(BF), pick_x.astype(BF), NT).astype(BF)
    px_ref[...] = dot(to_x, fy_ref[...], NN)
    py_ref[...] = dot(to_y, x_of(fx_ref), NN)


def final_kernel(count_ref, match_ref, own_lse, other_lse, px_ref, py_ref, dx_ref, dy_ref, g1, g2):
    role, _, _ = place()
    coef = scale_of(own_lse, other_lse)

    def grad_of(match, total, pair):
        live = live_column(onehot(match), count_ref[0])
        return coef * (jnp.where(live, total, 0.0) - 2.0 * pair)

    def write(gx, gy):
        gx[...] = grad_of(match_ref[0:1, :], dx_ref[...], px_ref[...])
        gy[...] = grad_of(match_ref[1:2, :], dy_ref[...], py_ref[...])

    @pl.when(role == 0)
    def _():
        write(g1, g2)

    @pl.when(role != 0)
    def _():
        write(g2, g1)


def vmem(n):
    return [pl.BlockSpec(memory_space=pltpu.VMEM)] * n


def call(kernel, ins, outs, scratch=(), smem=0, hbm=0, limit=32):
    return pl.pallas_call(
        kernel,
        out_shape=[jax.ShapeDtypeStruct(s, d) for s, d in outs],
        in_specs=[pl.BlockSpec(memory_space=pltpu.SMEM)] * smem
        + [pl.BlockSpec(memory_space=pltpu.HBM)] * hbm
        + vmem(len(ins) - smem - hbm),
        out_specs=vmem(len(outs)),
        scratch_shapes=list(scratch),
        compiler_params=pltpu.CompilerParams(vmem_limit_bytes=limit * 2**20),
        cost_estimate=pl.CostEstimate(flops=0, bytes_accessed=2**16, transcendentals=0),
    )(*ins)


def stats(first, last, xs, ys, carry):
    def kernel(*refs):
        stats_kernel(first, last, *refs)

    outs = [((1, 1152) if last else (8, 4 * N), F32), ((1, len(ys) * N), F32)]
    if last:
        outs.append(((32, 1, 2 * N), F32))
    return call(kernel, list(xs) + ([] if first else [carry]) + list(ys), outs)


def grads(pair, recv, lses, match, xs, ys, biases):
    def kernel(*refs):
        grad_kernel(pair, *refs)

    outs = [((2 * N, N), BF)] if pair else [((N, N), F32)] * 2 + [((1, N), F32)] * 2
    return call(kernel, [recv, *lses, match, *xs] + ys + biases, outs)


def local(feat_one, feat_two, match_one, match_two, valid_counts):
    held = [pltpu.VMEM((1, N), jnp.int32)] * 2 + [pltpu.VMEM((N, N), BF)] * 2
    held += [pltpu.SemaphoreType.DMA((4,))]
    own, xa, ya, give_x, give_y, match = call(
        pack_kernel,
        (valid_counts, match_one, match_two, feat_one, feat_two),
        [((2 * N, N), BF)] + [((N, N), BF)] * 4 + [((8, N), jnp.int32)],
        held,
        smem=1,
        hbm=4,
        limit=60,
    )
    yb, xb = send(give_x, ROLE), send(give_y, ROLE)
    ups, downs = [[ya, yb]], [[ya, yb]]
    for hop in range(3):
        ups.append([send(a, UP) for a in ups[-1]])
        downs.append([send(a, DOWN) for a in downs[-1]])
    xs = [own, xb, send(xa, HALF), send(xb, HALF)]
    ys = [own, yb]
    for hop in (1, 2, 3):
        ys += [ups[hop][0], downs[hop][0], ups[hop][1], downs[hop][1]]
    ys += [send(ups[3][0], UP), send(downs[3][1], DOWN)]
    carry, biases, start = None, [], 0
    for i, count in enumerate(CALLS):
        carry, bias, *message = stats(i == 0, i == 2, xs, ys[start : start + count], carry)
        biases.append(bias)
        start += count
    recv = lax.all_to_all(message[0], "blk", 0, 0)
    lses = [carry, send(carry, HALF)]
    px, py = call(pair_kernel, (valid_counts, match, own, give_y), [((N, N), F32)] * 2, smem=1)
    recv, px, py = lax.optimization_barrier((recv, px, py))
    (away,) = grads(1, recv, lses, match, xs[2:], ys, biases)
    away = send(away, HALF)
    d0, d1, row_lse, col_lse = grads(0, recv, lses, match, xs[:2], ys, biases)
    dx, dy = call(sum_kernel, (d0, d1, away), [((N, N), F32)] * 2)
    dy = send(dy, ROLE)
    grad_one, grad_two = call(
        final_kernel,
        [valid_counts, match, *lses, px, py, dx, dy],
        [((N, N), F32)] * 2,
        smem=1,
    )
    return grad_one, grad_two, row_lse.reshape(N), col_lse.reshape(N)


def solution(mesh):
    both = ("grp", "blk")
    return jax.shard_map(
        local,
        mesh=mesh,
        in_specs=(P(both, None),) * 4 + (P(both),),
        out_specs=(P(both, None), P(both, None), P(both), P(both)),
        check_vma=False,
    )
```

time: 75.9 us -> 74.1 us (0.976)
  blocking collectives: 18.3 us -> 0 us
  starting transfers between devices: 30.2 us -> 42.3 us
  waiting for transfers between devices: 4.85 us -> 13.7 us
  Pallas kernels: 18.3 us -> 15.6 us
  local copies, waits for them, and re-layouts: 2.58 us -> 0.96 us
    all_to_all x1 -> x0, blocking collectives: 18.3 us -> none  [local(): lax.all_to_all(jnp.broadcast_to(carry[None], (32, 1, 1152)), 'blk', 0, 0)]
    all_to_all x0 -> x1, starting transfers between devices: none -> 10.5 us  [local(): recv = lax.all_to_all(message[0], 'blk', 0, 0)]
    all_to_all x0 -> x1, waiting for transfers between devices: none -> 6.17 us  [local(): recv = lax.all_to_all(message[0], 'blk', 0, 0)]
    pallas_call x11 -> x9, Pallas kernels: 18.3 us -> 15.6 us  [call(): pl.pallas_call(kernel, out_shape=[jax.ShapeDtypeStruct(s, d) for s, d in...]
    ppermute x20 -> x21, waiting for transfers between devices: 4.85 us -> 7.51 us  [send(): return lax.ppermute(array, 'blk', pairs)]
    ppermute x20 -> x21, starting transfers between devices: 30.2 us -> 31.8 us  [send(): return lax.ppermute(array, 'blk', pairs)]
    unnamed x14 -> x8, local copies, waits for them, and re-layouts: 2.5 us -> 0.96 us
  transfers between devices with their start and end apart: 20 -> 22, of which waited for: 3 -> 6; matrix products, arithmetic and copies ran while one was open for 0% -> 0% of each run, Pallas kernels for 14% -> 11%
where the time goes in v3:
time: 74.1 us; the launch traced here: 73.9 us
  starting transfers between devices  42.3 us (57%)
  Pallas kernels  15.6 us (21%)
  waiting for transfers between devices  13.7 us (18%)
  between operations  1.38 us (2%)
  local copies, waits for them, and re-layouts  0.96 us (1%)
    ppermute x21, starting transfers between devices, send(): return lax.ppermute(array, 'blk', pairs)  31.8 us
    pallas_call x9, Pallas kernels, call(): pl.pallas_call(kernel, out_shape=[jax.ShapeDtypeStruct(s, d) for s, d in...  15.6 us
    all_to_all x1, starting transfers between devices, local(): recv = lax.all_to_all(message[0], 'blk', 0, 0)  10.5 us
    ppermute x21, waiting for transfers between devices, send(): return lax.ppermute(array, 'blk', pairs)  7.51 us
    all_to_all x1, waiting for transfers between devices, local(): recv = lax.all_to_all(message[0], 'blk', 0, 0)  6.17 us
  transfers between devices with their start and end apart: 22, of which 6 were waited for; matrix products, arithmetic and copies ran while one was open for 0% of the time, Pallas kernels for 11%

profile of v3, /device:TPU:1, one launch (start us, length us, event | category | flops | bytes accessed | tf_op | source)
XLA Modules:
  0.0 73.9 jit_solution(5128908827084331593)
XLA Ops:
  1.3 2.0 %shard_map.84 = (bf16[512,256]{1,0:T(8,128)(2,1)}, bf16[256,256]{1,0:T(8,128)(2,1)}, bf16[256,256]{1,0:T(8,128)(2,1)}, bf16[256,256]{1,0:T(8,128)(2,1)}, bf16[256,256]{1,0:T(8,128)(2,1)}, /*index=5*/s32[8,256]{1,0:T(8,128)}) custom-call(s32[1]{0:T(128)S(6)} %copy.9.count_ref, s32[1,256]{1,0:T(1,128)} %refs_0_.1, s32[1,256]{1,0:T(1,128)} %refs_1_.1, ...), custom_call_target="tpu_custom_call" | custom-call | bytes 65536 | tf_op jit(solution)/shard_map/pallas_call | solution.py:280
  3.3 3.3 %collective-permute-start.3 = (bf16[256,256]{1,0:T(8,128)(2,1)}, bf16[256,256]{1,0:T(8,128)(2,1)S(1)}, u32[]{:S(2)}, u32[]{:S(2)}) collective-permute-start(bf16[256,256]{1,0:T(8,128)(2,1)} %get-tuple-element.34), channel_id=1, source_target_pairs={{0,1},{1,0},{2,3},{3,2},{4,5},{5,4},{6,7},{7,6},{8,9},{9,8},{10,11... | collective-permute-start | bytes 393224 | tf_op jit(solution)/shard_map/ppermute | solution.py:47
  6.7 0.0 collective-permute-start.4
  6.7 1.2 %collective-permute-done.3.refs_5_.refs_7_ = bf16[256,256]{1,0:T(8,128)(2,1)S(1)} collective-permute-done((bf16[256,256]{1,0:T(8,128)(2,1)}, bf16[256,256]{1,0:T(8,128)(2,1)S(1)}, u32[]{:S(2)}, u32[]{:S(2)}) %collective-permute-start.3) | collective-permute-done | bytes 131104 | tf_op jit(solution)/shard_map/ppermute | solution.py:47
  7.9 3.8 %collective-permute-start.7 = (bf16[256,256]{1,0:T(8,128)(2,1)S(1)}, bf16[256,256]{1,0:T(8,128)(2,1)S(1)}, u32[]{:S(2)}, u32[]{:S(2)}) collective-permute-start(bf16[256,256]{1,0:T(8,128)(2,1)S(1)} %collective-permute-done.3.refs_5_.refs_7_), channel_id=1, source_target_pairs={{0,14},{1,15},{2,0},{3,1},{4,2},{5,3},{6,4},{7,5},{8,6},{9,7},{10,... | collective-permute-start | bytes 393224 | tf_op jit(solution)/shard_map/ppermute | solution.py:47
  11.7 2.7 %collective-permute-start.1 = (bf16[256,256]{1,0:T(8,128)(2,1)}, bf16[256,256]{1,0:T(8,128)(2,1)S(1)}, u32[]{:S(2)}, u32[]{:S(2)}) collective-permute-start(bf16[256,256]{1,0:T(8,128)(2,1)} %get-tuple-element.33), channel_id=1, source_target_pairs={{0,16},{1,17},{2,18},{3,19},{4,20},{5,21},{6,22},{7,23},{8,24},{9,... | collective-permute-start | bytes 393224 | tf_op jit(solution)/shard_map/ppermute | solution.py:47
  14.4 0.7 collective-permute-start.5
  15.2 0.7 collective-permute-start.6
  15.9 0.0 collective-permute-done.4.refs_6_.refs_8_
  15.9 0.0 collective-permute-start.8
  15.9 0.0 collective-permute-done.7.refs_9_.refs_11_
  16.0 2.6 %collective-permute-start.11 = (bf16[256,256]{1,0:T(8,128)(2,1)S(1)}, bf16[256,256]{1,0:T(8,128)(2,1)S(1)}, u32[]{:S(2)}, u32[]{:S(2)}) collective-permute-start(bf16[256,256]{1,0:T(8,128)(2,1)S(1)} %collective-permute-done.7.refs_9_.refs_11_), channel_id=1, source_target_pairs={{0,14},{1,15},{2,0},{3,1},{4,2},{5,3},{6,4},{7,5},{8,6},{9,7},{10,... | collective-permute-start | bytes 393224 | tf_op jit(solution)/shard_map/ppermute | solution.py:47
  18.6 0.0 collective-permute-done.1.refs_2_.refs_4_
  18.6 2.0 %collective-permute-start = (bf16[256,256]{1,0:T(8,128)(2,1)}, bf16[256,256]{1,0:T(8,128)(2,1)S(1)}, u32[]{:S(2)}, u32[]{:S(2)}) collective-permute-start(bf16[256,256]{1,0:T(8,128)(2,1)} %get-tuple-element.32.fy_ref), channel_id=1, source_target_pairs={{0,1},{1,0},{2,3},{3,2},{4,5},{5,4},{6,7},{7,6},{8,9},{9,8},{10,11... | collective-permute-start | bytes 393224 | tf_op jit(solution)/shard_map/ppermute | solution.py:47
  20.6 0.0 collective-permute-done.5.refs_7_.refs_9_
  20.6 0.7 collective-permute-start.9
  21.4 0.0 collective-permute-done.6.refs_8_.refs_10_
  21.4 0.7 collective-permute-start.10
  22.1 0.9 %collective-permute-done.8.refs_10_.refs_12_ = bf16[256,256]{1,0:T(8,128)(2,1)S(1)} collective-permute-done((bf16[256,256]{1,0:T(8,128)(2,1)S(1)}, bf16[256,256]{1,0:T(8,128)(2,1)S(1)}, u32[]{:S(2)}, u32[]{:S(2)}) %collective-permute-start.8) | collective-permute-done | bytes 131104 | tf_op jit(solution)/shard_map/ppermute | solution.py:47
  23.0 0.0 collective-permute-start.12
  23.0 0.0 collective-permute-done.11.refs_13_.refs_15_
  23.0 2.7 %collective-permute-start.15 = (bf16[256,256]{1,0:T(8,128)(2,1)S(1)}, bf16[256,256]{1,0:T(8,128)(2,1)S(1)}, u32[]{:S(2)}, u32[]{:S(2)}) collective-permute-start(bf16[256,256]{1,0:T(8,128)(2,1)S(1)} %collective-permute-done.11.refs_13_.refs_15_), channel_id=1, source_target_pairs={{0,14},{1,15},{2,0},{3,1},{4,2},{5,3},{6,4},{7,5},{8,6},{9,7},{10,... | collective-permute-start | bytes 393224 | tf_op jit(solution)/shard_map/ppermute | solution.py:47
  25.7 0.0 collective-permute-done.refs_1_.refs_5_
  25.7 1.2 %collective-permute-start.2 = (bf16[256,256]{1,0:T(8,128)(2,1)S(1)}, bf16[256,256]{1,0:T(8,128)(2,1)S(1)}, u32[]{:S(2)}, u32[]{:S(2)}) collective-permute-start(bf16[256,256]{1,0:T(8,128)(2,1)S(1)} %collective-permute-done.refs_1_.refs_5_), channel_id=1, source_target_pairs={{0,16},{1,17},{2,18},{3,19},{4,20},{5,21},{6,22},{7,23},{8,24},{9,... | collective-permute-start | bytes 393224 | tf_op jit(solution)/shard_map/ppermute | solution.py:47
  26.8 0.0 collective-permute-done.9.refs_11_.refs_13_
  26.8 1.2 %collective-permute-start.13 = (bf16[256,256]{1,0:T(8,128)(2,1)S(1)}, bf16[256,256]{1,0:T(8,128)(2,1)S(1)}, u32[]{:S(2)}, u32[]{:S(2)}) collective-permute-start(bf16[256,256]{1,0:T(8,128)(2,1)S(1)} %collective-permute-done.9.refs_11_.refs_13_), channel_id=1, source_target_pairs={{0,14},{1,15},{2,0},{3,1},{4,2},{5,3},{6,4},{7,5},{8,6},{9,7},{10,... | collective-permute-start | bytes 393224 | tf_op jit(solution)/shard_map/ppermute | solution.py:47
  28.0 0.0 collective-permute-done.10.refs_12_.refs_14_
  28.0 0.3 collective-permute-start.14
  28.3 0.2 collective-permute-done.12.refs_5_.refs_16_
  28.5 0.0 collective-permute-start.16
  28.6 0.0 collective-permute-done.15.refs_8_.refs_19_
  28.6 2.6 %collective-permute-start.17 = (bf16[256,256]{1,0:T(8,128)(2,1)S(1)}, bf16[256,256]{1,0:T(8,128)(2,1)S(1)}, u32[]{:S(2)}, u32[]{:S(2)}) collective-permute-start(bf16[256,256]{1,0:T(8,128)(2,1)S(1)} %collective-permute-done.15.refs_8_.refs_19_), channel_id=1, source_target_pairs={{0,14},{1,15},{2,0},{3,1},{4,2},{5,3},{6,4},{7,5},{8,6},{9,7},{10,... | collective-permute-start | bytes 393224 | tf_op jit(solution)/shard_map/ppermute | solution.py:47
  31.2 0.0 collective-permute-done.2.refs_3_.refs_5_
  31.2 0.0 copy-start
  31.2 0.9 %copy-done = bf16[512,256]{1,0:T(8,128)(2,1)S(1)} copy-done((bf16[512,256]{1,0:T(8,128)(2,1)S(1)}, bf16[512,256]{1,0:T(8,128)(2,1)}, u32[]{:S(2)}) %copy-start) | copy-done | bytes 262168
  32.1 3.1 %shard_map.85 = (f32[8,1024]{1,0:T(8,128)S(1)}, f32[1,2560]{1,0:T(1,128)S(1)}) custom-call(bf16[512,256]{1,0:T(8,128)(2,1)S(1)} %copy-done, bf16[256,256]{1,0:T(8,128)(2,1)S(1)} %collective-permute-done.refs_1_.refs_5_, bf16[256,256]{1,0:T(8,128)(2,1)S(1)} %collective-permute-done.1.refs_2_.refs_4_, ...), custom_call_target="tpu_custom_call" | custom-call | bytes 65536 | tf_op jit(solution)/shard_map/pallas_call | solution.py:280
  35.3 0.0 collective-permute-done.13.refs_6_.refs_17_
  35.3 0.0 collective-permute-done.14.refs_7_.refs_18_
  35.3 1.4 %shard_map.86 = (f32[8,1024]{1,0:T(8,128)S(1)}, f32[1,1024]{1,0:T(1,128)S(1)}) custom-call(bf16[512,256]{1,0:T(8,128)(2,1)S(1)} %copy-done, bf16[256,256]{1,0:T(8,128)(2,1)S(1)} %collective-permute-done.refs_1_.refs_5_, bf16[256,256]{1,0:T(8,128)(2,1)S(1)} %collective-permute-done.1.refs_2_.refs_4_, ...), custom_call_target="tpu_custom_call" | custom-call | bytes 65536 | tf_op jit(solution)/shard_map/pallas_call | solution.py:280
  36.7 0.0 collective-permute-done.16.refs_5_.refs_20_
  36.7 0.0 collective-permute-done.17.refs_6_.refs_21_
  36.7 0.0 copy-start.1
  36.7 0.0 copy-start.3
  36.7 1.5 %shard_map.87 = (f32[1,1152]{1,0:T(1,128)S(1)}, f32[1,512]{1,0:T(1,128)S(1)}, f32[32,1,512]{2,1,0:T(1,128)}) custom-call(bf16[512,256]{1,0:T(8,128)(2,1)S(1)} %copy-done, bf16[256,256]{1,0:T(8,128)(2,1)S(1)} %collective-permute-done.refs_1_.refs_5_, bf16[256,256]{1,0:T(8,128)(2,1)S(1)} %collective-permute-done.1.refs_2_.refs_4_, ...), custom_call_target="tpu_custom_call" | custom-call | bytes 65536 | tf_op jit(solution)/shard_map/pallas_call | solution.py:280
  38.2 0.0 copy-start.2
  38.2 10.5 %all-to-all-start = ((f32[32,1,512]{2,1,0:T(1,128)}), f32[32,1,512]{2,1,0:T(1,128)S(1)}, u32[]{:S(2)}, u32[]{:S(2)}) async-start(f32[32,1,512]{2,1,0:T(1,128)} %get-tuple-element.39), calls=%async_computation | async-start | bytes 131072 | tf_op jit(solution)/shard_map/all_to_all | solution.py:338
  48.7 3.0 %collective-permute-start.18 = (f32[1,1152]{1,0:T(1,128)S(1)}, f32[1,1152]{1,0:T(1,128)S(1)}, u32[]{:S(2)}, u32[]{:S(2)}) collective-permute-start(f32[1,1152]{1,0:T(1,128)S(1)} %get-tuple-element.38.refs_1_.own_lse), channel_id=1, source_target_pairs={{0,16},{1,17},{2,18},{3,19},{4,20},{5,21},{6,22},{7,23},{8,24},{9,... | collective-permute-start | bytes 13832 | tf_op jit(solution)/shard_map/ppermute | solution.py:47
  51.7 0.0 copy-done.1
  51.7 0.0 copy-done.3
  51.7 0.0 copy-done.2
  51.7 0.4 shard_map.88
  52.1 6.2 %all-to-all-done.refs_0_ = f32[32,1,512]{2,1,0:T(1,128)S(1)} async-done(((f32[32,1,512]{2,1,0:T(1,128)}), f32[32,1,512]{2,1,0:T(1,128)S(1)}, u32[]{:S(2)}, u32[]{:S(2)}) %all-to-all-start) | async-done | bytes 65568 | tf_op jit(solution)/shard_map/all_to_all | solution.py:338
  58.3 0.0 collective-permute-done.18.refs_2_.other_lse
  58.3 2.8 %shard_map.90 = bf16[512,256]{1,0:T(8,128)(2,1)S(1)} custom-call(f32[32,1,512]{2,1,0:T(1,128)S(1)} %all-to-all-done.refs_0_, f32[1,1152]{1,0:T(1,128)S(1)} %get-tuple-element.38.refs_1_.own_lse, f32[1,1152]{1,0:T(1,128)S(1)} %collective-permute-done.18.refs_2_.other_lse, s32[8,256]{1,0:T(8,128)S(1)} %copy-done.2, ...), custom_call_target="tpu_custom_call" | custom-call | bytes 65536 | tf_op jit(solution)/shard_map/pallas_call | solution.py:280
  61.1 1.0 %collective-permute-start.19 = (bf16[512,256]{1,0:T(8,128)(2,1)S(1)}, bf16[512,256]{1,0:T(8,128)(2,1)S(1)}, u32[]{:S(2)}, u32[]{:S(2)}) collective-permute-start(bf16[512,256]{1,0:T(8,128)(2,1)S(1)} %shard_map.90), channel_id=1, source_target_pairs={{0,16},{1,17},{2,18},{3,19},{4,20},{5,21},{6,22},{7,23},{8,24},{9,... | collective-permute-start | bytes 786440 | tf_op jit(solution)/shard_map/ppermute | solution.py:47
  62.1 3.3 %shard_map.89 = (f32[256,256]{1,0:T(8,128)S(1)}, f32[256,256]{1,0:T(8,128)S(1)}, f32[1,256]{1,0:T(1,128)}, f32[1,256]{1,0:T(1,128)}) custom-call(f32[32,1,512]{2,1,0:T(1,128)S(1)} %all-to-all-done.refs_0_, f32[1,1152]{1,0:T(1,128)S(1)} %get-tuple-element.38.refs_1_.own_lse, f32[1,1152]{1,0:T(1,128)S(1)} %collective-permute-done.18.refs_2_.other_lse, ...), custom_call_target="tpu_custom_call" | custom-call | bytes 65536 | tf_op jit(solution)/shard_map/pallas_call | solution.py:280
  65.4 4.0 %collective-permute-done.19.away_ref = bf16[512,256]{1,0:T(8,128)(2,1)S(1)} collective-permute-done((bf16[512,256]{1,0:T(8,128)(2,1)S(1)}, bf16[512,256]{1,0:T(8,128)(2,1)S(1)}, u32[]{:S(2)}, u32[]{:S(2)}) %collective-permute-start.19) | collective-permute-done | bytes 262176 | tf_op jit(solution)/shard_map/ppermute | solution.py:47
  69.4 0.1 shard_map.91
  69.5 2.3 %collective-permute-start.20 = (f32[256,256]{1,0:T(8,128)S(1)}, f32[256,256]{1,0:T(8,128)S(1)}, u32[]{:S(2)}, u32[]{:S(2)}) collective-permute-start(f32[256,256]{1,0:T(8,128)S(1)} %get-tuple-element.51), channel_id=1, source_target_pairs={{0,1},{1,0},{2,3},{3,2},{4,5},{5,4},{6,7},{7,6},{8,9},{9,8},{10,11... | collective-permute-start | bytes 786440 | tf_op jit(solution)/shard_map/ppermute | solution.py:47
  71.7 1.2 %collective-permute-done.20.dy_ref = f32[256,256]{1,0:T(8,128)S(1)} collective-permute-done((f32[256,256]{1,0:T(8,128)S(1)}, f32[256,256]{1,0:T(8,128)S(1)}, u32[]{:S(2)}, u32[]{:S(2)}) %collective-permute-start.20) | collective-permute-done | bytes 262176 | tf_op jit(solution)/shard_map/ppermute | solution.py:47
  72.9 1.0 %shard_map.92 = (f32[256,256]{1,0:T(8,128)}, f32[256,256]{1,0:T(8,128)}) custom-call(s32[1]{0:T(128)S(6)} %copy.9.count_ref, s32[8,256]{1,0:T(8,128)S(1)} %copy-done.2, f32[1,1152]{1,0:T(1,128)S(1)} %get-tuple-element.38.refs_1_.own_lse, f32[1,1152]{1,0:T(1,128)S(1)} %collective-permute-done.18.refs_2_.other_lse, f32[256,256]{1,0:T(8,128)S(1)} %get-tuple-element.42.px_ref, ...), custom_call_target="tpu_custom_call" | custom-call | bytes 65536 | tf_op jit(solution)/shard_map/pallas_call | solution.py:280
Async XLA Ops:
  3.3 4.5 %collective-permute-start.3 = (bf16[256,256]{1,0:T(8,128)(2,1)}, bf16[256,256]{1,0:T(8,128)(2,1)S(1)}, u32[]{:S(2)}, u32[]{:S(2)}) collective-permute-start(bf16[256,256]{1,0:T(8,128)(2,1)} %get-tuple-element.34), channel_id=1, source_target_pairs={{0,1},{1,0},{2,3},{3,2},{4,5},{5,4},{6,7},{7,6},{8,9},{9,8},{10,11... | collective-permute-start | bytes 393224 | tf_op jit(solution)/shard_map/ppermute | solution.py:47
  6.7 9.3 %collective-permute-start.4 = (bf16[256,256]{1,0:T(8,128)(2,1)}, bf16[256,256]{1,0:T(8,128)(2,1)S(1)}, u32[]{:S(2)}, u32[]{:S(2)}) collective-permute-start(bf16[256,256]{1,0:T(8,128)(2,1)} %get-tuple-element.35), channel_id=1, source_target_pairs={{0,2},{1,3},{2,4},{3,5},{4,6},{5,7},{6,8},{7,9},{8,10},{9,11},{10,... | collective-permute-start | bytes 393224 | tf_op jit(solution)/shard_map/ppermute | solution.py:47
  7.9 8.1 %collective-permute-start.7 = (bf16[256,256]{1,0:T(8,128)(2,1)S(1)}, bf16[256,256]{1,0:T(8,128)(2,1)S(1)}, u32[]{:S(2)}, u32[]{:S(2)}) collective-permute-start(bf16[256,256]{1,0:T(8,128)(2,1)S(1)} %collective-permute-done.3.refs_5_.refs_7_), channel_id=1, source_target_pairs={{0,14},{1,15},{2,0},{3,1},{4,2},{5,3},{6,4},{7,5},{8,6},{9,7},{10,... | collective-permute-start | bytes 393224 | tf_op jit(solution)/shard_map/ppermute | solution.py:47
  11.7 6.9 %collective-permute-start.1 = (bf16[256,256]{1,0:T(8,128)(2,1)}, bf16[256,256]{1,0:T(8,128)(2,1)S(1)}, u32[]{:S(2)}, u32[]{:S(2)}) collective-permute-start(bf16[256,256]{1,0:T(8,128)(2,1)} %get-tuple-element.33), channel_id=1, source_target_pairs={{0,16},{1,17},{2,18},{3,19},{4,20},{5,21},{6,22},{7,23},{8,24},{9,... | collective-permute-start | bytes 393224 | tf_op jit(solution)/shard_map/ppermute | solution.py:47
  14.4 6.2 %collective-permute-start.5 = (bf16[256,256]{1,0:T(8,128)(2,1)}, bf16[256,256]{1,0:T(8,128)(2,1)S(1)}, u32[]{:S(2)}, u32[]{:S(2)}) collective-permute-start(bf16[256,256]{1,0:T(8,128)(2,1)} %get-tuple-element.35), channel_id=1, source_target_pairs={{0,14},{1,15},{2,0},{3,1},{4,2},{5,3},{6,4},{7,5},{8,6},{9,7},{10,... | collective-permute-start | bytes 393224 | tf_op jit(solution)/shard_map/ppermute | solution.py:47
  15.2 6.2 %collective-permute-start.6 = (bf16[256,256]{1,0:T(8,128)(2,1)S(1)}, bf16[256,256]{1,0:T(8,128)(2,1)S(1)}, u32[]{:S(2)}, u32[]{:S(2)}) collective-permute-start(bf16[256,256]{1,0:T(8,128)(2,1)S(1)} %collective-permute-done.3.refs_5_.refs_7_), channel_id=1, source_target_pairs={{0,2},{1,3},{2,4},{3,5},{4,6},{5,7},{6,8},{7,9},{8,10},{9,11},{10,... | collective-permute-start | bytes 393224 | tf_op jit(solution)/shard_map/ppermute | solution.py:47
  15.9 7.1 %collective-permute-start.8 = (bf16[256,256]{1,0:T(8,128)(2,1)S(1)}, bf16[256,256]{1,0:T(8,128)(2,1)S(1)}, u32[]{:S(2)}, u32[]{:S(2)}) collective-permute-start(bf16[256,256]{1,0:T(8,128)(2,1)S(1)} %collective-permute-done.4.refs_6_.refs_8_), channel_id=1, source_target_pairs={{0,2},{1,3},{2,4},{3,5},{4,6},{5,7},{6,8},{7,9},{8,10},{9,11},{10,... | collective-permute-start | bytes 393224 | tf_op jit(solution)/shard_map/ppermute | solution.py:47
  16.0 7.0 %collective-permute-start.11 = (bf16[256,256]{1,0:T(8,128)(2,1)S(1)}, bf16[256,256]{1,0:T(8,128)(2,1)S(1)}, u32[]{:S(2)}, u32[]{:S(2)}) collective-permute-start(bf16[256,256]{1,0:T(8,128)(2,1)S(1)} %collective-permute-done.7.refs_9_.refs_11_), channel_id=1, source_target_pairs={{0,14},{1,15},{2,0},{3,1},{4,2},{5,3},{6,4},{7,5},{8,6},{9,7},{10,... | collective-permute-start | bytes 393224 | tf_op jit(solution)/shard_map/ppermute | solution.py:47
  18.6 7.1 %collective-permute-start = (bf16[256,256]{1,0:T(8,128)(2,1)}, bf16[256,256]{1,0:T(8,128)(2,1)S(1)}, u32[]{:S(2)}, u32[]{:S(2)}) collective-permute-start(bf16[256,256]{1,0:T(8,128)(2,1)} %get-tuple-element.32.fy_ref), channel_id=1, source_target_pairs={{0,1},{1,0},{2,3},{3,2},{4,5},{5,4},{6,7},{7,6},{8,9},{9,8},{10,11... | collective-permute-start | bytes 393224 | tf_op jit(solution)/shard_map/ppermute | solution.py:47
  20.6 6.2 %collective-permute-start.9 = (bf16[256,256]{1,0:T(8,128)(2,1)S(1)}, bf16[256,256]{1,0:T(8,128)(2,1)S(1)}, u32[]{:S(2)}, u32[]{:S(2)}) collective-permute-start(bf16[256,256]{1,0:T(8,128)(2,1)S(1)} %collective-permute-done.5.refs_7_.refs_9_), channel_id=1, source_target_pairs={{0,14},{1,15},{2,0},{3,1},{4,2},{5,3},{6,4},{7,5},{8,6},{9,7},{10,... | collective-permute-start | bytes 393224 | tf_op jit(solution)/shard_map/ppermute | solution.py:47
  21.4 6.7 %collective-permute-start.10 = (bf16[256,256]{1,0:T(8,128)(2,1)S(1)}, bf16[256,256]{1,0:T(8,128)(2,1)S(1)}, u32[]{:S(2)}, u32[]{:S(2)}) collective-permute-start(bf16[256,256]{1,0:T(8,128)(2,1)S(1)} %collective-permute-done.6.refs_8_.refs_10_), channel_id=1, source_target_pairs={{0,2},{1,3},{2,4},{3,5},{4,6},{5,7},{6,8},{7,9},{8,10},{9,11},{10,... | collective-permute-start | bytes 393224 | tf_op jit(solution)/shard_map/ppermute | solution.py:47
  23.0 5.5 %collective-permute-start.12 = (bf16[256,256]{1,0:T(8,128)(2,1)S(1)}, bf16[256,256]{1,0:T(8,128)(2,1)S(1)}, u32[]{:S(2)}, u32[]{:S(2)}) collective-permute-start(bf16[256,256]{1,0:T(8,128)(2,1)S(1)} %collective-permute-done.8.refs_10_.refs_12_), channel_id=1, source_target_pairs={{0,2},{1,3},{2,4},{3,5},{4,6},{5,7},{6,8},{7,9},{8,10},{9,11},{10,... | collective-permute-start | bytes 393224 | tf_op jit(solution)/shard_map/ppermute | solution.py:47
  23.0 5.6 %collective-permute-start.15 = (bf16[256,256]{1,0:T(8,128)(2,1)S(1)}, bf16[256,256]{1,0:T(8,128)(2,1)S(1)}, u32[]{:S(2)}, u32[]{:S(2)}) collective-permute-start(bf16[256,256]{1,0:T(8,128)(2,1)S(1)} %collective-permute-done.11.refs_13_.refs_15_), channel_id=1, source_target_pairs={{0,14},{1,15},{2,0},{3,1},{4,2},{5,3},{6,4},{7,5},{8,6},{9,7},{10,... | collective-permute-start | bytes 393224 | tf_op jit(solution)/shard_map/ppermute | solution.py:47
  25.7 5.5 %collective-permute-start.2 = (bf16[256,256]{1,0:T(8,128)(2,1)S(1)}, bf16[256,256]{1,0:T(8,128)(2,1)S(1)}, u32[]{:S(2)}, u32[]{:S(2)}) collective-permute-start(bf16[256,256]{1,0:T(8,128)(2,1)S(1)} %collective-permute-done.refs_1_.refs_5_), channel_id=1, source_target_pairs={{0,16},{1,17},{2,18},{3,19},{4,20},{5,21},{6,22},{7,23},{8,24},{9,... | collective-permute-start | bytes 393224 | tf_op jit(solution)/shard_map/ppermute | solution.py:47
  26.8 8.5 %collective-permute-start.13 = (bf16[256,256]{1,0:T(8,128)(2,1)S(1)}, bf16[256,256]{1,0:T(8,128)(2,1)S(1)}, u32[]{:S(2)}, u32[]{:S(2)}) collective-permute-start(bf16[256,256]{1,0:T(8,128)(2,1)S(1)} %collective-permute-done.9.refs_11_.refs_13_), channel_id=1, source_target_pairs={{0,14},{1,15},{2,0},{3,1},{4,2},{5,3},{6,4},{7,5},{8,6},{9,7},{10,... | collective-permute-start | bytes 393224 | tf_op jit(solution)/shard_map/ppermute | solution.py:47
  28.0 7.3 %collective-permute-start.14 = (bf16[256,256]{1,0:T(8,128)(2,1)S(1)}, bf16[256,256]{1,0:T(8,128)(2,1)S(1)}, u32[]{:S(2)}, u32[]{:S(2)}) collective-permute-start(bf16[256,256]{1,0:T(8,128)(2,1)S(1)} %collective-permute-done.10.refs_12_.refs_14_), channel_id=1, source_target_pairs={{0,2},{1,3},{2,4},{3,5},{4,6},{5,7},{6,8},{7,9},{8,10},{9,11},{10,... | collective-permute-start | bytes 393224 | tf_op jit(solution)/shard_map/ppermute | solution.py:47
  28.5 8.2 %collective-permute-start.16 = (bf16[256,256]{1,0:T(8,128)(2,1)S(1)}, bf16[256,256]{1,0:T(8,128)(2,1)S(1)}, u32[]{:S(2)}, u32[]{:S(2)}) collective-permute-start(bf16[256,256]{1,0:T(8,128)(2,1)S(1)} %collective-permute-done.12.refs_5_.refs_16_), channel_id=1, source_target_pairs={{0,2},{1,3},{2,4},{3,5},{4,6},{5,7},{6,8},{7,9},{8,10},{9,11},{10,... | collective-permute-start | bytes 393224 | tf_op jit(solution)/shard_map/ppermute | solution.py:47
  28.6 8.1 %collective-permute-start.17 = (bf16[256,256]{1,0:T(8,128)(2,1)S(1)}, bf16[256,256]{1,0:T(8,128)(2,1)S(1)}, u32[]{:S(2)}, u32[]{:S(2)}) collective-permute-start(bf16[256,256]{1,0:T(8,128)(2,1)S(1)} %collective-permute-done.15.refs_8_.refs_19_), channel_id=1, source_target_pairs={{0,14},{1,15},{2,0},{3,1},{4,2},{5,3},{6,4},{7,5},{8,6},{9,7},{10,... | collective-permute-start | bytes 393224 | tf_op jit(solution)/shard_map/ppermute | solution.py:47
  31.2 1.0 %copy-start = (bf16[512,256]{1,0:T(8,128)(2,1)S(1)}, bf16[512,256]{1,0:T(8,128)(2,1)}, u32[]{:S(2)}) copy-start(bf16[512,256]{1,0:T(8,128)(2,1)} %get-tuple-element.31.refs_0_.refs_4_.fx_ref.refs_6_) | copy-start | bytes 786436
  36.7 15.0 %copy-start.1 = (bf16[512,256]{1,0:T(8,128)(2,1)S(1)}, bf16[512,256]{1,0:T(8,128)(2,1)}, u32[]{:S(2)}) copy-start(bf16[512,256]{1,0:T(8,128)(2,1)} %get-tuple-element.31.refs_0_.refs_4_.fx_ref.refs_6_) | copy-start | bytes 786436
  36.7 15.0 %copy-start.3 = (bf16[256,256]{1,0:T(8,128)(2,1)S(1)}, bf16[256,256]{1,0:T(8,128)(2,1)}, u32[]{:S(2)}) copy-start(bf16[256,256]{1,0:T(8,128)(2,1)} %get-tuple-element.32.fy_ref) | copy-start | bytes 393220
  38.2 13.5 %copy-start.2 = (s32[8,256]{1,0:T(8,128)S(1)}, s32[8,256]{1,0:T(8,128)}, u32[]{:S(2)}) copy-start(s32[8,256]{1,0:T(8,128)} %get-tuple-element.30.match_ref.refs_3_) | copy-start | bytes 24580
  38.2 20.1 %all-to-all-start = ((f32[32,1,512]{2,1,0:T(1,128)}), f32[32,1,512]{2,1,0:T(1,128)S(1)}, u32[]{:S(2)}, u32[]{:S(2)}) async-start(f32[32,1,512]{2,1,0:T(1,128)} %get-tuple-element.39), calls=%async_computation | async-start | bytes 131072 | tf_op jit(solution)/shard_map/all_to_all | solution.py:338
  48.7 9.6 %collective-permute-start.18 = (f32[1,1152]{1,0:T(1,128)S(1)}, f32[1,1152]{1,0:T(1,128)S(1)}, u32[]{:S(2)}, u32[]{:S(2)}) collective-permute-start(f32[1,1152]{1,0:T(1,128)S(1)} %get-tuple-element.38.refs_1_.own_lse), channel_id=1, source_target_pairs={{0,16},{1,17},{2,18},{3,19},{4,20},{5,21},{6,22},{7,23},{8,24},{9,... | collective-permute-start | bytes 13832 | tf_op jit(solution)/shard_map/ppermute | solution.py:47
  61.1 8.4 %collective-permute-start.19 = (bf16[512,256]{1,0:T(8,128)(2,1)S(1)}, bf16[512,256]{1,0:T(8,128)(2,1)S(1)}, u32[]{:S(2)}, u32[]{:S(2)}) collective-permute-start(bf16[512,256]{1,0:T(8,128)(2,1)S(1)} %shard_map.90), channel_id=1, source_target_pairs={{0,16},{1,17},{2,18},{3,19},{4,20},{5,21},{6,22},{7,23},{8,24},{9,... | collective-permute-start | bytes 786440 | tf_op jit(solution)/shard_map/ppermute | solution.py:47
  69.5 3.4 %collective-permute-start.20 = (f32[256,256]{1,0:T(8,128)S(1)}, f32[256,256]{1,0:T(8,128)S(1)}, u32[]{:S(2)}, u32[]{:S(2)}) collective-permute-start(f32[256,256]{1,0:T(8,128)S(1)} %get-tuple-element.51), channel_id=1, source_target_pairs={{0,1},{1,0},{2,3},{3,2},{4,5},{5,4},{6,7},{7,6},{8,9},{9,8},{10,11... | collective-permute-start | bytes 786440 | tf_op jit(solution)/shard_map/ppermute | solution.py:47

commit v4 on v3

--- a/solution.py
+++ b/solution.py
@@ -19,7 +19,7 @@
 ARRIVAL = [(0, 0), (0, 1)]
 for hop in (1, 2, 3):
     ARRIVAL += [(-hop, 0), (hop, 0), (-hop, 1), (hop, 1)]
-ARRIVAL += [(-4, 0), (4, 1)]
+ARRIVAL += [(4, 0), (-4, 1)]
 CALLS = (10, 4, 2)
 
 
@@ -325,11 +325,12 @@
     for hop in range(3):
         ups.append([send(a, UP) for a in ups[-1]])
         downs.append([send(a, DOWN) for a in downs[-1]])
-    xs = [own, xb, send(xa, HALF), send(xb, HALF)]
+    xd, downs[1][0] = lax.optimization_barrier((xb, downs[1][0]))
+    xs = [own, xb, send(xa, HALF), send(xd, HALF)]
     ys = [own, yb]
     for hop in (1, 2, 3):
         ys += [ups[hop][0], downs[hop][0], ups[hop][1], downs[hop][1]]
-    ys += [send(ups[3][0], UP), send(downs[3][1], DOWN)]
+    ys += [send(downs[3][0], DOWN), send(ups[3][1], UP)]
     carry, biases, start = None, [], 0
     for i, count in enumerate(CALLS):
         carry, bias, *message = stats(i == 0, i == 2, xs, ys[start : start + count], carry)

time: 74.1 us -> 72.9 us (0.984)
  waiting for transfers between devices: 13.7 us -> 11.4 us
  starting transfers between devices: 42.3 us -> 43.4 us
    ppermute x21, waiting for transfers between devices: 7.51 us -> 5.24 us  [send(): return lax.ppermute(array, 'blk', pairs)]
    ppermute x21, starting transfers between devices: 31.8 us -> 33.2 us  [send(): return lax.ppermute(array, 'blk', pairs)]
  transfers between devices with their start and end apart: 22 -> 22, of which waited for: 6 -> 3; matrix products, arithmetic and copies ran while one was open for 0% -> 0% of each run, Pallas kernels for 11% -> 11%
where the time goes in v4:
time: 72.9 us; the launch traced here: 72.7 us
  starting transfers between devices  43.4 us (60%)
  Pallas kernels  15.6 us (21%)
  waiting for transfers between devices  11.4 us (16%)
  between operations  1.39 us (2%)
  local copies, waits for them, and re-layouts  0.96 us (1%)
    ppermute x21, starting transfers between devices, send(): return lax.ppermute(array, 'blk', pairs)  33.2 us
    pallas_call x9, Pallas kernels, call(): pl.pallas_call(kernel, out_shape=[jax.ShapeDtypeStruct(s, d) for s, d in...  15.6 us
    all_to_all x1, starting transfers between devices, local(): recv = lax.all_to_all(message[0], 'blk', 0, 0)  10.1 us
    all_to_all x1, waiting for transfers between devices, local(): recv = lax.all_to_all(message[0], 'blk', 0, 0)  6.17 us
    ppermute x21, waiting for transfers between devices, send(): return lax.ppermute(array, 'blk', pairs)  5.24 us
  transfers between devices with their start and end apart: 22, of which 3 were waited for; matrix products, arithmetic and copies ran while one was open for 0% of the time, Pallas kernels for 11%

profile of v4, /device:TPU:1, one launch (start us, length us, event | category | flops | bytes accessed | tf_op | source)
XLA Modules:
  0.0 72.7 jit_solution(5005386686628198848)
XLA Ops:
  1.3 2.0 %shard_map.84 = (bf16[512,256]{1,0:T(8,128)(2,1)}, bf16[256,256]{1,0:T(8,128)(2,1)}, bf16[256,256]{1,0:T(8,128)(2,1)}, bf16[256,256]{1,0:T(8,128)(2,1)}, bf16[256,256]{1,0:T(8,128)(2,1)}, /*index=5*/s32[8,256]{1,0:T(8,128)}) custom-call(s32[1]{0:T(128)S(6)} %copy.9.count_ref, s32[1,256]{1,0:T(1,128)} %refs_0_.1, s32[1,256]{1,0:T(1,128)} %refs_1_.1, ...), custom_call_target="tpu_custom_call" | custom-call | bytes 65536 | tf_op jit(solution)/shard_map/pallas_call | solution.py:280
  3.3 3.3 %collective-permute-start.4 = (bf16[256,256]{1,0:T(8,128)(2,1)}, bf16[256,256]{1,0:T(8,128)(2,1)S(1)}, u32[]{:S(2)}, u32[]{:S(2)}) collective-permute-start(bf16[256,256]{1,0:T(8,128)(2,1)} %get-tuple-element.38), channel_id=1, source_target_pairs={{0,1},{1,0},{2,3},{3,2},{4,5},{5,4},{6,7},{7,6},{8,9},{9,8},{10,11... | collective-permute-start | bytes 393224 | tf_op jit(solution)/shard_map/ppermute | solution.py:47
  6.7 3.9 %collective-permute-start.2 = (bf16[256,256]{1,0:T(8,128)(2,1)}, bf16[256,256]{1,0:T(8,128)(2,1)S(1)}, u32[]{:S(2)}, u32[]{:S(2)}) collective-permute-start(bf16[256,256]{1,0:T(8,128)(2,1)} %get-tuple-element.36), channel_id=1, source_target_pairs={{0,14},{1,15},{2,0},{3,1},{4,2},{5,3},{6,4},{7,5},{8,6},{9,7},{10,... | collective-permute-start | bytes 393224 | tf_op jit(solution)/shard_map/ppermute | solution.py:47
  10.5 0.0 collective-permute-done.4.refs_5_.refs_7_
  10.5 0.0 collective-permute-start.6
  10.5 0.4 collective-permute-start
  10.9 0.0 collective-permute-start.5
  10.9 3.0 %collective-permute-start.7 = (bf16[256,256]{1,0:T(8,128)(2,1)S(1)}, bf16[256,256]{1,0:T(8,128)(2,1)S(1)}, u32[]{:S(2)}, u32[]{:S(2)}) collective-permute-start(bf16[256,256]{1,0:T(8,128)(2,1)S(1)} %collective-permute-done.4.refs_5_.refs_7_), channel_id=1, source_target_pairs={{0,14},{1,15},{2,0},{3,1},{4,2},{5,3},{6,4},{7,5},{8,6},{9,7},{10,... | collective-permute-start | bytes 393224 | tf_op jit(solution)/shard_map/ppermute | solution.py:47
  13.8 0.0 collective-permute-done.2.refs_7_.refs_9_
  13.8 3.1 %collective-permute-start.9 = (bf16[256,256]{1,0:T(8,128)(2,1)S(1)}, bf16[256,256]{1,0:T(8,128)(2,1)S(1)}, u32[]{:S(2)}, u32[]{:S(2)}) collective-permute-start(bf16[256,256]{1,0:T(8,128)(2,1)S(1)} %collective-permute-done.2.refs_7_.refs_9_), channel_id=1, source_target_pairs={{0,14},{1,15},{2,0},{3,1},{4,2},{5,3},{6,4},{7,5},{8,6},{9,7},{10,... | collective-permute-start | bytes 393224 | tf_op jit(solution)/shard_map/ppermute | solution.py:47
  17.0 0.0 collective-permute-done.6.refs_8_.refs_10_
  17.0 0.0 collective-permute-start.10
  17.0 0.0 collective-permute-done.refs_1_.refs_5_
  17.0 2.8 %collective-permute-start.1 = (bf16[256,256]{1,0:T(8,128)(2,1)}, bf16[256,256]{1,0:T(8,128)(2,1)S(1)}, u32[]{:S(2)}, u32[]{:S(2)}) collective-permute-start(bf16[256,256]{1,0:T(8,128)(2,1)} %get-tuple-element.35), channel_id=1, source_target_pairs={{0,16},{1,17},{2,18},{3,19},{4,20},{5,21},{6,22},{7,23},{8,24},{9,... | collective-permute-start | bytes 393224 | tf_op jit(solution)/shard_map/ppermute | solution.py:47
  19.8 0.0 collective-permute-done.5.refs_6_.refs_8_
  19.8 0.0 collective-permute-start.8
  19.8 0.0 collective-permute-done.7.refs_9_.refs_11_
  19.8 2.7 %collective-permute-start.11 = (bf16[256,256]{1,0:T(8,128)(2,1)S(1)}, bf16[256,256]{1,0:T(8,128)(2,1)S(1)}, u32[]{:S(2)}, u32[]{:S(2)}) collective-permute-start(bf16[256,256]{1,0:T(8,128)(2,1)S(1)} %collective-permute-done.7.refs_9_.refs_11_), channel_id=1, source_target_pairs={{0,14},{1,15},{2,0},{3,1},{4,2},{5,3},{6,4},{7,5},{8,6},{9,7},{10,... | collective-permute-start | bytes 393224 | tf_op jit(solution)/shard_map/ppermute | solution.py:47
  22.5 0.0 collective-permute-done.9.refs_11_.refs_13_
  22.5 1.4 %collective-permute-start.13 = (bf16[256,256]{1,0:T(8,128)(2,1)S(1)}, bf16[256,256]{1,0:T(8,128)(2,1)S(1)}, u32[]{:S(2)}, u32[]{:S(2)}) collective-permute-start(bf16[256,256]{1,0:T(8,128)(2,1)S(1)} %collective-permute-done.9.refs_11_.refs_13_), channel_id=1, source_target_pairs={{0,14},{1,15},{2,0},{3,1},{4,2},{5,3},{6,4},{7,5},{8,6},{9,7},{10,... | collective-permute-start | bytes 393224 | tf_op jit(solution)/shard_map/ppermute | solution.py:47
  23.9 0.0 collective-permute-done.10.refs_12_.refs_14_
  23.9 0.1 collective-permute-start.14
  24.0 0.0 collective-permute-done.1.refs_2_.refs_4_
  24.0 2.2 %collective-permute-start.3 = (bf16[256,256]{1,0:T(8,128)(2,1)S(1)}, bf16[256,256]{1,0:T(8,128)(2,1)S(1)}, u32[]{:S(2)}, u32[]{:S(2)}) collective-permute-start(bf16[256,256]{1,0:T(8,128)(2,1)S(1)} %collective-permute-done.refs_1_.refs_5_), channel_id=1, source_target_pairs={{0,16},{1,17},{2,18},{3,19},{4,20},{5,21},{6,22},{7,23},{8,24},{9,... | collective-permute-start | bytes 393224 | tf_op jit(solution)/shard_map/ppermute | solution.py:47
  26.2 0.0 collective-permute-done.8.refs_10_.refs_12_
  26.2 0.1 collective-permute-start.12
  26.3 0.0 collective-permute-done.11.refs_13_.refs_15_
  26.3 2.6 %collective-permute-start.15 = (bf16[256,256]{1,0:T(8,128)(2,1)S(1)}, bf16[256,256]{1,0:T(8,128)(2,1)S(1)}, u32[]{:S(2)}, u32[]{:S(2)}) collective-permute-start(bf16[256,256]{1,0:T(8,128)(2,1)S(1)} %collective-permute-done.11.refs_13_.refs_15_), channel_id=1, source_target_pairs={{0,14},{1,15},{2,0},{3,1},{4,2},{5,3},{6,4},{7,5},{8,6},{9,7},{10,... | collective-permute-start | bytes 393224 | tf_op jit(solution)/shard_map/ppermute | solution.py:47
  28.9 0.0 collective-permute-done.13.refs_6_.refs_17_
  28.9 0.7 collective-permute-start.16
  29.5 0.0 collective-permute-done.14.refs_7_.refs_18_
  29.5 0.8 %collective-permute-start.17 = (bf16[256,256]{1,0:T(8,128)(2,1)S(1)}, bf16[256,256]{1,0:T(8,128)(2,1)S(1)}, u32[]{:S(2)}, u32[]{:S(2)}) collective-permute-start(bf16[256,256]{1,0:T(8,128)(2,1)S(1)} %collective-permute-done.14.refs_7_.refs_18_), channel_id=1, source_target_pairs={{0,2},{1,3},{2,4},{3,5},{4,6},{5,7},{6,8},{7,9},{8,10},{9,11},{10,... | collective-permute-start | bytes 393224 | tf_op jit(solution)/shard_map/ppermute | solution.py:47
  30.3 0.0 collective-permute-done.3.refs_3_.refs_5_
  30.3 0.0 copy-start
  30.3 0.9 %copy-done = bf16[512,256]{1,0:T(8,128)(2,1)S(1)} copy-done((bf16[512,256]{1,0:T(8,128)(2,1)S(1)}, bf16[512,256]{1,0:T(8,128)(2,1)}, u32[]{:S(2)}) %copy-start) | copy-done | bytes 262168
  31.3 3.1 %shard_map.85 = (f32[8,1024]{1,0:T(8,128)S(1)}, f32[1,2560]{1,0:T(1,128)S(1)}) custom-call(bf16[512,256]{1,0:T(8,128)(2,1)S(1)} %copy-done, bf16[256,256]{1,0:T(8,128)(2,1)S(1)} %collective-permute-done.refs_1_.refs_5_, bf16[256,256]{1,0:T(8,128)(2,1)S(1)} %collective-permute-done.1.refs_2_.refs_4_, ...), custom_call_target="tpu_custom_call" | custom-call | bytes 65536 | tf_op jit(solution)/shard_map/pallas_call | solution.py:280
  34.4 0.0 collective-permute-done.12.refs_5_.refs_16_
  34.4 0.0 collective-permute-done.15.refs_8_.refs_19_
  34.5 1.4 %shard_map.86 = (f32[8,1024]{1,0:T(8,128)S(1)}, f32[1,1024]{1,0:T(1,128)S(1)}) custom-call(bf16[512,256]{1,0:T(8,128)(2,1)S(1)} %copy-done, bf16[256,256]{1,0:T(8,128)(2,1)S(1)} %collective-permute-done.refs_1_.refs_5_, bf16[256,256]{1,0:T(8,128)(2,1)S(1)} %collective-permute-done.1.refs_2_.refs_4_, ...), custom_call_target="tpu_custom_call" | custom-call | bytes 65536 | tf_op jit(solution)/shard_map/pallas_call | solution.py:280
  35.8 0.0 collective-permute-done.16.refs_5_.refs_20_
  35.8 0.0 collective-permute-done.17.refs_6_.refs_21_
  35.8 0.0 copy-start.1
  35.9 0.0 copy-start.3
  35.9 1.5 %shard_map.87 = (f32[1,1152]{1,0:T(1,128)S(1)}, f32[1,512]{1,0:T(1,128)S(1)}, f32[32,1,512]{2,1,0:T(1,128)}) custom-call(bf16[512,256]{1,0:T(8,128)(2,1)S(1)} %copy-done, bf16[256,256]{1,0:T(8,128)(2,1)S(1)} %collective-permute-done.refs_1_.refs_5_, bf16[256,256]{1,0:T(8,128)(2,1)S(1)} %collective-permute-done.1.refs_2_.refs_4_, ...), custom_call_target="tpu_custom_call" | custom-call | bytes 65536 | tf_op jit(solution)/shard_map/pallas_call | solution.py:280
  37.3 0.0 copy-start.2
  37.3 10.1 %all-to-all-start = ((f32[32,1,512]{2,1,0:T(1,128)}), f32[32,1,512]{2,1,0:T(1,128)S(1)}, u32[]{:S(2)}, u32[]{:S(2)}) async-start(f32[32,1,512]{2,1,0:T(1,128)} %get-tuple-element.43), calls=%async_computation | async-start | bytes 131072 | tf_op jit(solution)/shard_map/all_to_all | solution.py:339
  47.5 3.0 %collective-permute-start.18 = (f32[1,1152]{1,0:T(1,128)S(1)}, f32[1,1152]{1,0:T(1,128)S(1)}, u32[]{:S(2)}, u32[]{:S(2)}) collective-permute-start(f32[1,1152]{1,0:T(1,128)S(1)} %get-tuple-element.42.refs_1_.own_lse), channel_id=1, source_target_pairs={{0,16},{1,17},{2,18},{3,19},{4,20},{5,21},{6,22},{7,23},{8,24},{9,... | collective-permute-start | bytes 13832 | tf_op jit(solution)/shard_map/ppermute | solution.py:47
  50.5 0.0 copy-done.1
  50.5 0.0 copy-done.3
  50.5 0.0 copy-done.2
  50.5 0.4 shard_map.88
  50.9 6.2 %all-to-all-done.refs_0_ = f32[32,1,512]{2,1,0:T(1,128)S(1)} async-done(((f32[32,1,512]{2,1,0:T(1,128)}), f32[32,1,512]{2,1,0:T(1,128)S(1)}, u32[]{:S(2)}, u32[]{:S(2)}) %all-to-all-start) | async-done | bytes 65568 | tf_op jit(solution)/shard_map/all_to_all | solution.py:339
  57.1 0.0 collective-permute-done.18.refs_2_.other_lse
  57.1 2.8 %shard_map.90 = bf16[512,256]{1,0:T(8,128)(2,1)S(1)} custom-call(f32[32,1,512]{2,1,0:T(1,128)S(1)} %all-to-all-done.refs_0_, f32[1,1152]{1,0:T(1,128)S(1)} %get-tuple-element.42.refs_1_.own_lse, f32[1,1152]{1,0:T(1,128)S(1)} %collective-permute-done.18.refs_2_.other_lse, s32[8,256]{1,0:T(8,128)S(1)} %copy-done.2, ...), custom_call_target="tpu_custom_call" | custom-call | bytes 65536 | tf_op jit(solution)/shard_map/pallas_call | solution.py:280
  59.8 1.0 %collective-permute-start.19 = (bf16[512,256]{1,0:T(8,128)(2,1)S(1)}, bf16[512,256]{1,0:T(8,128)(2,1)S(1)}, u32[]{:S(2)}, u32[]{:S(2)}) collective-permute-start(bf16[512,256]{1,0:T(8,128)(2,1)S(1)} %shard_map.90), channel_id=1, source_target_pairs={{0,16},{1,17},{2,18},{3,19},{4,20},{5,21},{6,22},{7,23},{8,24},{9,... | collective-permute-start | bytes 786440 | tf_op jit(solution)/shard_map/ppermute | solution.py:47
  60.9 3.3 %shard_map.89 = (f32[256,256]{1,0:T(8,128)S(1)}, f32[256,256]{1,0:T(8,128)S(1)}, f32[1,256]{1,0:T(1,128)}, f32[1,256]{1,0:T(1,128)}) custom-call(f32[32,1,512]{2,1,0:T(1,128)S(1)} %all-to-all-done.refs_0_, f32[1,1152]{1,0:T(1,128)S(1)} %get-tuple-element.42.refs_1_.own_lse, f32[1,1152]{1,0:T(1,128)S(1)} %collective-permute-done.18.refs_2_.other_lse, ...), custom_call_target="tpu_custom_call" | custom-call | bytes 65536 | tf_op jit(solution)/shard_map/pallas_call | solution.py:280
  64.2 4.0 %collective-permute-done.19.away_ref = bf16[512,256]{1,0:T(8,128)(2,1)S(1)} collective-permute-done((bf16[512,256]{1,0:T(8,128)(2,1)S(1)}, bf16[512,256]{1,0:T(8,128)(2,1)S(1)}, u32[]{:S(2)}, u32[]{:S(2)}) %collective-permute-start.19) | collective-permute-done | bytes 262176 | tf_op jit(solution)/shard_map/ppermute | solution.py:47
  68.2 0.1 shard_map.91
  68.3 2.3 %collective-permute-start.20 = (f32[256,256]{1,0:T(8,128)S(1)}, f32[256,256]{1,0:T(8,128)S(1)}, u32[]{:S(2)}, u32[]{:S(2)}) collective-permute-start(f32[256,256]{1,0:T(8,128)S(1)} %get-tuple-element.55), channel_id=1, source_target_pairs={{0,1},{1,0},{2,3},{3,2},{4,5},{5,4},{6,7},{7,6},{8,9},{9,8},{10,11... | collective-permute-start | bytes 786440 | tf_op jit(solution)/shard_map/ppermute | solution.py:47
  70.5 1.2 %collective-permute-done.20.dy_ref = f32[256,256]{1,0:T(8,128)S(1)} collective-permute-done((f32[256,256]{1,0:T(8,128)S(1)}, f32[256,256]{1,0:T(8,128)S(1)}, u32[]{:S(2)}, u32[]{:S(2)}) %collective-permute-start.20) | collective-permute-done | bytes 262176 | tf_op jit(solution)/shard_map/ppermute | solution.py:47
  71.7 1.0 %shard_map.92 = (f32[256,256]{1,0:T(8,128)}, f32[256,256]{1,0:T(8,128)}) custom-call(s32[1]{0:T(128)S(6)} %copy.9.count_ref, s32[8,256]{1,0:T(8,128)S(1)} %copy-done.2, f32[1,1152]{1,0:T(1,128)S(1)} %get-tuple-element.42.refs_1_.own_lse, f32[1,1152]{1,0:T(1,128)S(1)} %collective-permute-done.18.refs_2_.other_lse, f32[256,256]{1,0:T(8,128)S(1)} %get-tuple-element.46.px_ref, ...), custom_call_target="tpu_custom_call" | custom-call | bytes 65536 | tf_op jit(solution)/shard_map/pallas_call | solution.py:280
Async XLA Ops:
  3.3 7.2 %collective-permute-start.4 = (bf16[256,256]{1,0:T(8,128)(2,1)}, bf16[256,256]{1,0:T(8,128)(2,1)S(1)}, u32[]{:S(2)}, u32[]{:S(2)}) collective-permute-start(bf16[256,256]{1,0:T(8,128)(2,1)} %get-tuple-element.38), channel_id=1, source_target_pairs={{0,1},{1,0},{2,3},{3,2},{4,5},{5,4},{6,7},{7,6},{8,9},{9,8},{10,11... | collective-permute-start | bytes 393224 | tf_op jit(solution)/shard_map/ppermute | solution.py:47
  6.7 7.2 %collective-permute-start.2 = (bf16[256,256]{1,0:T(8,128)(2,1)}, bf16[256,256]{1,0:T(8,128)(2,1)S(1)}, u32[]{:S(2)}, u32[]{:S(2)}) collective-permute-start(bf16[256,256]{1,0:T(8,128)(2,1)} %get-tuple-element.36), channel_id=1, source_target_pairs={{0,14},{1,15},{2,0},{3,1},{4,2},{5,3},{6,4},{7,5},{8,6},{9,7},{10,... | collective-permute-start | bytes 393224 | tf_op jit(solution)/shard_map/ppermute | solution.py:47
  10.5 6.5 %collective-permute-start.6 = (bf16[256,256]{1,0:T(8,128)(2,1)S(1)}, bf16[256,256]{1,0:T(8,128)(2,1)S(1)}, u32[]{:S(2)}, u32[]{:S(2)}) collective-permute-start(bf16[256,256]{1,0:T(8,128)(2,1)S(1)} %collective-permute-done.4.refs_5_.refs_7_), channel_id=1, source_target_pairs={{0,2},{1,3},{2,4},{3,5},{4,6},{5,7},{6,8},{7,9},{8,10},{9,11},{10,... | collective-permute-start | bytes 393224 | tf_op jit(solution)/shard_map/ppermute | solution.py:47
  10.5 6.5 %collective-permute-start = (bf16[256,256]{1,0:T(8,128)(2,1)}, bf16[256,256]{1,0:T(8,128)(2,1)S(1)}, u32[]{:S(2)}, u32[]{:S(2)}) collective-permute-start(bf16[256,256]{1,0:T(8,128)(2,1)} %get-tuple-element.34.fy_ref), channel_id=1, source_target_pairs={{0,1},{1,0},{2,3},{3,2},{4,5},{5,4},{6,7},{7,6},{8,9},{9,8},{10,11... | collective-permute-start | bytes 393224 | tf_op jit(solution)/shard_map/ppermute | solution.py:47
  10.9 9.0 %collective-permute-start.5 = (bf16[256,256]{1,0:T(8,128)(2,1)}, bf16[256,256]{1,0:T(8,128)(2,1)S(1)}, u32[]{:S(2)}, u32[]{:S(2)}) collective-permute-start(bf16[256,256]{1,0:T(8,128)(2,1)} %get-tuple-element.36), channel_id=1, source_target_pairs={{0,2},{1,3},{2,4},{3,5},{4,6},{5,7},{6,8},{7,9},{8,10},{9,11},{10,... | collective-permute-start | bytes 393224 | tf_op jit(solution)/shard_map/ppermute | solution.py:47
  10.9 9.0 %collective-permute-start.7 = (bf16[256,256]{1,0:T(8,128)(2,1)S(1)}, bf16[256,256]{1,0:T(8,128)(2,1)S(1)}, u32[]{:S(2)}, u32[]{:S(2)}) collective-permute-start(bf16[256,256]{1,0:T(8,128)(2,1)S(1)} %collective-permute-done.4.refs_5_.refs_7_), channel_id=1, source_target_pairs={{0,14},{1,15},{2,0},{3,1},{4,2},{5,3},{6,4},{7,5},{8,6},{9,7},{10,... | collective-permute-start | bytes 393224 | tf_op jit(solution)/shard_map/ppermute | solution.py:47
  13.8 8.7 %collective-permute-start.9 = (bf16[256,256]{1,0:T(8,128)(2,1)S(1)}, bf16[256,256]{1,0:T(8,128)(2,1)S(1)}, u32[]{:S(2)}, u32[]{:S(2)}) collective-permute-start(bf16[256,256]{1,0:T(8,128)(2,1)S(1)} %collective-permute-done.2.refs_7_.refs_9_), channel_id=1, source_target_pairs={{0,14},{1,15},{2,0},{3,1},{4,2},{5,3},{6,4},{7,5},{8,6},{9,7},{10,... | collective-permute-start | bytes 393224 | tf_op jit(solution)/shard_map/ppermute | solution.py:47
  17.0 6.9 %collective-permute-start.10 = (bf16[256,256]{1,0:T(8,128)(2,1)S(1)}, bf16[256,256]{1,0:T(8,128)(2,1)S(1)}, u32[]{:S(2)}, u32[]{:S(2)}) collective-permute-start(bf16[256,256]{1,0:T(8,128)(2,1)S(1)} %collective-permute-done.6.refs_8_.refs_10_), channel_id=1, source_target_pairs={{0,2},{1,3},{2,4},{3,5},{4,6},{5,7},{6,8},{7,9},{8,10},{9,11},{10,... | collective-permute-start | bytes 393224 | tf_op jit(solution)/shard_map/ppermute | solution.py:47
  17.0 7.0 %collective-permute-start.1 = (bf16[256,256]{1,0:T(8,128)(2,1)}, bf16[256,256]{1,0:T(8,128)(2,1)S(1)}, u32[]{:S(2)}, u32[]{:S(2)}) collective-permute-start(bf16[256,256]{1,0:T(8,128)(2,1)} %get-tuple-element.35), channel_id=1, source_target_pairs={{0,16},{1,17},{2,18},{3,19},{4,20},{5,21},{6,22},{7,23},{8,24},{9,... | collective-permute-start | bytes 393224 | tf_op jit(solution)/shard_map/ppermute | solution.py:47
  19.8 6.3 %collective-permute-start.8 = (bf16[256,256]{1,0:T(8,128)(2,1)S(1)}, bf16[256,256]{1,0:T(8,128)(2,1)S(1)}, u32[]{:S(2)}, u32[]{:S(2)}) collective-permute-start(bf16[256,256]{1,0:T(8,128)(2,1)S(1)} %collective-permute-done.5.refs_6_.refs_8_), channel_id=1, source_target_pairs={{0,2},{1,3},{2,4},{3,5},{4,6},{5,7},{6,8},{7,9},{8,10},{9,11},{10,... | collective-permute-start | bytes 393224 | tf_op jit(solution)/shard_map/ppermute | solution.py:47
  19.8 6.4 %collective-permute-start.11 = (bf16[256,256]{1,0:T(8,128)(2,1)S(1)}, bf16[256,256]{1,0:T(8,128)(2,1)S(1)}, u32[]{:S(2)}, u32[]{:S(2)}) collective-permute-start(bf16[256,256]{1,0:T(8,128)(2,1)S(1)} %collective-permute-done.7.refs_9_.refs_11_), channel_id=1, source_target_pairs={{0,14},{1,15},{2,0},{3,1},{4,2},{5,3},{6,4},{7,5},{8,6},{9,7},{10,... | collective-permute-start | bytes 393224 | tf_op jit(solution)/shard_map/ppermute | solution.py:47
  22.5 6.3 %collective-permute-start.13 = (bf16[256,256]{1,0:T(8,128)(2,1)S(1)}, bf16[256,256]{1,0:T(8,128)(2,1)S(1)}, u32[]{:S(2)}, u32[]{:S(2)}) collective-permute-start(bf16[256,256]{1,0:T(8,128)(2,1)S(1)} %collective-permute-done.9.refs_11_.refs_13_), channel_id=1, source_target_pairs={{0,14},{1,15},{2,0},{3,1},{4,2},{5,3},{6,4},{7,5},{8,6},{9,7},{10,... | collective-permute-start | bytes 393224 | tf_op jit(solution)/shard_map/ppermute | solution.py:47
  23.9 5.6 %collective-permute-start.14 = (bf16[256,256]{1,0:T(8,128)(2,1)S(1)}, bf16[256,256]{1,0:T(8,128)(2,1)S(1)}, u32[]{:S(2)}, u32[]{:S(2)}) collective-permute-start(bf16[256,256]{1,0:T(8,128)(2,1)S(1)} %collective-permute-done.10.refs_12_.refs_14_), channel_id=1, source_target_pairs={{0,2},{1,3},{2,4},{3,5},{4,6},{5,7},{6,8},{7,9},{8,10},{9,11},{10,... | collective-permute-start | bytes 393224 | tf_op jit(solution)/shard_map/ppermute | solution.py:47
  24.0 6.3 %collective-permute-start.3 = (bf16[256,256]{1,0:T(8,128)(2,1)S(1)}, bf16[256,256]{1,0:T(8,128)(2,1)S(1)}, u32[]{:S(2)}, u32[]{:S(2)}) collective-permute-start(bf16[256,256]{1,0:T(8,128)(2,1)S(1)} %collective-permute-done.refs_1_.refs_5_), channel_id=1, source_target_pairs={{0,16},{1,17},{2,18},{3,19},{4,20},{5,21},{6,22},{7,23},{8,24},{9,... | collective-permute-start | bytes 393224 | tf_op jit(solution)/shard_map/ppermute | solution.py:47
  26.2 8.3 %collective-permute-start.12 = (bf16[256,256]{1,0:T(8,128)(2,1)S(1)}, bf16[256,256]{1,0:T(8,128)(2,1)S(1)}, u32[]{:S(2)}, u32[]{:S(2)}) collective-permute-start(bf16[256,256]{1,0:T(8,128)(2,1)S(1)} %collective-permute-done.8.refs_10_.refs_12_), channel_id=1, source_target_pairs={{0,2},{1,3},{2,4},{3,5},{4,6},{5,7},{6,8},{7,9},{8,10},{9,11},{10,... | collective-permute-start | bytes 393224 | tf_op jit(solution)/shard_map/ppermute | solution.py:47
  26.3 8.2 %collective-permute-start.15 = (bf16[256,256]{1,0:T(8,128)(2,1)S(1)}, bf16[256,256]{1,0:T(8,128)(2,1)S(1)}, u32[]{:S(2)}, u32[]{:S(2)}) collective-permute-start(bf16[256,256]{1,0:T(8,128)(2,1)S(1)} %collective-permute-done.11.refs_13_.refs_15_), channel_id=1, source_target_pairs={{0,14},{1,15},{2,0},{3,1},{4,2},{5,3},{6,4},{7,5},{8,6},{9,7},{10,... | collective-permute-start | bytes 393224 | tf_op jit(solution)/shard_map/ppermute | solution.py:47
  28.9 7.0 %collective-permute-start.16 = (bf16[256,256]{1,0:T(8,128)(2,1)S(1)}, bf16[256,256]{1,0:T(8,128)(2,1)S(1)}, u32[]{:S(2)}, u32[]{:S(2)}) collective-permute-start(bf16[256,256]{1,0:T(8,128)(2,1)S(1)} %collective-permute-done.13.refs_6_.refs_17_), channel_id=1, source_target_pairs={{0,14},{1,15},{2,0},{3,1},{4,2},{5,3},{6,4},{7,5},{8,6},{9,7},{10,... | collective-permute-start | bytes 393224 | tf_op jit(solution)/shard_map/ppermute | solution.py:47
  29.5 6.3 %collective-permute-start.17 = (bf16[256,256]{1,0:T(8,128)(2,1)S(1)}, bf16[256,256]{1,0:T(8,128)(2,1)S(1)}, u32[]{:S(2)}, u32[]{:S(2)}) collective-permute-start(bf16[256,256]{1,0:T(8,128)(2,1)S(1)} %collective-permute-done.14.refs_7_.refs_18_), channel_id=1, source_target_pairs={{0,2},{1,3},{2,4},{3,5},{4,6},{5,7},{6,8},{7,9},{8,10},{9,11},{10,... | collective-permute-start | bytes 393224 | tf_op jit(solution)/shard_map/ppermute | solution.py:47
  30.3 1.0 %copy-start = (bf16[512,256]{1,0:T(8,128)(2,1)S(1)}, bf16[512,256]{1,0:T(8,128)(2,1)}, u32[]{:S(2)}) copy-start(bf16[512,256]{1,0:T(8,128)(2,1)} %get-tuple-element.33.refs_0_.refs_4_.fx_ref.refs_6_) | copy-start | bytes 786436
  35.8 14.6 %copy-start.1 = (bf16[512,256]{1,0:T(8,128)(2,1)S(1)}, bf16[512,256]{1,0:T(8,128)(2,1)}, u32[]{:S(2)}) copy-start(bf16[512,256]{1,0:T(8,128)(2,1)} %get-tuple-element.33.refs_0_.refs_4_.fx_ref.refs_6_) | copy-start | bytes 786436
  35.9 14.6 %copy-start.3 = (bf16[256,256]{1,0:T(8,128)(2,1)S(1)}, bf16[256,256]{1,0:T(8,128)(2,1)}, u32[]{:S(2)}) copy-start(bf16[256,256]{1,0:T(8,128)(2,1)} %get-tuple-element.34.fy_ref) | copy-start | bytes 393220
  37.3 13.1 %copy-start.2 = (s32[8,256]{1,0:T(8,128)S(1)}, s32[8,256]{1,0:T(8,128)}, u32[]{:S(2)}) copy-start(s32[8,256]{1,0:T(8,128)} %get-tuple-element.32.match_ref.refs_3_) | copy-start | bytes 24580
  37.3 19.7 %all-to-all-start = ((f32[32,1,512]{2,1,0:T(1,128)}), f32[32,1,512]{2,1,0:T(1,128)S(1)}, u32[]{:S(2)}, u32[]{:S(2)}) async-start(f32[32,1,512]{2,1,0:T(1,128)} %get-tuple-element.43), calls=%async_computation | async-start | bytes 131072 | tf_op jit(solution)/shard_map/all_to_all | solution.py:339
  47.5 9.6 %collective-permute-start.18 = (f32[1,1152]{1,0:T(1,128)S(1)}, f32[1,1152]{1,0:T(1,128)S(1)}, u32[]{:S(2)}, u32[]{:S(2)}) collective-permute-start(f32[1,1152]{1,0:T(1,128)S(1)} %get-tuple-element.42.refs_1_.own_lse), channel_id=1, source_target_pairs={{0,16},{1,17},{2,18},{3,19},{4,20},{5,21},{6,22},{7,23},{8,24},{9,... | collective-permute-start | bytes 13832 | tf_op jit(solution)/shard_map/ppermute | solution.py:47
  59.8 8.4 %collective-permute-start.19 = (bf16[512,256]{1,0:T(8,128)(2,1)S(1)}, bf16[512,256]{1,0:T(8,128)(2,1)S(1)}, u32[]{:S(2)}, u32[]{:S(2)}) collective-permute-start(bf16[512,256]{1,0:T(8,128)(2,1)S(1)} %shard_map.90), channel_id=1, source_target_pairs={{0,16},{1,17},{2,18},{3,19},{4,20},{5,21},{6,22},{7,23},{8,24},{9,... | collective-permute-start | bytes 786440 | tf_op jit(solution)/shard_map/ppermute | solution.py:47
  68.3 3.4 %collective-permute-start.20 = (f32[256,256]{1,0:T(8,128)S(1)}, f32[256,256]{1,0:T(8,128)S(1)}, u32[]{:S(2)}, u32[]{:S(2)}) collective-permute-start(f32[256,256]{1,0:T(8,128)S(1)} %get-tuple-element.55), channel_id=1, source_target_pairs={{0,1},{1,0},{2,3},{3,2},{4,5},{5,4},{6,7},{7,6},{8,9},{9,8},{10,11... | collective-permute-start | bytes 786440 | tf_op jit(solution)/shard_map/ppermute | solution.py:47

commit v5 on v4

--- a/solution.py
+++ b/solution.py
@@ -88,33 +88,32 @@
     return ref[ref.shape[0] - N :, :]
 
 
-def fetch(hbm, held, sems):
+def pack_kernel(count_ref, *refs):
+    hbm, outs, held, sems = refs[:4], refs[4:10], refs[10:14], refs[14]
+    own_ref, x_ref, y_ref, give_x, give_y, match_ref = outs
     copies = [
         pltpu.make_async_copy(src, dst, sems.at[i]) for i, (src, dst) in enumerate(zip(hbm, held))
     ]
     for copy in copies:
         copy.start()
-    for copy in copies:
-        copy.wait()
-
-
-def pack_kernel(count_ref, *refs):
-    hbm, outs, held, sems = refs[:4], refs[4:10], refs[10:14], refs[14]
-    own_ref, x_ref, y_ref, give_x, give_y, match_ref = outs
-    fetch(hbm, held, sems)
     m1, m2, f1, f2 = held
-
-    def masked(m_ref, f_ref):
-        live = live_column(onehot(m_ref[...]), count_ref[0])
+    copies[0].wait()
+    copies[1].wait()
+    live1 = live_column(onehot(m1[...]), count_ref[0])
+    live2 = live_column(onehot(m2[...]), count_ref[0])
+    copies[2].wait()
+    copies[3].wait()
+
+    def masked(live, f_ref):
         return jnp.where(live, f_ref[...].astype(F32), MARK).astype(BF)
 
-    def write(mx, fx, my, fy):
-        y = masked(my, fy)
+    def write(mx, lx, fx, my, ly, fy):
+        y = masked(ly, fy)
         y_ref[...] = y
         own_ref[N:, :] = y
         own_ref[:N, :] = fx[...]
         x_ref[...] = fx[...]
-        give_x[...] = masked(mx, fx)
+        give_x[...] = masked(lx, fx)
         give_y[...] = fy[...]
         match_ref[...] = jnp.concatenate([mx[...], my[...], jnp.zeros((6, N), jnp.int32)], axis=0)
 
@@ -122,11 +121,11 @@
 
     @pl.when(role == 0)
     def _():
-        write(m1, f1, m2, f2)
+        write(m1, live1, f1, m2, live2, f2)
 
     @pl.when(role != 0)
     def _():
-        write(m2, f2, m1, f1)
+        write(m2, live2, f2, m1, live1, f1)
 
 
 def stats_kernel(first, last, *refs):

time: 72.9 us -> 72.8 us (level)
  no operation moved by 1% of the time
where the time goes in v5:
time: 72.8 us; the launch traced here: 72.6 us
  starting transfers between devices  43.4 us (60%)
  Pallas kernels  15.5 us (21%)
  waiting for transfers between devices  11.4 us (16%)
  between operations  1.39 us (2%)
  local copies, waits for them, and re-layouts  0.96 us (1%)
    ppermute x21, starting transfers between devices, send(): return lax.ppermute(array, 'blk', pairs)  33.2 us
    pallas_call x9, Pallas kernels, call(): pl.pallas_call(kernel, out_shape=[jax.ShapeDtypeStruct(s, d) for s, d in...  15.5 us
    all_to_all x1, starting transfers between devices, local(): recv = lax.all_to_all(message[0], 'blk', 0, 0)  10.1 us
    all_to_all x1, waiting for transfers between devices, local(): recv = lax.all_to_all(message[0], 'blk', 0, 0)  6.17 us
    ppermute x21, waiting for transfers between devices, send(): return lax.ppermute(array, 'blk', pairs)  5.24 us
  transfers between devices with their start and end apart: 22, of which 3 were waited for; matrix products, arithmetic and copies ran while one was open for 0% of the time, Pallas kernels for 11%

profile of v5, /device:TPU:1, one launch (start us, length us, event | category | flops | bytes accessed | tf_op | source)
XLA Modules:
  0.0 72.6 jit_solution(5925277840783764186)
XLA Ops:
  1.3 2.0 %shard_map.84 = (bf16[512,256]{1,0:T(8,128)(2,1)}, bf16[256,256]{1,0:T(8,128)(2,1)}, bf16[256,256]{1,0:T(8,128)(2,1)}, bf16[256,256]{1,0:T(8,128)(2,1)}, bf16[256,256]{1,0:T(8,128)(2,1)}, /*index=5*/s32[8,256]{1,0:T(8,128)}) custom-call(s32[1]{0:T(128)S(6)} %copy.9.count_ref, s32[1,256]{1,0:T(1,128)} %refs_0_.1, s32[1,256]{1,0:T(1,128)} %refs_1_.1, ...), custom_call_target="tpu_custom_call" | custom-call | bytes 65536 | tf_op jit(solution)/shard_map/pallas_call | solution.py:279
  3.3 3.3 %collective-permute-start.4 = (bf16[256,256]{1,0:T(8,128)(2,1)}, bf16[256,256]{1,0:T(8,128)(2,1)S(1)}, u32[]{:S(2)}, u32[]{:S(2)}) collective-permute-start(bf16[256,256]{1,0:T(8,128)(2,1)} %get-tuple-element.38), channel_id=1, source_target_pairs={{0,1},{1,0},{2,3},{3,2},{4,5},{5,4},{6,7},{7,6},{8,9},{9,8},{10,11... | collective-permute-start | bytes 393224 | tf_op jit(solution)/shard_map/ppermute | solution.py:47
  6.6 3.9 %collective-permute-start.2 = (bf16[256,256]{1,0:T(8,128)(2,1)}, bf16[256,256]{1,0:T(8,128)(2,1)S(1)}, u32[]{:S(2)}, u32[]{:S(2)}) collective-permute-start(bf16[256,256]{1,0:T(8,128)(2,1)} %get-tuple-element.36), channel_id=1, source_target_pairs={{0,14},{1,15},{2,0},{3,1},{4,2},{5,3},{6,4},{7,5},{8,6},{9,7},{10,... | collective-permute-start | bytes 393224 | tf_op jit(solution)/shard_map/ppermute | solution.py:47
  10.5 0.0 collective-permute-done.4.refs_5_.refs_7_
  10.5 0.0 collective-permute-start.6
  10.5 0.4 collective-permute-start
  10.8 0.0 collective-permute-start.5
  10.8 3.0 %collective-permute-start.7 = (bf16[256,256]{1,0:T(8,128)(2,1)S(1)}, bf16[256,256]{1,0:T(8,128)(2,1)S(1)}, u32[]{:S(2)}, u32[]{:S(2)}) collective-permute-start(bf16[256,256]{1,0:T(8,128)(2,1)S(1)} %collective-permute-done.4.refs_5_.refs_7_), channel_id=1, source_target_pairs={{0,14},{1,15},{2,0},{3,1},{4,2},{5,3},{6,4},{7,5},{8,6},{9,7},{10,... | collective-permute-start | bytes 393224 | tf_op jit(solution)/shard_map/ppermute | solution.py:47
  13.8 0.0 collective-permute-done.2.refs_7_.refs_9_
  13.8 3.1 %collective-permute-start.9 = (bf16[256,256]{1,0:T(8,128)(2,1)S(1)}, bf16[256,256]{1,0:T(8,128)(2,1)S(1)}, u32[]{:S(2)}, u32[]{:S(2)}) collective-permute-start(bf16[256,256]{1,0:T(8,128)(2,1)S(1)} %collective-permute-done.2.refs_7_.refs_9_), channel_id=1, source_target_pairs={{0,14},{1,15},{2,0},{3,1},{4,2},{5,3},{6,4},{7,5},{8,6},{9,7},{10,... | collective-permute-start | bytes 393224 | tf_op jit(solution)/shard_map/ppermute | solution.py:47
  16.9 0.0 collective-permute-done.6.refs_8_.refs_10_
  16.9 0.0 collective-permute-start.10
  16.9 0.0 collective-permute-done.refs_1_.refs_5_
  16.9 2.8 %collective-permute-start.1 = (bf16[256,256]{1,0:T(8,128)(2,1)}, bf16[256,256]{1,0:T(8,128)(2,1)S(1)}, u32[]{:S(2)}, u32[]{:S(2)}) collective-permute-start(bf16[256,256]{1,0:T(8,128)(2,1)} %get-tuple-element.35), channel_id=1, source_target_pairs={{0,16},{1,17},{2,18},{3,19},{4,20},{5,21},{6,22},{7,23},{8,24},{9,... | collective-permute-start | bytes 393224 | tf_op jit(solution)/shard_map/ppermute | solution.py:47
  19.8 0.0 collective-permute-done.5.refs_6_.refs_8_
  19.8 0.0 collective-permute-start.8
  19.8 0.0 collective-permute-done.7.refs_9_.refs_11_
  19.8 2.7 %collective-permute-start.11 = (bf16[256,256]{1,0:T(8,128)(2,1)S(1)}, bf16[256,256]{1,0:T(8,128)(2,1)S(1)}, u32[]{:S(2)}, u32[]{:S(2)}) collective-permute-start(bf16[256,256]{1,0:T(8,128)(2,1)S(1)} %collective-permute-done.7.refs_9_.refs_11_), channel_id=1, source_target_pairs={{0,14},{1,15},{2,0},{3,1},{4,2},{5,3},{6,4},{7,5},{8,6},{9,7},{10,... | collective-permute-start | bytes 393224 | tf_op jit(solution)/shard_map/ppermute | solution.py:47
  22.4 0.0 collective-permute-done.9.refs_11_.refs_13_
  22.4 1.4 %collective-permute-start.13 = (bf16[256,256]{1,0:T(8,128)(2,1)S(1)}, bf16[256,256]{1,0:T(8,128)(2,1)S(1)}, u32[]{:S(2)}, u32[]{:S(2)}) collective-permute-start(bf16[256,256]{1,0:T(8,128)(2,1)S(1)} %collective-permute-done.9.refs_11_.refs_13_), channel_id=1, source_target_pairs={{0,14},{1,15},{2,0},{3,1},{4,2},{5,3},{6,4},{7,5},{8,6},{9,7},{10,... | collective-permute-start | bytes 393224 | tf_op jit(solution)/shard_map/ppermute | solution.py:47
  23.8 0.0 collective-permute-done.10.refs_12_.refs_14_
  23.8 0.1 collective-permute-start.14
  23.9 0.0 collective-permute-done.1.refs_2_.refs_4_
  23.9 2.2 %collective-permute-start.3 = (bf16[256,256]{1,0:T(8,128)(2,1)S(1)}, bf16[256,256]{1,0:T(8,128)(2,1)S(1)}, u32[]{:S(2)}, u32[]{:S(2)}) collective-permute-start(bf16[256,256]{1,0:T(8,128)(2,1)S(1)} %collective-permute-done.refs_1_.refs_5_), channel_id=1, source_target_pairs={{0,16},{1,17},{2,18},{3,19},{4,20},{5,21},{6,22},{7,23},{8,24},{9,... | collective-permute-start | bytes 393224 | tf_op jit(solution)/shard_map/ppermute | solution.py:47
  26.1 0.0 collective-permute-done.8.refs_10_.refs_12_
  26.1 0.1 collective-permute-start.12
  26.2 0.0 collective-permute-done.11.refs_13_.refs_15_
  26.2 2.6 %collective-permute-start.15 = (bf16[256,256]{1,0:T(8,128)(2,1)S(1)}, bf16[256,256]{1,0:T(8,128)(2,1)S(1)}, u32[]{:S(2)}, u32[]{:S(2)}) collective-permute-start(bf16[256,256]{1,0:T(8,128)(2,1)S(1)} %collective-permute-done.11.refs_13_.refs_15_), channel_id=1, source_target_pairs={{0,14},{1,15},{2,0},{3,1},{4,2},{5,3},{6,4},{7,5},{8,6},{9,7},{10,... | collective-permute-start | bytes 393224 | tf_op jit(solution)/shard_map/ppermute | solution.py:47
  28.8 0.0 collective-permute-done.13.refs_6_.refs_17_
  28.8 0.7 collective-permute-start.16
  29.5 0.0 collective-permute-done.14.refs_7_.refs_18_
  29.5 0.8 %collective-permute-start.17 = (bf16[256,256]{1,0:T(8,128)(2,1)S(1)}, bf16[256,256]{1,0:T(8,128)(2,1)S(1)}, u32[]{:S(2)}, u32[]{:S(2)}) collective-permute-start(bf16[256,256]{1,0:T(8,128)(2,1)S(1)} %collective-permute-done.14.refs_7_.refs_18_), channel_id=1, source_target_pairs={{0,2},{1,3},{2,4},{3,5},{4,6},{5,7},{6,8},{7,9},{8,10},{9,11},{10,... | collective-permute-start | bytes 393224 | tf_op jit(solution)/shard_map/ppermute | solution.py:47
  30.3 0.0 collective-permute-done.3.refs_3_.refs_5_
  30.3 0.0 copy-start
  30.3 0.9 %copy-done = bf16[512,256]{1,0:T(8,128)(2,1)S(1)} copy-done((bf16[512,256]{1,0:T(8,128)(2,1)S(1)}, bf16[512,256]{1,0:T(8,128)(2,1)}, u32[]{:S(2)}) %copy-start) | copy-done | bytes 262168
  31.2 3.1 %shard_map.85 = (f32[8,1024]{1,0:T(8,128)S(1)}, f32[1,2560]{1,0:T(1,128)S(1)}) custom-call(bf16[512,256]{1,0:T(8,128)(2,1)S(1)} %copy-done, bf16[256,256]{1,0:T(8,128)(2,1)S(1)} %collective-permute-done.refs_1_.refs_5_, bf16[256,256]{1,0:T(8,128)(2,1)S(1)} %collective-permute-done.1.refs_2_.refs_4_, ...), custom_call_target="tpu_custom_call" | custom-call | bytes 65536 | tf_op jit(solution)/shard_map/pallas_call | solution.py:279
  34.4 0.0 collective-permute-done.12.refs_5_.refs_16_
  34.4 0.0 collective-permute-done.15.refs_8_.refs_19_
  34.4 1.4 %shard_map.86 = (f32[8,1024]{1,0:T(8,128)S(1)}, f32[1,1024]{1,0:T(1,128)S(1)}) custom-call(bf16[512,256]{1,0:T(8,128)(2,1)S(1)} %copy-done, bf16[256,256]{1,0:T(8,128)(2,1)S(1)} %collective-permute-done.refs_1_.refs_5_, bf16[256,256]{1,0:T(8,128)(2,1)S(1)} %collective-permute-done.1.refs_2_.refs_4_, ...), custom_call_target="tpu_custom_call" | custom-call | bytes 65536 | tf_op jit(solution)/shard_map/pallas_call | solution.py:279
  35.8 0.0 collective-permute-done.16.refs_5_.refs_20_
  35.8 0.0 collective-permute-done.17.refs_6_.refs_21_
  35.8 0.0 copy-start.1
  35.8 0.0 copy-start.3
  35.8 1.5 %shard_map.87 = (f32[1,1152]{1,0:T(1,128)S(1)}, f32[1,512]{1,0:T(1,128)S(1)}, f32[32,1,512]{2,1,0:T(1,128)}) custom-call(bf16[512,256]{1,0:T(8,128)(2,1)S(1)} %copy-done, bf16[256,256]{1,0:T(8,128)(2,1)S(1)} %collective-permute-done.refs_1_.refs_5_, bf16[256,256]{1,0:T(8,128)(2,1)S(1)} %collective-permute-done.1.refs_2_.refs_4_, ...), custom_call_target="tpu_custom_call" | custom-call | bytes 65536 | tf_op jit(solution)/shard_map/pallas_call | solution.py:279
  37.3 0.0 copy-start.2
  37.3 10.1 %all-to-all-start = ((f32[32,1,512]{2,1,0:T(1,128)}), f32[32,1,512]{2,1,0:T(1,128)S(1)}, u32[]{:S(2)}, u32[]{:S(2)}) async-start(f32[32,1,512]{2,1,0:T(1,128)} %get-tuple-element.43), calls=%async_computation | async-start | bytes 131072 | tf_op jit(solution)/shard_map/all_to_all | solution.py:338
  47.4 3.0 %collective-permute-start.18 = (f32[1,1152]{1,0:T(1,128)S(1)}, f32[1,1152]{1,0:T(1,128)S(1)}, u32[]{:S(2)}, u32[]{:S(2)}) collective-permute-start(f32[1,1152]{1,0:T(1,128)S(1)} %get-tuple-element.42.refs_1_.own_lse), channel_id=1, source_target_pairs={{0,16},{1,17},{2,18},{3,19},{4,20},{5,21},{6,22},{7,23},{8,24},{9,... | collective-permute-start | bytes 13832 | tf_op jit(solution)/shard_map/ppermute | solution.py:47
  50.4 0.0 copy-done.1
  50.4 0.0 copy-done.3
  50.4 0.0 copy-done.2
  50.4 0.4 shard_map.88
  50.8 6.2 %all-to-all-done.refs_0_ = f32[32,1,512]{2,1,0:T(1,128)S(1)} async-done(((f32[32,1,512]{2,1,0:T(1,128)}), f32[32,1,512]{2,1,0:T(1,128)S(1)}, u32[]{:S(2)}, u32[]{:S(2)}) %all-to-all-start) | async-done | bytes 65568 | tf_op jit(solution)/shard_map/all_to_all | solution.py:338
  57.0 0.0 collective-permute-done.18.refs_2_.other_lse
  57.0 2.8 %shard_map.90 = bf16[512,256]{1,0:T(8,128)(2,1)S(1)} custom-call(f32[32,1,512]{2,1,0:T(1,128)S(1)} %all-to-all-done.refs_0_, f32[1,1152]{1,0:T(1,128)S(1)} %get-tuple-element.42.refs_1_.own_lse, f32[1,1152]{1,0:T(1,128)S(1)} %collective-permute-done.18.refs_2_.other_lse, s32[8,256]{1,0:T(8,128)S(1)} %copy-done.2, ...), custom_call_target="tpu_custom_call" | custom-call | bytes 65536 | tf_op jit(solution)/shard_map/pallas_call | solution.py:279
  59.8 1.0 %collective-permute-start.19 = (bf16[512,256]{1,0:T(8,128)(2,1)S(1)}, bf16[512,256]{1,0:T(8,128)(2,1)S(1)}, u32[]{:S(2)}, u32[]{:S(2)}) collective-permute-start(bf16[512,256]{1,0:T(8,128)(2,1)S(1)} %shard_map.90), channel_id=1, source_target_pairs={{0,16},{1,17},{2,18},{3,19},{4,20},{5,21},{6,22},{7,23},{8,24},{9,... | collective-permute-start | bytes 786440 | tf_op jit(solution)/shard_map/ppermute | solution.py:47
  60.8 3.3 %shard_map.89 = (f32[256,256]{1,0:T(8,128)S(1)}, f32[256,256]{1,0:T(8,128)S(1)}, f32[1,256]{1,0:T(1,128)}, f32[1,256]{1,0:T(1,128)}) custom-call(f32[32,1,512]{2,1,0:T(1,128)S(1)} %all-to-all-done.refs_0_, f32[1,1152]{1,0:T(1,128)S(1)} %get-tuple-element.42.refs_1_.own_lse, f32[1,1152]{1,0:T(1,128)S(1)} %collective-permute-done.18.refs_2_.other_lse, ...), custom_call_target="tpu_custom_call" | custom-call | bytes 65536 | tf_op jit(solution)/shard_map/pallas_call | solution.py:279
  64.1 4.0 %collective-permute-done.19.away_ref = bf16[512,256]{1,0:T(8,128)(2,1)S(1)} collective-permute-done((bf16[512,256]{1,0:T(8,128)(2,1)S(1)}, bf16[512,256]{1,0:T(8,128)(2,1)S(1)}, u32[]{:S(2)}, u32[]{:S(2)}) %collective-permute-start.19) | collective-permute-done | bytes 262176 | tf_op jit(solution)/shard_map/ppermute | solution.py:47
  68.1 0.1 shard_map.91
  68.2 2.3 %collective-permute-start.20 = (f32[256,256]{1,0:T(8,128)S(1)}, f32[256,256]{1,0:T(8,128)S(1)}, u32[]{:S(2)}, u32[]{:S(2)}) collective-permute-start(f32[256,256]{1,0:T(8,128)S(1)} %get-tuple-element.55), channel_id=1, source_target_pairs={{0,1},{1,0},{2,3},{3,2},{4,5},{5,4},{6,7},{7,6},{8,9},{9,8},{10,11... | collective-permute-start | bytes 786440 | tf_op jit(solution)/shard_map/ppermute | solution.py:47
  70.5 1.2 %collective-permute-done.20.dy_ref = f32[256,256]{1,0:T(8,128)S(1)} collective-permute-done((f32[256,256]{1,0:T(8,128)S(1)}, f32[256,256]{1,0:T(8,128)S(1)}, u32[]{:S(2)}, u32[]{:S(2)}) %collective-permute-start.20) | collective-permute-done | bytes 262176 | tf_op jit(solution)/shard_map/ppermute | solution.py:47
  71.6 1.0 %shard_map.92 = (f32[256,256]{1,0:T(8,128)}, f32[256,256]{1,0:T(8,128)}) custom-call(s32[1]{0:T(128)S(6)} %copy.9.count_ref, s32[8,256]{1,0:T(8,128)S(1)} %copy-done.2, f32[1,1152]{1,0:T(1,128)S(1)} %get-tuple-element.42.refs_1_.own_lse, f32[1,1152]{1,0:T(1,128)S(1)} %collective-permute-done.18.refs_2_.other_lse, f32[256,256]{1,0:T(8,128)S(1)} %get-tuple-element.46.px_ref, ...), custom_call_target="tpu_custom_call" | custom-call | bytes 65536 | tf_op jit(solution)/shard_map/pallas_call | solution.py:279
Async XLA Ops:
  3.3 7.2 %collective-permute-start.4 = (bf16[256,256]{1,0:T(8,128)(2,1)}, bf16[256,256]{1,0:T(8,128)(2,1)S(1)}, u32[]{:S(2)}, u32[]{:S(2)}) collective-permute-start(bf16[256,256]{1,0:T(8,128)(2,1)} %get-tuple-element.38), channel_id=1, source_target_pairs={{0,1},{1,0},{2,3},{3,2},{4,5},{5,4},{6,7},{7,6},{8,9},{9,8},{10,11... | collective-permute-start | bytes 393224 | tf_op jit(solution)/shard_map/ppermute | solution.py:47
  6.6 7.2 %collective-permute-start.2 = (bf16[256,256]{1,0:T(8,128)(2,1)}, bf16[256,256]{1,0:T(8,128)(2,1)S(1)}, u32[]{:S(2)}, u32[]{:S(2)}) collective-permute-start(bf16[256,256]{1,0:T(8,128)(2,1)} %get-tuple-element.36), channel_id=1, source_target_pairs={{0,14},{1,15},{2,0},{3,1},{4,2},{5,3},{6,4},{7,5},{8,6},{9,7},{10,... | collective-permute-start | bytes 393224 | tf_op jit(solution)/shard_map/ppermute | solution.py:47
  10.5 6.5 %collective-permute-start.6 = (bf16[256,256]{1,0:T(8,128)(2,1)S(1)}, bf16[256,256]{1,0:T(8,128)(2,1)S(1)}, u32[]{:S(2)}, u32[]{:S(2)}) collective-permute-start(bf16[256,256]{1,0:T(8,128)(2,1)S(1)} %collective-permute-done.4.refs_5_.refs_7_), channel_id=1, source_target_pairs={{0,2},{1,3},{2,4},{3,5},{4,6},{5,7},{6,8},{7,9},{8,10},{9,11},{10,... | collective-permute-start | bytes 393224 | tf_op jit(solution)/shard_map/ppermute | solution.py:47
  10.5 6.5 %collective-permute-start = (bf16[256,256]{1,0:T(8,128)(2,1)}, bf16[256,256]{1,0:T(8,128)(2,1)S(1)}, u32[]{:S(2)}, u32[]{:S(2)}) collective-permute-start(bf16[256,256]{1,0:T(8,128)(2,1)} %get-tuple-element.34.fy_ref), channel_id=1, source_target_pairs={{0,1},{1,0},{2,3},{3,2},{4,5},{5,4},{6,7},{7,6},{8,9},{9,8},{10,11... | collective-permute-start | bytes 393224 | tf_op jit(solution)/shard_map/ppermute | solution.py:47
  10.8 9.0 %collective-permute-start.5 = (bf16[256,256]{1,0:T(8,128)(2,1)}, bf16[256,256]{1,0:T(8,128)(2,1)S(1)}, u32[]{:S(2)}, u32[]{:S(2)}) collective-permute-start(bf16[256,256]{1,0:T(8,128)(2,1)} %get-tuple-element.36), channel_id=1, source_target_pairs={{0,2},{1,3},{2,4},{3,5},{4,6},{5,7},{6,8},{7,9},{8,10},{9,11},{10,... | collective-permute-start | bytes 393224 | tf_op jit(solution)/shard_map/ppermute | solution.py:47
  10.8 9.0 %collective-permute-start.7 = (bf16[256,256]{1,0:T(8,128)(2,1)S(1)}, bf16[256,256]{1,0:T(8,128)(2,1)S(1)}, u32[]{:S(2)}, u32[]{:S(2)}) collective-permute-start(bf16[256,256]{1,0:T(8,128)(2,1)S(1)} %collective-permute-done.4.refs_5_.refs_7_), channel_id=1, source_target_pairs={{0,14},{1,15},{2,0},{3,1},{4,2},{5,3},{6,4},{7,5},{8,6},{9,7},{10,... | collective-permute-start | bytes 393224 | tf_op jit(solution)/shard_map/ppermute | solution.py:47
  13.8 8.7 %collective-permute-start.9 = (bf16[256,256]{1,0:T(8,128)(2,1)S(1)}, bf16[256,256]{1,0:T(8,128)(2,1)S(1)}, u32[]{:S(2)}, u32[]{:S(2)}) collective-permute-start(bf16[256,256]{1,0:T(8,128)(2,1)S(1)} %collective-permute-done.2.refs_7_.refs_9_), channel_id=1, source_target_pairs={{0,14},{1,15},{2,0},{3,1},{4,2},{5,3},{6,4},{7,5},{8,6},{9,7},{10,... | collective-permute-start | bytes 393224 | tf_op jit(solution)/shard_map/ppermute | solution.py:47
  16.9 6.9 %collective-permute-start.10 = (bf16[256,256]{1,0:T(8,128)(2,1)S(1)}, bf16[256,256]{1,0:T(8,128)(2,1)S(1)}, u32[]{:S(2)}, u32[]{:S(2)}) collective-permute-start(bf16[256,256]{1,0:T(8,128)(2,1)S(1)} %collective-permute-done.6.refs_8_.refs_10_), channel_id=1, source_target_pairs={{0,2},{1,3},{2,4},{3,5},{4,6},{5,7},{6,8},{7,9},{8,10},{9,11},{10,... | collective-permute-start | bytes 393224 | tf_op jit(solution)/shard_map/ppermute | solution.py:47
  16.9 7.0 %collective-permute-start.1 = (bf16[256,256]{1,0:T(8,128)(2,1)}, bf16[256,256]{1,0:T(8,128)(2,1)S(1)}, u32[]{:S(2)}, u32[]{:S(2)}) collective-permute-start(bf16[256,256]{1,0:T(8,128)(2,1)} %get-tuple-element.35), channel_id=1, source_target_pairs={{0,16},{1,17},{2,18},{3,19},{4,20},{5,21},{6,22},{7,23},{8,24},{9,... | collective-permute-start | bytes 393224 | tf_op jit(solution)/shard_map/ppermute | solution.py:47
  19.8 6.3 %collective-permute-start.8 = (bf16[256,256]{1,0:T(8,128)(2,1)S(1)}, bf16[256,256]{1,0:T(8,128)(2,1)S(1)}, u32[]{:S(2)}, u32[]{:S(2)}) collective-permute-start(bf16[256,256]{1,0:T(8,128)(2,1)S(1)} %collective-permute-done.5.refs_6_.refs_8_), channel_id=1, source_target_pairs={{0,2},{1,3},{2,4},{3,5},{4,6},{5,7},{6,8},{7,9},{8,10},{9,11},{10,... | collective-permute-start | bytes 393224 | tf_op jit(solution)/shard_map/ppermute | solution.py:47
  19.8 6.4 %collective-permute-start.11 = (bf16[256,256]{1,0:T(8,128)(2,1)S(1)}, bf16[256,256]{1,0:T(8,128)(2,1)S(1)}, u32[]{:S(2)}, u32[]{:S(2)}) collective-permute-start(bf16[256,256]{1,0:T(8,128)(2,1)S(1)} %collective-permute-done.7.refs_9_.refs_11_), channel_id=1, source_target_pairs={{0,14},{1,15},{2,0},{3,1},{4,2},{5,3},{6,4},{7,5},{8,6},{9,7},{10,... | collective-permute-start | bytes 393224 | tf_op jit(solution)/shard_map/ppermute | solution.py:47
  22.4 6.3 %collective-permute-start.13 = (bf16[256,256]{1,0:T(8,128)(2,1)S(1)}, bf16[256,256]{1,0:T(8,128)(2,1)S(1)}, u32[]{:S(2)}, u32[]{:S(2)}) collective-permute-start(bf16[256,256]{1,0:T(8,128)(2,1)S(1)} %collective-permute-done.9.refs_11_.refs_13_), channel_id=1, source_target_pairs={{0,14},{1,15},{2,0},{3,1},{4,2},{5,3},{6,4},{7,5},{8,6},{9,7},{10,... | collective-permute-start | bytes 393224 | tf_op jit(solution)/shard_map/ppermute | solution.py:47
  23.8 5.6 %collective-permute-start.14 = (bf16[256,256]{1,0:T(8,128)(2,1)S(1)}, bf16[256,256]{1,0:T(8,128)(2,1)S(1)}, u32[]{:S(2)}, u32[]{:S(2)}) collective-permute-start(bf16[256,256]{1,0:T(8,128)(2,1)S(1)} %collective-permute-done.10.refs_12_.refs_14_), channel_id=1, source_target_pairs={{0,2},{1,3},{2,4},{3,5},{4,6},{5,7},{6,8},{7,9},{8,10},{9,11},{10,... | collective-permute-start | bytes 393224 | tf_op jit(solution)/shard_map/ppermute | solution.py:47
  23.9 6.3 %collective-permute-start.3 = (bf16[256,256]{1,0:T(8,128)(2,1)S(1)}, bf16[256,256]{1,0:T(8,128)(2,1)S(1)}, u32[]{:S(2)}, u32[]{:S(2)}) collective-permute-start(bf16[256,256]{1,0:T(8,128)(2,1)S(1)} %collective-permute-done.refs_1_.refs_5_), channel_id=1, source_target_pairs={{0,16},{1,17},{2,18},{3,19},{4,20},{5,21},{6,22},{7,23},{8,24},{9,... | collective-permute-start | bytes 393224 | tf_op jit(solution)/shard_map/ppermute | solution.py:47
  26.1 8.3 %collective-permute-start.12 = (bf16[256,256]{1,0:T(8,128)(2,1)S(1)}, bf16[256,256]{1,0:T(8,128)(2,1)S(1)}, u32[]{:S(2)}, u32[]{:S(2)}) collective-permute-start(bf16[256,256]{1,0:T(8,128)(2,1)S(1)} %collective-permute-done.8.refs_10_.refs_12_), channel_id=1, source_target_pairs={{0,2},{1,3},{2,4},{3,5},{4,6},{5,7},{6,8},{7,9},{8,10},{9,11},{10,... | collective-permute-start | bytes 393224 | tf_op jit(solution)/shard_map/ppermute | solution.py:47
  26.2 8.2 %collective-permute-start.15 = (bf16[256,256]{1,0:T(8,128)(2,1)S(1)}, bf16[256,256]{1,0:T(8,128)(2,1)S(1)}, u32[]{:S(2)}, u32[]{:S(2)}) collective-permute-start(bf16[256,256]{1,0:T(8,128)(2,1)S(1)} %collective-permute-done.11.refs_13_.refs_15_), channel_id=1, source_target_pairs={{0,14},{1,15},{2,0},{3,1},{4,2},{5,3},{6,4},{7,5},{8,6},{9,7},{10,... | collective-permute-start | bytes 393224 | tf_op jit(solution)/shard_map/ppermute | solution.py:47
  28.8 7.0 %collective-permute-start.16 = (bf16[256,256]{1,0:T(8,128)(2,1)S(1)}, bf16[256,256]{1,0:T(8,128)(2,1)S(1)}, u32[]{:S(2)}, u32[]{:S(2)}) collective-permute-start(bf16[256,256]{1,0:T(8,128)(2,1)S(1)} %collective-permute-done.13.refs_6_.refs_17_), channel_id=1, source_target_pairs={{0,14},{1,15},{2,0},{3,1},{4,2},{5,3},{6,4},{7,5},{8,6},{9,7},{10,... | collective-permute-start | bytes 393224 | tf_op jit(solution)/shard_map/ppermute | solution.py:47
  29.5 6.3 %collective-permute-start.17 = (bf16[256,256]{1,0:T(8,128)(2,1)S(1)}, bf16[256,256]{1,0:T(8,128)(2,1)S(1)}, u32[]{:S(2)}, u32[]{:S(2)}) collective-permute-start(bf16[256,256]{1,0:T(8,128)(2,1)S(1)} %collective-permute-done.14.refs_7_.refs_18_), channel_id=1, source_target_pairs={{0,2},{1,3},{2,4},{3,5},{4,6},{5,7},{6,8},{7,9},{8,10},{9,11},{10,... | collective-permute-start | bytes 393224 | tf_op jit(solution)/shard_map/ppermute | solution.py:47
  30.3 1.0 %copy-start = (bf16[512,256]{1,0:T(8,128)(2,1)S(1)}, bf16[512,256]{1,0:T(8,128)(2,1)}, u32[]{:S(2)}) copy-start(bf16[512,256]{1,0:T(8,128)(2,1)} %get-tuple-element.33.refs_0_.refs_4_.fx_ref.refs_6_) | copy-start | bytes 786436
  35.8 14.6 %copy-start.1 = (bf16[512,256]{1,0:T(8,128)(2,1)S(1)}, bf16[512,256]{1,0:T(8,128)(2,1)}, u32[]{:S(2)}) copy-start(bf16[512,256]{1,0:T(8,128)(2,1)} %get-tuple-element.33.refs_0_.refs_4_.fx_ref.refs_6_) | copy-start | bytes 786436
  35.8 14.6 %copy-start.3 = (bf16[256,256]{1,0:T(8,128)(2,1)S(1)}, bf16[256,256]{1,0:T(8,128)(2,1)}, u32[]{:S(2)}) copy-start(bf16[256,256]{1,0:T(8,128)(2,1)} %get-tuple-element.34.fy_ref) | copy-start | bytes 393220
  37.3 13.1 %copy-start.2 = (s32[8,256]{1,0:T(8,128)S(1)}, s32[8,256]{1,0:T(8,128)}, u32[]{:S(2)}) copy-start(s32[8,256]{1,0:T(8,128)} %get-tuple-element.32.match_ref.refs_3_) | copy-start | bytes 24580
  37.3 19.7 %all-to-all-start = ((f32[32,1,512]{2,1,0:T(1,128)}), f32[32,1,512]{2,1,0:T(1,128)S(1)}, u32[]{:S(2)}, u32[]{:S(2)}) async-start(f32[32,1,512]{2,1,0:T(1,128)} %get-tuple-element.43), calls=%async_computation | async-start | bytes 131072 | tf_op jit(solution)/shard_map/all_to_all | solution.py:338
  47.4 9.6 %collective-permute-start.18 = (f32[1,1152]{1,0:T(1,128)S(1)}, f32[1,1152]{1,0:T(1,128)S(1)}, u32[]{:S(2)}, u32[]{:S(2)}) collective-permute-start(f32[1,1152]{1,0:T(1,128)S(1)} %get-tuple-element.42.refs_1_.own_lse), channel_id=1, source_target_pairs={{0,16},{1,17},{2,18},{3,19},{4,20},{5,21},{6,22},{7,23},{8,24},{9,... | collective-permute-start | bytes 13832 | tf_op jit(solution)/shard_map/ppermute | solution.py:47
  59.8 8.4 %collective-permute-start.19 = (bf16[512,256]{1,0:T(8,128)(2,1)S(1)}, bf16[512,256]{1,0:T(8,128)(2,1)S(1)}, u32[]{:S(2)}, u32[]{:S(2)}) collective-permute-start(bf16[512,256]{1,0:T(8,128)(2,1)S(1)} %shard_map.90), channel_id=1, source_target_pairs={{0,16},{1,17},{2,18},{3,19},{4,20},{5,21},{6,22},{7,23},{8,24},{9,... | collective-permute-start | bytes 786440 | tf_op jit(solution)/shard_map/ppermute | solution.py:47
  68.2 3.4 %collective-permute-start.20 = (f32[256,256]{1,0:T(8,128)S(1)}, f32[256,256]{1,0:T(8,128)S(1)}, u32[]{:S(2)}, u32[]{:S(2)}) collective-permute-start(f32[256,256]{1,0:T(8,128)S(1)} %get-tuple-element.55), channel_id=1, source_target_pairs={{0,1},{1,0},{2,3},{3,2},{4,5},{5,4},{6,7},{7,6},{8,9},{9,8},{10,11... | collective-permute-start | bytes 786440 | tf_op jit(solution)/shard_map/ppermute | solution.py:47
